TPU v7x, 32 devices: a whole 2x2x4 slice. The times are simulated.
32 devices in a mesh: samp: 16 (over z, y, x), mark: 2 (over core).
Axes of the slice: x: 2, y: 2, z: 4, core: 2. Of those that a mesh axis runs over, the one named last changes fastest.
Arguments:
- dosage: bfloat16 [8192, 512], P('samp', 'mark'), may hold values from 0 to 2
- alt_count: int32 [512], P('mark'), may hold values from 40000 to 759999
- obs_count: int32 [512], P('mark'), may hold values from 400000 to 500000
- sample_weight: float32 [8192], P('samp'), may hold values from 0.25 to 12, as said below
- test_matrix: bfloat16 [512, 256], P(('mark', 'samp')), may hold values from -6 to 6
Outputs:
- basis: float32 [8192, 256], P(('samp', 'mark'))
- loadings: float32 [512, 256], P(('mark', 'samp'))
Inputs may be any that keep to these rules, and one draw needn't show every extreme that they name: `sample_weight`: every weight is positive.
All inputs are finite; a program needn't handle non-finite values.
Results may differ from a plain program's by a relative error of at most 0.004.
Values may be sent and summed in bfloat16 or wider, within the bound.
No kernel may reach another device: no remote copies, remote signals or barrier semaphores. Data moves between devices by JAX's collectives and lax.ppermute only.
A program may use at most 64 MiB of HBM per device.

v0:
```python
import math

import jax
import jax.numpy as jnp
from jax import lax
from jax.sharding import PartitionSpec as P


def gram_of(matrix):
    return lax.dot_general(
        matrix,
        matrix,
        (((0,), (0,)), ((), ())),
        precision=lax.Precision.HIGHEST,
        preferred_element_type=jnp.float32,
    )


def per_device(dosage, alt_count, obs_count, sample_weight, test_matrix):
    freq = alt_count.astype(jnp.float32) / (2.0 * obs_count.astype(jnp.float32))
    scale = 1.0 / jnp.sqrt(2.0 * freq * (1.0 - freq))
    standard = (
        jnp.sqrt(sample_weight)[:, None] * (dosage.astype(jnp.float32) - 2.0 * freq) * scale
    ).astype(jnp.bfloat16)
    sample_rows, marker_cols = standard.shape
    rank = test_matrix.shape[1]
    columns = standard
    partial_value = jnp.dot(
        columns,
        lax.all_gather(test_matrix, "samp", axis=0, tiled=True),
        preferred_element_type=jnp.float32,
    )
    share = sample_rows // lax.axis_size("mark")
    sketch = lax.psum(partial_value, "mark")
    own_rows = lax.dynamic_slice_in_dim(sketch, lax.axis_index("mark") * share, share, 0)
    gram = gram_of(sketch)
    sketch_round = sketch.astype(jnp.bfloat16)
    lower = jnp.linalg.cholesky(lax.psum(gram, "samp"))
    inverse = lax.linalg.triangular_solve(
        lower, jnp.eye(rank, dtype=jnp.float32), left_side=True, lower=True
    )
    total_samples = sample_rows * lax.axis_size("samp")
    basis = math.sqrt(total_samples) * jnp.dot(
        own_rows, inverse.T, precision=lax.Precision.HIGHEST, preferred_element_type=jnp.float32
    )
    columns = standard
    projected = lax.psum_scatter(
        lax.dot_general(
            columns, sketch_round, (((0,), (0,)), ((), ())), preferred_element_type=jnp.float32
        ),
        "samp",
        scatter_dimension=0,
        tiled=True,
    )
    loadings = jnp.dot(
        projected, inverse.T, precision=lax.Precision.HIGHEST, preferred_element_type=jnp.float32
    )
    return (basis, loadings)


def solution(mesh):
    return jax.shard_map(
        per_device,
        mesh=mesh,
        in_specs=(P("samp", "mark"), P("mark"), P("mark"), P("samp"), P(("mark", "samp"), None)),
        out_specs=(P(("samp", "mark"), None), P(("mark", "samp"), None)),
        check_vma=False,
    )
```

profile of v0, /device:TPU:0, one launch (start us, length us, event | category | flops | bytes accessed | tf_op | source)
XLA Modules:
  0.0 269.2 jit_solution(4157904342971323625)
XLA Ops:
  7.2 0.7 broadcast_multiply_fusion
  7.9 0.7 sqrt.6
  8.6 43.1 %all_gather.3 = bf16[256,256]{1,0:T(8,128)(2,1)S(1)} all-gather(bf16[16,256]{1,0:T(8,128)(2,1)S(1)} %copy-done.3), channel_id=1, replica_groups=mesh['samp'=16,'mark'=2] {'samp'}, dimensions={0}, use_global_device_ids=true | all-gather | bytes 139264 | tf_op jit(solution)/shard_map/all_gather | solution.py:30
  51.7 2.0 fusion.12
  53.8 14.7 %all-reduce.4.cloned.1.call-done = f32[512,256]{1,0:T(8,128)} async-done(((f32[512,256]{1,0:T(8,128)}), f32[512,256]{1,0:T(8,128)}) %all-reduce.4.cloned.1.call-update) | async-done | bytes 524304 | tf_op jit(solution)/shard_map/psum | solution.py:34
  68.5 3.0 %fusion.17 = f32[256,256]{0,1:T(8,128)} fusion(f32[512,256]{1,0:T(8,128)} %all-reduce.4.cloned.1.call-done), kind=kOutput, calls=%fused_computation.43 | convolution fusion | flops 402653184 | bytes 786432 | tf_op jit(solution)/shard_map/dot_general | solution.py:10
  71.6 0.8 copy-done.2
  72.4 1.1 fusion.1
  73.5 109.5 %all-reduce.6.cloned.1.call-done = f32[256,256]{0,1:T(8,128)} async-done(((f32[256,256]{0,1:T(8,128)}), f32[256,256]{0,1:T(8,128)}) %all-reduce.6.cloned.1.call-update) | async-done | bytes 262160 | tf_op jit(solution)/shard_map/psum | solution.py:38
  183.0 1.1 copy.8
  184.3 11.7 %cholesky.50 = f32[128,128]{1,0:T(8,128)S(1)} custom-call(f32[128,128]{1,0:T(8,128)S(1)} %cholesky.118), custom_call_target="Cholesky" | custom-call | tf_op jit(solution)/shard_map/jit(cholesky)/cholesky | solution.py:38
  196.0 9.8 %custom-call.14 = f32[1,128,128]{1,2,0:T(8,128)S(1)} custom-call(f32[1,128,128]{2,1,0:T(8,128)S(1)} %get-tuple-element.25), custom_call_target="InvertDiagBlocksLowerTriangular" | custom-call | tf_op jit(solution)/shard_map/jit(cholesky)/cholesky | solution.py:38
  206.3 11.7 %cholesky.105 = f32[128,128]{1,0:T(8,128)S(1)} custom-call(f32[128,128]{1,0:T(8,128)S(1)} %convolution_subtract_fusion.1), custom_call_target="Cholesky" | custom-call | tf_op jit(solution)/shard_map/jit(cholesky)/cholesky | solution.py:38
  218.1 0.7 compare_reduce_fusion
  220.2 4.1 %while.1 = (s32[]{:T(128)}, f32[256,256]{1,0:T(8,128)S(1)}, s32[2,2]{1,0:T(2,128)S(1)}, f32[2,128,128]{2,1,0:T(8,128)S(1)}, s32[]{:T(128)}) while((s32[]{:T(128)}, f32[256,256]{1,0:T(8,128)S(1)}, s32[2,2]{1,0:T(2,128)S(1)}, f32[2,128,128]{2,1,0:T(8,128)S(1)}, s32[]{:T(128)}) %tuple.28), condition=%wide.while_cond, body=%wide.while_body.sunk | while | flops 2 | bytes 131181 | solution.py:39
  220.3 0.6 fusion.27
  220.9 1.4 bitcast_dynamic-update-slice_fusion.2
  222.3 0.6 fusion.27
  222.9 1.4 bitcast_dynamic-update-slice_fusion.2
  224.3 19.7 %custom-call.15 = f32[2,128,128]{1,2,0:T(8,128)S(1)} custom-call(f32[2,128,128]{2,1,0:T(8,128)S(1)} %get-tuple-element.9), custom_call_target="InvertDiagBlocksLowerTriangular" | custom-call | tf_op jit(solution)/shard_map/triangular_solve | solution.py:39
  244.5 0.3 fusion.8
  244.8 1.1 convolution_multiply_fusion
  245.9 15.0 %reduce-scatter.2.cloned.1.call-done = f32[16,256]{1,0:T(8,128)} async-done(((f32[256,256]{1,0:T(8,128)}), f32[16,256]{1,0:T(8,128)}) %reduce-scatter.2.cloned.1.call-update) | async-done | bytes 16400 | tf_op jit(solution)/shard_map/reduce_scatter | solution.py:47
  261.0 1.6 fusion.4
  (30 shorter events, 1.5 us)
Async XLA Ops:
  7.2 1.5 copy-start.3
  7.2 61.3 %all-reduce.4.cloned.1.call-start = ((), (), s32[]{:S(2)}) async-start(), calls=%async_computation.1 | async-start | bytes 1048576 | tf_op jit(solution)/shard_map/psum | solution.py:34
  53.8 129.3 %all-reduce.6.cloned.1.call-start = ((), (), s32[]{:S(2)}) async-start(), calls=%async_computation.2 | async-start | bytes 524288 | tf_op jit(solution)/shard_map/psum | solution.py:38
  68.5 3.1 %copy-start = (f32[512,256]{1,0:T(8,128)S(1)}, f32[512,256]{1,0:T(8,128)}, u32[]{:S(2)}) copy-start(f32[512,256]{1,0:T(8,128)} %all-reduce.4.cloned.1.call-done) | copy-start | bytes 1572868
  71.5 0.9 copy-start.2
  71.5 189.5 %reduce-scatter.2.cloned.1.call-start = ((), (), s32[]{:S(2)}) async-start(), calls=%async_computation.3 | async-start | bytes 278528 | tf_op jit(solution)/shard_map/reduce_scatter | solution.py:47
  183.0 1.2 copy-start.1
Sparse Core Ops, SparseCore 0:
  53.9 14.5 all-reduce.3
  75.1 107.8 all-reduce.5
  185.3 75.6 reduce-scatter.1
where the time goes:
time: 270 us; the launch traced here: 269 us
  waiting for transfers between devices  139 us (51%)
  other arithmetic  54.5 us (20%)
  blocking collectives  43.1 us (16%)
  between operations  15.2 us (6%)
  matrix products  10.1 us (4%)
  local copies, waits for them, and re-layouts  6.72 us (2%)
    psum x1, waiting for transfers between devices, per_device(): lower = jnp.linalg.cholesky(lax.psum(gram, 'samp'))  110 us
    all_gather x1, blocking collectives, per_device(): lax.all_gather(test_matrix, 'samp', axis=0, tiled=True)  43.1 us
    another operation x6, other arithmetic, per_device(): lower = jnp.linalg.cholesky(lax.psum(gram, 'samp'))  34 us
    another operation x3, other arithmetic, per_device(): lax.linalg.triangular_solve(lower, jnp.eye(rank, dtype=jnp.float32), left...  19.7 us
    reduce_scatter x1, waiting for transfers between devices, per_device(): lax.psum_scatter(lax.dot_general(columns, sketch_round, (((0,), (0,)), ((...  15 us
    psum x1, waiting for transfers between devices, per_device(): sketch = lax.psum(partial_value, 'mark')  14.7 us
  transfers between devices with their start and end apart: 3, of which 3 were waited for; matrix products, arithmetic and copies ran while one was open for 23% of the time, Pallas kernels for 0%

commit v1 on v0

v1 whole, which is shorter than its diff:
```python
import math

import jax
import jax.numpy as jnp
from jax import lax
from jax.experimental import pallas as pl
from jax.experimental.pallas import tpu as pltpu
from jax.sharding import PartitionSpec as P

F32, BF16 = jnp.float32, jnp.bfloat16
HALF = 128
BLOCK = 64
PIVOTS = 8
VMEM = pltpu.VMEM


def dot(a, b, ca, cb, precision=lax.Precision.HIGHEST):
    return lax.dot_general(
        a, b, (((ca,), (cb,)), ((), ())), precision=precision, preferred_element_type=F32
    )


def pieces(x):
    high = x.astype(BF16)
    rest = x - high.astype(F32)
    mid = rest.astype(BF16)
    return high, mid, (rest - mid.astype(F32)).astype(BF16)


def dot_pieces(parts, b, ca, cb):
    terms = [dot(p, b, ca, cb, lax.Precision.DEFAULT) for p in parts]
    return terms[0] + (terms[1] + terms[2])


def dot_pieces_right(a, parts, ca, cb):
    terms = [dot(a, p, ca, cb, lax.Precision.DEFAULT) for p in parts]
    return terms[0] + (terms[1] + terms[2])


def standard_kernel(dosage, alt, obs, weight, out):
    freq = alt[...].astype(F32) / (2.0 * obs[...].astype(F32))
    scale = 1.0 / jnp.sqrt(2.0 * freq * (1.0 - freq))
    root = jnp.sqrt(weight[...])
    rows, cols = dosage.shape
    for r in range(0, rows, HALF):
        column = jnp.transpose(jnp.broadcast_to(root[:, r : r + HALF], (HALF, HALF)))
        for c in range(0, cols, HALF):
            x = dosage[r : r + HALF, c : c + HALF].astype(F32)
            f = freq[:, c : c + HALF]
            out[r : r + HALF, c : c + HALF] = (column * (x - 2.0 * f) * scale[:, c : c + HALF]).astype(BF16)


def moment_kernel(place, own, other, out):
    core = place[1]
    low, high = own[:, :HALF], own[:, HALF:]
    first = other[:, pl.ds(pl.multiple_of(core * HALF, HALF), HALF)]
    second = other[:, pl.ds(pl.multiple_of((1 - core) * HALF, HALF), HALF)]
    for i, (a, b) in enumerate(((low, low), (high, low), (high, high), (low, first), (high, second))):
        out[i * HALF : (i + 1) * HALF, :] = dot(a, b, 0, 0, lax.Precision.DEFAULT)


def eliminate(groups, width):
    shape = (8, width)
    lane = lax.broadcasted_iota(jnp.int32, shape, 1)
    sub = lax.broadcasted_iota(jnp.int32, shape, 0)
    groups, result = list(groups), []
    for g in range(len(groups)):
        j = 8 * g
        rows = [jnp.broadcast_to(groups[g][k : k + 1, :], shape) for k in range(8)]
        a = {
            (i, k): jnp.broadcast_to(groups[g][i : i + 1, j + k : j + k + 1], shape)
            for i in range(8)
            for k in range(i + 1)
        }
        inside = (lane >= j) & (lane < j + 8)
        root, done, low = [], [], {}
        block = jnp.zeros(shape, F32)
        for k in range(8):
            q = lax.rsqrt(a[k, k])
            root.append(q)
            for i in range(k + 1, 8):
                low[i, k] = a[i, k] * q
            for i in range(k + 1, 8):
                for m in range(k + 1, i + 1):
                    a[i, m] = a[i, m] - low[i, k] * low[m, k]
            row = jnp.where(inside, jnp.where(lane == j + k, 1.0, 0.0), rows[k])
            for m in range(k):
                row = row - low[k, m] * done[m]
            done.append(row * q)
            block = jnp.where((sub == k) & (lane <= j + k), done[k], block)
        result.append(block)
        if g + 1 == len(groups):
            break
        update = [None] * 8
        for k in reversed(range(8)):
            x = done[k]
            for m in range(k + 1, 8):
                x = x - low[m, k] * update[m]
            update[k] = x * root[k]
        for n in range(g + 1, len(groups)):
            x = jnp.where(inside, 0.0, groups[n])
            for k in range(8):
                x = x - jnp.broadcast_to(groups[n][:, j + k : j + k + 1], shape) * update[k]
            groups[n] = x
    return result


def inverse_factor(gram, out):
    n = gram.shape[0]
    rest = gram
    for at in range(0, n, BLOCK):
        end = at + BLOCK
        row = rest[:BLOCK]
        inv = jnp.concatenate(eliminate([row[i : i + 8, at:end] for i in range(0, BLOCK, 8)], BLOCK), 0)
        if end < n:
            full = dot(inv, row, 1, 0)
            joined = jnp.concatenate(([full[:, :at]] if at else []) + [inv, full[:, end:]], 1)
            lane = lax.broadcasted_iota(jnp.int32, (BLOCK, n), 1)
            out[at:end, :] = jnp.where(lane < end, joined, 0.0)
            below = rest[BLOCK:]
            lane = lax.broadcasted_iota(jnp.int32, below.shape, 1)
            rest = jnp.where((lane >= at) & (lane < end), 0.0, below) - dot(joined[:, end:], joined, 0, 0)
        else:
            out[at:end, :] = jnp.concatenate([dot(inv, row[:, :at], 1, 0), inv], 1) if at else inv


def final_kernel(
    total, place, blocks, others, test, test_other, standard, standard_other, basis, loadings, moments, inverse, product
):
    samp, core = place[0], place[1]
    side = 2 * HALF
    block = lambda ref, i: ref[i * HALF : (i + 1) * HALF, :]
    for ref, at in ((blocks, 0), (others, side)):
        corner = block(ref, 1)
        moments[at : at + HALF, at : at + HALF] = block(ref, 0)
        moments[at + HALF : at + side, at : at + HALF] = corner
        moments[at : at + HALF, at + HALF : at + side] = corner.T
        moments[at + HALF : at + side, at + HALF : at + side] = block(ref, 2)
    mine, theirs = (block(blocks, 3), block(blocks, 4)), (block(others, 3), block(others, 4))
    for h in range(2):
        column = pl.ds(pl.multiple_of(side + (h + core - 2 * h * core) * HALF, HALF), HALF)
        moments[h * HALF : (h + 1) * HALF, column] = mine[h]
        moments[column, h * HALF : (h + 1) * HALF] = mine[h].T
        away = 1 - core
        column = pl.ds(pl.multiple_of((h + away - 2 * h * away) * HALF, HALF), HALF)
        moments[side + h * HALF : side + (h + 1) * HALF, column] = theirs[h]
        moments[column, side + h * HALF : side + (h + 1) * HALF] = theirs[h].T
    tests = jnp.concatenate([test[...], test_other[...]], 0)
    product[...] = dot_pieces(pieces(moments[...]), tests, 1, 0)
    gram = dot_pieces_right(tests, pieces(product[...]), 0, 0)
    inverse_factor(gram, inverse)
    share = basis.shape[0]
    rows = pl.ds(pl.multiple_of(core * share, share), share)
    sketch = dot(standard[rows, :], test[...], 1, 0, lax.Precision.DEFAULT) + dot(
        standard_other[rows, :], test_other[...], 1, 0, lax.Precision.DEFAULT
    )
    basis[...] = math.sqrt(total) * dot(sketch, inverse[...], 1, 1)
    few = loadings.shape[0]
    own = product[pl.ds(pl.multiple_of(samp * few, few), few), :]
    loadings[...] = dot(own, inverse[...], 1, 1)


def call(kernel, shapes, inputs, place=None, scratch=()):
    vmem = pl.BlockSpec(memory_space=VMEM)
    specs = [vmem] * len(inputs)
    if place is not None:
        specs, inputs = [pl.BlockSpec(memory_space=pltpu.SMEM)] + specs, [place] + list(inputs)
    many = isinstance(shapes, (list, tuple))
    return pl.pallas_call(
        kernel,
        out_shape=shapes,
        in_specs=specs,
        out_specs=[vmem] * len(shapes) if many else vmem,
        scratch_shapes=list(scratch),
        compiler_params=pltpu.CompilerParams(vmem_limit_bytes=24 * 2**20),
    )(*inputs)


def swap(x, axis, bit):
    return lax.ppermute(x, axis, [(i, i ^ bit) for i in range(lax.axis_size(axis))])


def upper(axis, bit):
    return (lax.axis_index(axis) // bit) % 2


def keep_half(x, axis, bit):
    half, up = x.shape[0] // 2, upper(axis, bit)
    kept = lax.dynamic_slice_in_dim(x, up * half, half, 0)
    sent = lax.dynamic_slice_in_dim(x, (1 - up) * half, half, 0)
    return kept + swap(sent, axis, bit)


def join(x, axis, bit):
    got = swap(x, axis, bit)
    return jnp.where(upper(axis, bit) == 0, jnp.concatenate([x, got], 0), jnp.concatenate([got, x], 0))


def sum_over(x, axis):
    bits = [1 << i for i in range((lax.axis_size(axis) - 1).bit_length())]
    half = x.shape[0] // 2
    plans = ((bits[0], bits[2:3] + bits[1:2] + bits[3:]), (bits[1], bits[0:1] + bits[2:]))
    parts = []
    for part, (first, rest) in zip((x[:half], x[half:]), plans):
        part = keep_half(part, axis, first)
        for bit in rest:
            part = part + swap(part, axis, bit)
        parts.append(join(part, axis, first))
    return jnp.concatenate(parts, 0)


def two_marks(dosage, alt_count, obs_count, sample_weight, test_matrix):
    rows, cols = dosage.shape
    few, rank = test_matrix.shape
    samples = rows * lax.axis_size("samp")
    place = jnp.stack([lax.axis_index("samp"), lax.axis_index("mark")]).astype(jnp.int32)
    standard = call(
        standard_kernel,
        jax.ShapeDtypeStruct((rows, cols), BF16),
        [dosage, alt_count.reshape(1, cols), obs_count.reshape(1, cols), sample_weight.reshape(1, rows)],
    )
    standard_other = swap(standard, "mark", 1)
    blocks = call(
        moment_kernel, jax.ShapeDtypeStruct((5 * HALF, HALF), F32), [standard, standard_other], place
    )
    test = test_matrix
    for i in range((lax.axis_size("samp") - 1).bit_length()):
        test = join(test, "samp", 1 << i)
    test_other = swap(test, "mark", 1)
    blocks = sum_over(blocks, "samp")
    others = swap(blocks, "mark", 1)
    kernel = lambda *refs: final_kernel(samples, *refs)
    basis, loadings = call(
        kernel,
        [jax.ShapeDtypeStruct((rows // 2, rank), F32), jax.ShapeDtypeStruct((few, rank), F32)],
        [blocks, others, test, test_other, standard, standard_other],
        place,
        [VMEM((2 * cols, 2 * cols), F32), VMEM((rank, rank), F32), VMEM((2 * cols, rank), F32)],
    )
    return basis, loadings


def any_marks(dosage, alt_count, obs_count, sample_weight, test_matrix):
    freq = alt_count.astype(F32) / (2.0 * obs_count.astype(F32))
    scale = 1.0 / jnp.sqrt(2.0 * freq * (1.0 - freq))
    standard = (jnp.sqrt(sample_weight)[:, None] * (dosage.astype(F32) - 2.0 * freq) * scale).astype(BF16)
    rank = test_matrix.shape[1]
    partial_value = jnp.dot(
        standard, lax.all_gather(test_matrix, "samp", axis=0, tiled=True), preferred_element_type=F32
    )
    share = standard.shape[0] // lax.axis_size("mark")
    sketch = lax.psum(partial_value, "mark")
    own_rows = lax.dynamic_slice_in_dim(sketch, lax.axis_index("mark") * share, share, 0)
    gram = dot(sketch, sketch, 0, 0)
    lower = jnp.linalg.cholesky(lax.psum(gram, "samp"))
    inverse = lax.linalg.triangular_solve(lower, jnp.eye(rank, dtype=F32), left_side=True, lower=True)
    basis = math.sqrt(standard.shape[0] * lax.axis_size("samp")) * dot(own_rows, inverse, 1, 1)
    projected = lax.psum_scatter(
        dot(standard, sketch.astype(BF16), 0, 0, lax.Precision.DEFAULT), "samp", scatter_dimension=0, tiled=True
    )
    return basis, dot(projected, inverse, 1, 1)


def solution(mesh):
    samp, mark = mesh.shape["samp"], mesh.shape["mark"]

    def per_device(dosage, *rest):
        fits = mark == 2 and samp >= 4 and samp & (samp - 1) == 0 and dosage.shape[1] == 2 * HALF
        return (two_marks if fits else any_marks)(dosage, *rest)

    return jax.shard_map(
        per_device,
        mesh=mesh,
        in_specs=(P("samp", "mark"), P("mark"), P("mark"), P("samp"), P(("mark", "samp"), None)),
        out_specs=(P(("samp", "mark"), None), P(("mark", "samp"), None)),
        check_vma=False,
    )
```

time: 270 us -> 58.5 us (0.22)
  waiting for transfers between devices: 139 us -> 14.3 us
  other arithmetic: 54.5 us -> 0.27 us
  blocking collectives: 43.1 us -> 0 us
  starting transfers between devices: 0.12 us -> 25.5 us
  Pallas kernels: 0 us -> 15.8 us
  between operations: 15.2 us -> 0.81 us
  matrix products: 10.1 us -> 0 us
  local copies, waits for them, and re-layouts: 6.72 us -> 1.69 us
    psum x2 -> x0, waiting for transfers between devices: 124 us -> none  [the longest x1 110 us: per_device(): lower = jnp.linalg.cholesky(lax.psum(gram, 'samp'))]
    another operation x9 -> x1, other arithmetic: 53.7 us -> 0.07 us  [two_marks(): jnp.stack([lax.axis_index('samp'), lax.axis_index('mark')])]
    all_gather x1 -> x0, blocking collectives: 43.1 us -> none  [per_device(): lax.all_gather(test_matrix, 'samp', axis=0, tiled=True)]
    ppermute x0 -> x17, starting transfers between devices: none -> 25.5 us  [swap(): lax.ppermute(x, axis, [(i, i ^ bit) for i in range(lax.axis_size(axis))])]
    pallas_call x0 -> x3, Pallas kernels: none -> 15.8 us  [call(): pl.pallas_call(kernel, out_shape=shapes, in_specs=specs, out_specs=[vmem]...]
    reduce_scatter x1 -> x0, waiting for transfers between devices: 15 us -> none  [per_device(): lax.psum_scatter(lax.dot_general(columns, sketch_round, (((0,), (0,)), ((...]
    ppermute x0 -> x17, waiting for transfers between devices: none -> 14.3 us  [swap(): lax.ppermute(x, axis, [(i, i ^ bit) for i in range(lax.axis_size(axis))])]
    dot_general x5 -> x0, matrix products: 8.83 us -> none  [the longest x1 2.96 us: gram_of(): lax.dot_general(matrix, matrix, (((0,), (0,)), ((), ())), precision=lax.P...]
  transfers between devices with their start and end apart: 3 -> 17, of which waited for: 3 -> 8; matrix products, arithmetic and copies ran while one was open for 23% -> 0% of each run, Pallas kernels for 0% -> 0%
where the time goes in v1:
time: 58.5 us; the launch traced here: 58.3 us
  starting transfers between devices  25.5 us (44%)
  Pallas kernels  15.8 us (27%)
  waiting for transfers between devices  14.3 us (24%)
  local copies, waits for them, and re-layouts  1.69 us (3%)
  between operations  0.81 us (1%)
    ppermute x17, starting transfers between devices, swap(): lax.ppermute(x, axis, [(i, i ^ bit) for i in range(lax.axis_size(axis))])  25.5 us
    pallas_call x3, Pallas kernels, call(): pl.pallas_call(kernel, out_shape=shapes, in_specs=specs, out_specs=[vmem]...  15.8 us
    ppermute x17, waiting for transfers between devices, swap(): lax.ppermute(x, axis, [(i, i ^ bit) for i in range(lax.axis_size(axis))])  14.3 us
    unnamed x10, local copies, waits for them, and re-layouts  1.64 us
  transfers between devices with their start and end apart: 17, of which 8 were waited for; matrix products, arithmetic and copies ran while one was open for 0% of the time, Pallas kernels for 0%

profile of v1, /device:TPU:0, one launch (start us, length us, event | category | flops | bytes accessed | tf_op | source)
XLA Modules:
  0.0 58.3 jit_solution(14434537350358672824)
XLA Ops:
  0.7 0.7 %copy-done.3 = s32[256]{0:T(256)S(1)} copy-done((s32[256]{0:T(256)S(1)}, s32[256]{0:T(256)}, u32[]{:S(2)}) %copy-start.3) | copy-done | bytes 1048
  1.3 0.9 %copy-done = bf16[512,256]{1,0:T(8,128)(2,1)S(1)} copy-done((bf16[512,256]{1,0:T(8,128)(2,1)S(1)}, bf16[512,256]{1,0:T(8,128)(2,1)}, u32[]{:S(2)}) %copy-start) | copy-done | bytes 262168
  3.0 1.1 %collective-permute-done.other.refs_6_ = bf16[512,256]{1,0:T(8,128)(2,1)S(1)} collective-permute-done((bf16[512,256]{1,0:T(8,128)(2,1)S(1)}, bf16[512,256]{1,0:T(8,128)(2,1)S(1)}, u32[]{:S(2)}, u32[]{:S(2)}) %collective-permute-start) | collective-permute-done | bytes 262176 | tf_op jit(solution)/shard_map/ppermute | solution.py:180
  4.1 0.9 %shard_map.69 = f32[640,128]{1,0:T(8,128)S(1)} custom-call(s32[2]{0:T(128)S(1)} %pad_add_fusion.place.refs_0_, bf16[512,256]{1,0:T(8,128)(2,1)S(1)} %shard_map.68.own.refs_5_, bf16[512,256]{1,0:T(8,128)(2,1)S(1)} %collective-permute-done.other.refs_6_), custom_call_target="tpu_custom_call" | custom-call | tf_op jit(solution)/shard_map/pallas_call | solution.py:169
  5.1 3.0 %collective-permute-start.6 = (f32[160,128]{1,0:T(8,128)S(1)}, f32[160,128]{1,0:T(8,128)S(1)}, u32[]{:S(2)}, u32[]{:S(2)}) collective-permute-start(f32[160,128]{1,0:T(8,128)S(1)} %constant_dynamic-slice_fusion), channel_id=1, source_target_pairs={{0,4},{2,6},{4,0},{6,2},{8,12},{10,14},{12,8},{14,10},{16,20},{18,... | collective-permute-start | bytes 245768 | tf_op jit(solution)/shard_map/ppermute | solution.py:180
  8.1 1.5 %collective-permute-start.1 = (f32[160,128]{1,0:T(8,128)S(1)}, f32[160,128]{1,0:T(8,128)S(1)}, u32[]{:S(2)}, u32[]{:S(2)}) collective-permute-start(f32[160,128]{1,0:T(8,128)S(1)} %constant_dynamic-slice_fusion.1), channel_id=1, source_target_pairs={{0,2},{2,0},{4,6},{6,4},{8,10},{10,8},{12,14},{14,12},{16,18},{18,... | collective-permute-start | bytes 245768 | tf_op jit(solution)/shard_map/ppermute | solution.py:180
  9.6 1.2 %collective-permute-done.6 = f32[160,128]{1,0:T(8,128)S(1)} collective-permute-done((f32[160,128]{1,0:T(8,128)S(1)}, f32[160,128]{1,0:T(8,128)S(1)}, u32[]{:S(2)}, u32[]{:S(2)}) %collective-permute-start.6) | collective-permute-done | bytes 81952 | tf_op jit(solution)/shard_map/ppermute | solution.py:180
  10.8 1.8 %collective-permute-start.7 = (f32[160,128]{1,0:T(8,128)S(1)}, f32[160,128]{1,0:T(8,128)S(1)}, u32[]{:S(2)}, u32[]{:S(2)}) collective-permute-start(f32[160,128]{1,0:T(8,128)S(1)} %dynamic-slice_add_fusion), channel_id=1, source_target_pairs={{0,2},{2,0},{4,6},{6,4},{8,10},{10,8},{12,14},{14,12},{16,18},{18,... | collective-permute-start | bytes 245768 | tf_op jit(solution)/shard_map/ppermute | solution.py:180
  12.6 1.6 %collective-permute-start.2 = (f32[160,128]{1,0:T(8,128)S(1)}, f32[160,128]{1,0:T(8,128)S(1)}, u32[]{:S(2)}, u32[]{:S(2)}) collective-permute-start(f32[160,128]{1,0:T(8,128)S(1)} %dynamic-slice_add_fusion.1), channel_id=1, source_target_pairs={{0,8},{2,10},{4,12},{6,14},{8,0},{10,2},{12,4},{14,6},{16,24},{18,... | collective-permute-start | bytes 245768 | tf_op jit(solution)/shard_map/ppermute | solution.py:180
  14.3 1.1 %collective-permute-done.7 = f32[160,128]{1,0:T(8,128)S(1)} collective-permute-done((f32[160,128]{1,0:T(8,128)S(1)}, f32[160,128]{1,0:T(8,128)S(1)}, u32[]{:S(2)}, u32[]{:S(2)}) %collective-permute-start.7) | collective-permute-done | bytes 81952 | tf_op jit(solution)/shard_map/ppermute | solution.py:180
  15.3 1.9 %collective-permute-start.8 = (f32[160,128]{1,0:T(8,128)S(1)}, f32[160,128]{1,0:T(8,128)S(1)}, u32[]{:S(2)}, u32[]{:S(2)}) collective-permute-start(f32[160,128]{1,0:T(8,128)S(1)} %add.68), channel_id=1, source_target_pairs={{0,8},{2,10},{4,12},{6,14},{8,0},{10,2},{12,4},{14,6},{16,24},{18,... | collective-permute-start | bytes 245768 | tf_op jit(solution)/shard_map/ppermute | solution.py:180
  17.2 1.5 %collective-permute-start.12 = (bf16[16,256]{1,0:T(8,128)(2,1)S(1)}, bf16[16,256]{1,0:T(8,128)(2,1)S(1)}, u32[]{:S(2)}, u32[]{:S(2)}) collective-permute-start(bf16[16,256]{1,0:T(8,128)(2,1)S(1)} %copy-done.4), channel_id=1, source_target_pairs={{0,2},{2,0},{4,6},{6,4},{8,10},{10,8},{12,14},{14,12},{16,18},{18,... | collective-permute-start | bytes 24584 | tf_op jit(solution)/shard_map/ppermute | solution.py:180
  18.7 1.6 %collective-permute-start.3 = (f32[160,128]{1,0:T(8,128)S(1)}, f32[160,128]{1,0:T(8,128)S(1)}, u32[]{:S(2)}, u32[]{:S(2)}) collective-permute-start(f32[160,128]{1,0:T(8,128)S(1)} %add.61), channel_id=1, source_target_pairs={{0,4},{2,6},{4,0},{6,2},{8,12},{10,14},{12,8},{14,10},{16,20},{18,... | collective-permute-start | bytes 245768 | tf_op jit(solution)/shard_map/ppermute | solution.py:180
  20.3 2.7 %collective-permute-start.9 = (f32[160,128]{1,0:T(8,128)S(1)}, f32[160,128]{1,0:T(8,128)S(1)}, u32[]{:S(2)}, u32[]{:S(2)}) collective-permute-start(f32[160,128]{1,0:T(8,128)S(1)} %add.69), channel_id=1, source_target_pairs={{0,16},{2,18},{4,20},{6,22},{8,24},{10,26},{12,28},{14,30},{16,0},... | collective-permute-start | bytes 245768 | tf_op jit(solution)/shard_map/ppermute | solution.py:180
  23.0 1.3 %collective-permute-start.13 = (bf16[32,256]{1,0:T(8,128)(2,1)S(1)}, bf16[32,256]{1,0:T(8,128)(2,1)S(1)}, u32[]{:S(2)}, u32[]{:S(2)}) collective-permute-start(bf16[32,256]{1,0:T(8,128)(2,1)S(1)} %maximum_select_fusion.5), channel_id=1, source_target_pairs={{0,4},{2,6},{4,0},{6,2},{8,12},{10,14},{12,8},{14,10},{16,20},{18,... | collective-permute-start | bytes 49160 | tf_op jit(solution)/shard_map/ppermute | solution.py:180
  24.3 1.5 %collective-permute-start.4 = (f32[160,128]{1,0:T(8,128)S(1)}, f32[160,128]{1,0:T(8,128)S(1)}, u32[]{:S(2)}, u32[]{:S(2)}) collective-permute-start(f32[160,128]{1,0:T(8,128)S(1)} %add.62), channel_id=1, source_target_pairs={{0,16},{2,18},{4,20},{6,22},{8,24},{10,26},{12,28},{14,30},{16,0},... | collective-permute-start | bytes 245768 | tf_op jit(solution)/shard_map/ppermute | solution.py:180
  25.9 2.1 %collective-permute-done.9 = f32[160,128]{1,0:T(8,128)S(1)} collective-permute-done((f32[160,128]{1,0:T(8,128)S(1)}, f32[160,128]{1,0:T(8,128)S(1)}, u32[]{:S(2)}, u32[]{:S(2)}) %collective-permute-start.9) | collective-permute-done | bytes 81952 | tf_op jit(solution)/shard_map/ppermute | solution.py:180
  28.0 1.4 %collective-permute-start.10 = (f32[160,128]{1,0:T(8,128)S(1)}, f32[160,128]{1,0:T(8,128)S(1)}, u32[]{:S(2)}, u32[]{:S(2)}) collective-permute-start(f32[160,128]{1,0:T(8,128)S(1)} %add.70), channel_id=1, source_target_pairs={{0,4},{2,6},{4,0},{6,2},{8,12},{10,14},{12,8},{14,10},{16,20},{18,... | collective-permute-start | bytes 245768 | tf_op jit(solution)/shard_map/ppermute | solution.py:180
  29.8 2.9 %collective-permute-start.5 = (f32[160,128]{1,0:T(8,128)S(1)}, f32[160,128]{1,0:T(8,128)S(1)}, u32[]{:S(2)}, u32[]{:S(2)}) collective-permute-start(f32[160,128]{1,0:T(8,128)S(1)} %add.63), channel_id=1, source_target_pairs={{0,2},{2,0},{4,6},{6,4},{8,10},{10,8},{12,14},{14,12},{16,18},{18,... | collective-permute-start | bytes 245768 | tf_op jit(solution)/shard_map/ppermute | solution.py:180
  32.7 2.4 %collective-permute-done.5 = f32[160,128]{1,0:T(8,128)S(1)} collective-permute-done((f32[160,128]{1,0:T(8,128)S(1)}, f32[160,128]{1,0:T(8,128)S(1)}, u32[]{:S(2)}, u32[]{:S(2)}) %collective-permute-start.5) | collective-permute-done | bytes 81952 | tf_op jit(solution)/shard_map/ppermute | solution.py:180
  35.3 2.1 %collective-permute-start.15 = (bf16[128,256]{1,0:T(8,128)(2,1)S(1)}, bf16[128,256]{1,0:T(8,128)(2,1)S(1)}, u32[]{:S(2)}, u32[]{:S(2)}) collective-permute-start(bf16[128,256]{1,0:T(8,128)(2,1)S(1)} %maximum_select_fusion.3), channel_id=1, source_target_pairs={{0,16},{2,18},{4,20},{6,22},{8,24},{10,26},{12,28},{14,30},{16,0},... | collective-permute-start | bytes 196616 | tf_op jit(solution)/shard_map/ppermute | solution.py:180
  37.4 4.7 %collective-permute-done.15 = bf16[128,256]{1,0:T(8,128)(2,1)S(1)} collective-permute-done((bf16[128,256]{1,0:T(8,128)(2,1)S(1)}, bf16[128,256]{1,0:T(8,128)(2,1)S(1)}, u32[]{:S(2)}, u32[]{:S(2)}) %collective-permute-start.15) | collective-permute-done | bytes 65568 | tf_op jit(solution)/shard_map/ppermute | solution.py:180
  42.3 1.3 %collective-permute-done.16.refs_4_ = bf16[256,256]{1,0:T(8,128)(2,1)S(1)} collective-permute-done((bf16[256,256]{1,0:T(8,128)(2,1)S(1)}, bf16[256,256]{1,0:T(8,128)(2,1)S(1)}, u32[]{:S(2)}, u32[]{:S(2)}) %collective-permute-start.16) | collective-permute-done | bytes 131104 | tf_op jit(solution)/shard_map/ppermute | solution.py:180
  43.6 14.7 %shard_map.70 = (f32[256,256]{1,0:T(8,128)}, f32[16,256]{1,0:T(8,128)}) custom-call(s32[2]{0:T(128)S(1)} %pad_add_fusion.place.refs_0_, f32[640,128]{1,0:T(8,128)S(1)} %pad_maximum_fusion.refs_1_, f32[640,128]{1,0:T(8,128)S(1)} %collective-permute-done.11.refs_2_, bf16[256,256]{1,0:T(8,128)(2,1)S(1)} %maximum_select_fusion.2.refs_3_, ...), custom_call_target="tpu_custom_call" | custom-call | tf_op jit(solution)/shard_map/pallas_call | solution.py:169
  (42 shorter events, 1.5 us)
Async XLA Ops:
  0.6 0.7 %copy-start.3 = (s32[256]{0:T(256)S(1)}, s32[256]{0:T(256)}, u32[]{:S(2)}) copy-start(s32[256]{0:T(256)} %param.7) | copy-start | bytes 3076
  0.6 0.7 %copy-start.1 = (f32[512]{0:T(512)S(1)}, f32[512]{0:T(512)}, u32[]{:S(2)}) copy-start(f32[512]{0:T(512)} %param.8) | copy-start | bytes 6148
  0.7 0.7 %copy-start.2 = (s32[256]{0:T(256)S(1)}, s32[256]{0:T(256)}, u32[]{:S(2)}) copy-start(s32[256]{0:T(256)} %param.6) | copy-start | bytes 3076
  1.3 0.9 %copy-start = (bf16[512,256]{1,0:T(8,128)(2,1)S(1)}, bf16[512,256]{1,0:T(8,128)(2,1)}, u32[]{:S(2)}) copy-start(bf16[512,256]{1,0:T(8,128)(2,1)} %dosage.1) | copy-start | bytes 786436
  2.4 1.7 %collective-permute-start = (bf16[512,256]{1,0:T(8,128)(2,1)S(1)}, bf16[512,256]{1,0:T(8,128)(2,1)S(1)}, u32[]{:S(2)}, u32[]{:S(2)}) collective-permute-start(bf16[512,256]{1,0:T(8,128)(2,1)S(1)} %shard_map.68.own.refs_5_), channel_id=1, source_target_pairs={{0,1},{1,0},{2,3},{3,2},{4,5},{5,4},{6,7},{7,6},{8,9},{9,8},{10,11... | collective-permute-start | bytes 786440 | tf_op jit(solution)/shard_map/ppermute | solution.py:180
  5.1 5.7 %collective-permute-start.6 = (f32[160,128]{1,0:T(8,128)S(1)}, f32[160,128]{1,0:T(8,128)S(1)}, u32[]{:S(2)}, u32[]{:S(2)}) collective-permute-start(f32[160,128]{1,0:T(8,128)S(1)} %constant_dynamic-slice_fusion), channel_id=1, source_target_pairs={{0,4},{2,6},{4,0},{6,2},{8,12},{10,14},{12,8},{14,10},{16,20},{18,... | collective-permute-start | bytes 245768 | tf_op jit(solution)/shard_map/ppermute | solution.py:180
  8.1 4.5 %collective-permute-start.1 = (f32[160,128]{1,0:T(8,128)S(1)}, f32[160,128]{1,0:T(8,128)S(1)}, u32[]{:S(2)}, u32[]{:S(2)}) collective-permute-start(f32[160,128]{1,0:T(8,128)S(1)} %constant_dynamic-slice_fusion.1), channel_id=1, source_target_pairs={{0,2},{2,0},{4,6},{6,4},{8,10},{10,8},{12,14},{14,12},{16,18},{18,... | collective-permute-start | bytes 245768 | tf_op jit(solution)/shard_map/ppermute | solution.py:180
  10.8 4.5 %collective-permute-start.7 = (f32[160,128]{1,0:T(8,128)S(1)}, f32[160,128]{1,0:T(8,128)S(1)}, u32[]{:S(2)}, u32[]{:S(2)}) collective-permute-start(f32[160,128]{1,0:T(8,128)S(1)} %dynamic-slice_add_fusion), channel_id=1, source_target_pairs={{0,2},{2,0},{4,6},{6,4},{8,10},{10,8},{12,14},{14,12},{16,18},{18,... | collective-permute-start | bytes 245768 | tf_op jit(solution)/shard_map/ppermute | solution.py:180
  12.6 4.6 %copy-start.4 = (bf16[16,256]{1,0:T(8,128)(2,1)S(1)}, bf16[16,256]{1,0:T(8,128)(2,1)}, u32[]{:S(2)}) copy-start(bf16[16,256]{1,0:T(8,128)(2,1)} %param.9) | copy-start | bytes 24580
  12.6 6.1 %collective-permute-start.2 = (f32[160,128]{1,0:T(8,128)S(1)}, f32[160,128]{1,0:T(8,128)S(1)}, u32[]{:S(2)}, u32[]{:S(2)}) collective-permute-start(f32[160,128]{1,0:T(8,128)S(1)} %dynamic-slice_add_fusion.1), channel_id=1, source_target_pairs={{0,8},{2,10},{4,12},{6,14},{8,0},{10,2},{12,4},{14,6},{16,24},{18,... | collective-permute-start | bytes 245768 | tf_op jit(solution)/shard_map/ppermute | solution.py:180
  15.3 5.0 %collective-permute-start.8 = (f32[160,128]{1,0:T(8,128)S(1)}, f32[160,128]{1,0:T(8,128)S(1)}, u32[]{:S(2)}, u32[]{:S(2)}) collective-permute-start(f32[160,128]{1,0:T(8,128)S(1)} %add.68), channel_id=1, source_target_pairs={{0,8},{2,10},{4,12},{6,14},{8,0},{10,2},{12,4},{14,6},{16,24},{18,... | collective-permute-start | bytes 245768 | tf_op jit(solution)/shard_map/ppermute | solution.py:180
  17.2 5.8 %collective-permute-start.12 = (bf16[16,256]{1,0:T(8,128)(2,1)S(1)}, bf16[16,256]{1,0:T(8,128)(2,1)S(1)}, u32[]{:S(2)}, u32[]{:S(2)}) collective-permute-start(bf16[16,256]{1,0:T(8,128)(2,1)S(1)} %copy-done.4), channel_id=1, source_target_pairs={{0,2},{2,0},{4,6},{6,4},{8,10},{10,8},{12,14},{14,12},{16,18},{18,... | collective-permute-start | bytes 24584 | tf_op jit(solution)/shard_map/ppermute | solution.py:180
  18.7 5.6 %collective-permute-start.3 = (f32[160,128]{1,0:T(8,128)S(1)}, f32[160,128]{1,0:T(8,128)S(1)}, u32[]{:S(2)}, u32[]{:S(2)}) collective-permute-start(f32[160,128]{1,0:T(8,128)S(1)} %add.61), channel_id=1, source_target_pairs={{0,4},{2,6},{4,0},{6,2},{8,12},{10,14},{12,8},{14,10},{16,20},{18,... | collective-permute-start | bytes 245768 | tf_op jit(solution)/shard_map/ppermute | solution.py:180
  20.3 7.7 %collective-permute-start.9 = (f32[160,128]{1,0:T(8,128)S(1)}, f32[160,128]{1,0:T(8,128)S(1)}, u32[]{:S(2)}, u32[]{:S(2)}) collective-permute-start(f32[160,128]{1,0:T(8,128)S(1)} %add.69), channel_id=1, source_target_pairs={{0,16},{2,18},{4,20},{6,22},{8,24},{10,26},{12,28},{14,30},{16,0},... | collective-permute-start | bytes 245768 | tf_op jit(solution)/shard_map/ppermute | solution.py:180
  23.0 6.4 %collective-permute-start.13 = (bf16[32,256]{1,0:T(8,128)(2,1)S(1)}, bf16[32,256]{1,0:T(8,128)(2,1)S(1)}, u32[]{:S(2)}, u32[]{:S(2)}) collective-permute-start(bf16[32,256]{1,0:T(8,128)(2,1)S(1)} %maximum_select_fusion.5), channel_id=1, source_target_pairs={{0,4},{2,6},{4,0},{6,2},{8,12},{10,14},{12,8},{14,10},{16,20},{18,... | collective-permute-start | bytes 49160 | tf_op jit(solution)/shard_map/ppermute | solution.py:180
  24.3 5.4 %collective-permute-start.4 = (f32[160,128]{1,0:T(8,128)S(1)}, f32[160,128]{1,0:T(8,128)S(1)}, u32[]{:S(2)}, u32[]{:S(2)}) collective-permute-start(f32[160,128]{1,0:T(8,128)S(1)} %add.62), channel_id=1, source_target_pairs={{0,16},{2,18},{4,20},{6,22},{8,24},{10,26},{12,28},{14,30},{16,0},... | collective-permute-start | bytes 245768 | tf_op jit(solution)/shard_map/ppermute | solution.py:180
  28.0 4.7 %collective-permute-start.10 = (f32[160,128]{1,0:T(8,128)S(1)}, f32[160,128]{1,0:T(8,128)S(1)}, u32[]{:S(2)}, u32[]{:S(2)}) collective-permute-start(f32[160,128]{1,0:T(8,128)S(1)} %add.70), channel_id=1, source_target_pairs={{0,4},{2,6},{4,0},{6,2},{8,12},{10,14},{12,8},{14,10},{16,20},{18,... | collective-permute-start | bytes 245768 | tf_op jit(solution)/shard_map/ppermute | solution.py:180
  29.4 5.9 %collective-permute-start.14 = (bf16[64,256]{1,0:T(8,128)(2,1)S(1)}, bf16[64,256]{1,0:T(8,128)(2,1)S(1)}, u32[]{:S(2)}, u32[]{:S(2)}) collective-permute-start(bf16[64,256]{1,0:T(8,128)(2,1)S(1)} %maximum_select_fusion.4), channel_id=1, source_target_pairs={{0,8},{2,10},{4,12},{6,14},{8,0},{10,2},{12,4},{14,6},{16,24},{18,... | collective-permute-start | bytes 98312 | tf_op jit(solution)/shard_map/ppermute | solution.py:180
  29.8 5.4 %collective-permute-start.5 = (f32[160,128]{1,0:T(8,128)S(1)}, f32[160,128]{1,0:T(8,128)S(1)}, u32[]{:S(2)}, u32[]{:S(2)}) collective-permute-start(f32[160,128]{1,0:T(8,128)S(1)} %add.63), channel_id=1, source_target_pairs={{0,2},{2,0},{4,6},{6,4},{8,10},{10,8},{12,14},{14,12},{16,18},{18,... | collective-permute-start | bytes 245768 | tf_op jit(solution)/shard_map/ppermute | solution.py:180
  35.2 8.4 %collective-permute-start.11 = (f32[640,128]{1,0:T(8,128)S(1)}, f32[640,128]{1,0:T(8,128)S(1)}, u32[]{:S(2)}, u32[]{:S(2)}) collective-permute-start(f32[640,128]{1,0:T(8,128)S(1)} %pad_maximum_fusion.refs_1_), channel_id=1, source_target_pairs={{0,1},{1,0},{2,3},{3,2},{4,5},{5,4},{6,7},{7,6},{8,9},{9,8},{10,11... | collective-permute-start | bytes 983048 | tf_op jit(solution)/shard_map/ppermute | solution.py:180
  35.3 6.9 %collective-permute-start.15 = (bf16[128,256]{1,0:T(8,128)(2,1)S(1)}, bf16[128,256]{1,0:T(8,128)(2,1)S(1)}, u32[]{:S(2)}, u32[]{:S(2)}) collective-permute-start(bf16[128,256]{1,0:T(8,128)(2,1)S(1)} %maximum_select_fusion.3), channel_id=1, source_target_pairs={{0,16},{2,18},{4,20},{6,22},{8,24},{10,26},{12,28},{14,30},{16,0},... | collective-permute-start | bytes 196616 | tf_op jit(solution)/shard_map/ppermute | solution.py:180
  42.2 1.4 %collective-permute-start.16 = (bf16[256,256]{1,0:T(8,128)(2,1)S(1)}, bf16[256,256]{1,0:T(8,128)(2,1)S(1)}, u32[]{:S(2)}, u32[]{:S(2)}) collective-permute-start(bf16[256,256]{1,0:T(8,128)(2,1)S(1)} %maximum_select_fusion.2.refs_3_), channel_id=1, source_target_pairs={{0,1},{1,0},{2,3},{3,2},{4,5},{5,4},{6,7},{7,6},{8,9},{9,8},{10,11... | collective-permute-start | bytes 393224 | tf_op jit(solution)/shard_map/ppermute | solution.py:180

commit v2 on v1

--- a/solution.py
+++ b/solution.py
@@ -10,7 +10,6 @@
 F32, BF16 = jnp.float32, jnp.bfloat16
 HALF = 128
 BLOCK = 64
-PIVOTS = 8
 VMEM = pltpu.VMEM
 
 
@@ -63,15 +62,13 @@
     shape = (8, width)
     lane = lax.broadcasted_iota(jnp.int32, shape, 1)
     sub = lax.broadcasted_iota(jnp.int32, shape, 0)
+    spread = lambda x: jnp.broadcast_to(x, shape)
     groups, result = list(groups), []
     for g in range(len(groups)):
         j = 8 * g
-        rows = [jnp.broadcast_to(groups[g][k : k + 1, :], shape) for k in range(8)]
-        a = {
-            (i, k): jnp.broadcast_to(groups[g][i : i + 1, j + k : j + k + 1], shape)
-            for i in range(8)
-            for k in range(i + 1)
-        }
+        columns = lambda group: [spread(group[:, j + k : j + k + 1]) for k in range(8)]
+        rows = [spread(groups[g][k : k + 1, :]) for k in range(8)]
+        a = {(i, k): spread(c[i : i + 1, :]) for k, c in enumerate(columns(groups[g])) for i in range(k, 8)}
         inside = (lane >= j) & (lane < j + 8)
         root, done, low = [], [], {}
         block = jnp.zeros(shape, F32)
@@ -91,41 +88,52 @@
         result.append(block)
         if g + 1 == len(groups):
             break
+        factors = []
+        for k, c in enumerate(columns(groups[g + 1])):
+            for m in range(k):
+                c = c - factors[m] * low[k, m]
+            factors.append(c * root[k])
+        x = jnp.where(inside, 0.0, groups[g + 1])
+        for k in range(8):
+            x = x - factors[k] * done[k]
+        groups[g + 1] = x
         update = [None] * 8
         for k in reversed(range(8)):
             x = done[k]
             for m in range(k + 1, 8):
                 x = x - low[m, k] * update[m]
             update[k] = x * root[k]
-        for n in range(g + 1, len(groups)):
+        for n in range(g + 2, len(groups)):
             x = jnp.where(inside, 0.0, groups[n])
-            for k in range(8):
-                x = x - jnp.broadcast_to(groups[n][:, j + k : j + k + 1], shape) * update[k]
+            for k, c in enumerate(columns(groups[n])):
+                x = x - c * update[k]
             groups[n] = x
     return result
 
 
 def inverse_factor(gram, out):
     n = gram.shape[0]
-    rest = gram
+    rest, corner = gram, gram[:BLOCK, :BLOCK]
     for at in range(0, n, BLOCK):
         end = at + BLOCK
         row = rest[:BLOCK]
-        inv = jnp.concatenate(eliminate([row[i : i + 8, at:end] for i in range(0, BLOCK, 8)], BLOCK), 0)
-        if end < n:
-            full = dot(inv, row, 1, 0)
-            joined = jnp.concatenate(([full[:, :at]] if at else []) + [inv, full[:, end:]], 1)
-            lane = lax.broadcasted_iota(jnp.int32, (BLOCK, n), 1)
-            out[at:end, :] = jnp.where(lane < end, joined, 0.0)
-            below = rest[BLOCK:]
-            lane = lax.broadcasted_iota(jnp.int32, below.shape, 1)
-            rest = jnp.where((lane >= at) & (lane < end), 0.0, below) - dot(joined[:, end:], joined, 0, 0)
-        else:
+        inv = jnp.concatenate(eliminate([corner[i : i + 8, :] for i in range(0, BLOCK, 8)], BLOCK), 0)
+        if end == n:
             out[at:end, :] = jnp.concatenate([dot(inv, row[:, :at], 1, 0), inv], 1) if at else inv
+            break
+        ahead = dot(inv, row[:, end : end + BLOCK], 1, 0)
+        corner = rest[BLOCK : 2 * BLOCK, end : end + BLOCK] - dot(ahead, ahead, 0, 0)
+        full = dot(inv, row, 1, 0)
+        joined = jnp.concatenate(([full[:, :at]] if at else []) + [inv, full[:, end:]], 1)
+        lane = lax.broadcasted_iota(jnp.int32, (BLOCK, n), 1)
+        out[at:end, :] = jnp.where(lane < end, joined, 0.0)
+        below = rest[BLOCK:]
+        lane = lax.broadcasted_iota(jnp.int32, below.shape, 1)
+        rest = jnp.where((lane >= at) & (lane < end), 0.0, below) - dot(joined[:, end:], joined, 0, 0)
 
 
 def final_kernel(
-    total, place, blocks, others, test, test_other, standard, standard_other, basis, loadings, moments, inverse, product
+    total, place, blocks, others, test, test_other, standard, standard_other, basis, loadings, moments, inverse, product, gathered
 ):
     samp, core = place[0], place[1]
     side = 2 * HALF
@@ -145,17 +153,22 @@
         column = pl.ds(pl.multiple_of((h + away - 2 * h * away) * HALF, HALF), HALF)
         moments[side + h * HALF : side + (h + 1) * HALF, column] = theirs[h]
         moments[column, side + h * HALF : side + (h + 1) * HALF] = theirs[h].T
-    tests = jnp.concatenate([test[...], test_other[...]], 0)
+    few = loadings.shape[0]
+    count = test.shape[0] // few
+    for ref, at in ((test, 0), (test_other, side)):
+        for i in range(count):
+            row = pl.multiple_of(at + (samp ^ source(i, count)) * few, few)
+            gathered[pl.ds(row, few), :] = ref[i * few : (i + 1) * few, :]
+    tests = gathered[...]
     product[...] = dot_pieces(pieces(moments[...]), tests, 1, 0)
     gram = dot_pieces_right(tests, pieces(product[...]), 0, 0)
     inverse_factor(gram, inverse)
     share = basis.shape[0]
     rows = pl.ds(pl.multiple_of(core * share, share), share)
-    sketch = dot(standard[rows, :], test[...], 1, 0, lax.Precision.DEFAULT) + dot(
-        standard_other[rows, :], test_other[...], 1, 0, lax.Precision.DEFAULT
+    sketch = dot(standard[rows, :], tests[:side], 1, 0, lax.Precision.DEFAULT) + dot(
+        standard_other[rows, :], tests[side:], 1, 0, lax.Precision.DEFAULT
     )
     basis[...] = math.sqrt(total) * dot(sketch, inverse[...], 1, 1)
-    few = loadings.shape[0]
     own = product[pl.ds(pl.multiple_of(samp * few, few), few), :]
     loadings[...] = dot(own, inverse[...], 1, 1)
 
@@ -180,33 +193,69 @@
     return lax.ppermute(x, axis, [(i, i ^ bit) for i in range(lax.axis_size(axis))])
 
 
-def upper(axis, bit):
-    return (lax.axis_index(axis) // bit) % 2
-
-
-def keep_half(x, axis, bit):
-    half, up = x.shape[0] // 2, upper(axis, bit)
-    kept = lax.dynamic_slice_in_dim(x, up * half, half, 0)
-    sent = lax.dynamic_slice_in_dim(x, (1 - up) * half, half, 0)
-    return kept + swap(sent, axis, bit)
-
-
-def join(x, axis, bit):
-    got = swap(x, axis, bit)
-    return jnp.where(upper(axis, bit) == 0, jnp.concatenate([x, got], 0), jnp.concatenate([got, x], 0))
-
-
-def sum_over(x, axis):
-    bits = [1 << i for i in range((lax.axis_size(axis) - 1).bit_length())]
-    half = x.shape[0] // 2
-    plans = ((bits[0], bits[2:3] + bits[1:2] + bits[3:]), (bits[1], bits[0:1] + bits[2:]))
-    parts = []
-    for part, (first, rest) in zip((x[:half], x[half:]), plans):
-        part = keep_half(part, axis, first)
-        for bit in rest:
-            part = part + swap(part, axis, bit)
-        parts.append(join(part, axis, first))
-    return jnp.concatenate(parts, 0)
+def swap_by_core(x, bits):
+    pairs = [(2 * i + c, 2 * (i ^ bits[c]) + c) for i in range(lax.axis_size("samp")) for c in range(2)]
+    return lax.ppermute(x, ("samp", "mark"), pairs)
+
+
+def upper(bits):
+    mine = jnp.where(lax.axis_index("mark") == 0, bits[0], bits[1])
+    return (lax.axis_index("samp") & mine) != 0
+
+
+def in_order(x, got, up):
+    return jnp.where(up, jnp.concatenate([got, x], 0), jnp.concatenate([x, got], 0))
+
+
+def samp_bits():
+    return [1 << i for i in range((lax.axis_size("samp") - 1).bit_length())]
+
+
+def step_kernel(x, got, blocks, got_blocks, total, joined):
+    total[...] = x[...] + got[...]
+    joined[: blocks.shape[0], :] = blocks[...]
+    joined[blocks.shape[0] :, :] = got_blocks[...]
+
+
+def sum_plan(count):
+    bits = [1 << i for i in range((count - 1).bit_length())]
+    if len(bits) < 3:
+        return list(zip(bits, bits[::-1]))
+    return list(zip(bits[:1] + bits[2:3] + bits[1:2] + bits[3:], bits[2:3] + bits[:1] + bits[3:] + bits[1:2]))
+
+
+def gather_plan(count):
+    return [1 << i for i in reversed(range((count - 1).bit_length()))]
+
+
+def source(i, count):
+    return sum(bit for n, bit in enumerate(gather_plan(count)) if i >> n & 1)
+
+
+def sum_and_gather(x, test, got_test):
+    count = lax.axis_size("samp")
+    sums, gathers = sum_plan(count), gather_plan(count)
+    half, up = x.shape[0] // 2, upper(sums[0])
+    kept = jnp.where(up, x[half:], x[:half])
+    sent = jnp.where(up, x[:half], x[half:])
+    test = jnp.concatenate([test, got_test], 0)
+    for step, pair in enumerate(sums):
+        got = swap_by_core(sent, pair)
+        if step + 1 < len(gathers):
+            got_test = swap(test, "samp", gathers[step + 1])
+            kept, test = call(
+                step_kernel,
+                [
+                    jax.ShapeDtypeStruct(kept.shape, kept.dtype),
+                    jax.ShapeDtypeStruct((2 * test.shape[0], test.shape[1]), test.dtype),
+                ],
+                [kept, got, test, got_test],
+            )
+        else:
+            kept = kept + got
+        sent = kept
+    test_other = swap(test, "mark", 1)
+    return in_order(kept, swap_by_core(kept, sums[0]), up), test, test_other
 
 
 def two_marks(dosage, alt_count, obs_count, sample_weight, test_matrix):
@@ -220,14 +269,14 @@
         [dosage, alt_count.reshape(1, cols), obs_count.reshape(1, cols), sample_weight.reshape(1, rows)],
     )
     standard_other = swap(standard, "mark", 1)
+    got_test = swap(test_matrix, "samp", gather_plan(lax.axis_size("samp"))[0])
     blocks = call(
-        moment_kernel, jax.ShapeDtypeStruct((5 * HALF, HALF), F32), [standard, standard_other], place
-    )
-    test = test_matrix
-    for i in range((lax.axis_size("samp") - 1).bit_length()):
-        test = join(test, "samp", 1 << i)
-    test_other = swap(test, "mark", 1)
-    blocks = sum_over(blocks, "samp")
+        moment_kernel,
+        jax.ShapeDtypeStruct((5 * HALF, HALF), F32),
+        [standard, standard_other],
+        place,
+    )
+    blocks, test, test_other = sum_and_gather(blocks, test_matrix, got_test)
     others = swap(blocks, "mark", 1)
     kernel = lambda *refs: final_kernel(samples, *refs)
     basis, loadings = call(
@@ -235,7 +284,7 @@
         [jax.ShapeDtypeStruct((rows // 2, rank), F32), jax.ShapeDtypeStruct((few, rank), F32)],
         [blocks, others, test, test_other, standard, standard_other],
         place,
-        [VMEM((2 * cols, 2 * cols), F32), VMEM((rank, rank), F32), VMEM((2 * cols, rank), F32)],
+        [VMEM((2 * cols, 2 * cols), F32), VMEM((rank, rank), F32), VMEM((2 * cols, rank), F32), VMEM((2 * cols, rank), BF16)],
     )
     return basis, loadings
 

time: 58.5 us -> 53.8 us (0.920)
  starting transfers between devices: 25.5 us -> 18 us
  waiting for transfers between devices: 14.3 us -> 18.7 us
  Pallas kernels: 15.8 us -> 14.4 us
    ppermute x17 -> x7, starting transfers between devices: 25.5 us -> 9.71 us  [swap(): lax.ppermute(x, axis, [(i, i ^ bit) for i in range(lax.axis_size(axis))])]
    ppermute x0 -> x5, waiting for transfers between devices: none -> 10 us  [swap_by_core(): return lax.ppermute(x, ('samp', 'mark'), pairs)]
    ppermute x0 -> x5, starting transfers between devices: none -> 8.29 us  [swap_by_core(): return lax.ppermute(x, ('samp', 'mark'), pairs)]
    ppermute x17 -> x7, waiting for transfers between devices: 14.3 us -> 8.65 us  [swap(): lax.ppermute(x, axis, [(i, i ^ bit) for i in range(lax.axis_size(axis))])]
    pallas_call x3 -> x6, Pallas kernels: 15.8 us -> 14.4 us  [call(): pl.pallas_call(kernel, out_shape=shapes, in_specs=specs, out_specs=[vmem]...]
    unnamed x10 -> x11, local copies, waits for them, and re-layouts: 1.64 us -> 1.66 us
  transfers between devices with their start and end apart: 17 -> 12, of which waited for: 8 -> 7; matrix products, arithmetic and copies ran while one was open for 0% -> 0% of each run, Pallas kernels for 0% -> 2%
where the time goes in v2:
time: 53.8 us; the launch traced here: 53.6 us
  waiting for transfers between devices  18.7 us (35%)
  starting transfers between devices  18 us (33%)
  Pallas kernels  14.4 us (27%)
  local copies, waits for them, and re-layouts  1.66 us (3%)
  between operations  0.72 us (1%)
    pallas_call x6, Pallas kernels, call(): pl.pallas_call(kernel, out_shape=shapes, in_specs=specs, out_specs=[vmem]...  14.4 us
    ppermute x5, waiting for transfers between devices, swap_by_core(): return lax.ppermute(x, ('samp', 'mark'), pairs)  10 us
    ppermute x7, starting transfers between devices, swap(): lax.ppermute(x, axis, [(i, i ^ bit) for i in range(lax.axis_size(axis))])  9.71 us
    ppermute x7, waiting for transfers between devices, swap(): lax.ppermute(x, axis, [(i, i ^ bit) for i in range(lax.axis_size(axis))])  8.65 us
    ppermute x5, starting transfers between devices, swap_by_core(): return lax.ppermute(x, ('samp', 'mark'), pairs)  8.29 us
    unnamed x11, local copies, waits for them, and re-layouts  1.66 us
  transfers between devices with their start and end apart: 12, of which 7 were waited for; matrix products, arithmetic and copies ran while one was open for 0% of the time, Pallas kernels for 2%

profile of v2, /device:TPU:0, one launch (start us, length us, event | category | flops | bytes accessed | tf_op | source)
XLA Modules:
  0.0 53.6 jit_solution(18184450775175454641)
XLA Ops:
  0.7 0.7 %copy-done.3 = s32[256]{0:T(256)S(1)} copy-done((s32[256]{0:T(256)S(1)}, s32[256]{0:T(256)}, u32[]{:S(2)}) %copy-start.3) | copy-done | bytes 1048
  1.3 0.9 %copy-done = bf16[512,256]{1,0:T(8,128)(2,1)S(1)} copy-done((bf16[512,256]{1,0:T(8,128)(2,1)S(1)}, bf16[512,256]{1,0:T(8,128)(2,1)}, u32[]{:S(2)}) %copy-start) | copy-done | bytes 262168
  2.3 0.1 shard_map.68.own.refs_5_
  2.5 0.5 collective-permute-start
  3.0 4.0 %collective-permute-start.2 = (bf16[16,256]{1,0:T(8,128)(2,1)S(1)}, bf16[16,256]{1,0:T(8,128)(2,1)S(1)}, u32[]{:S(2)}, u32[]{:S(2)}) collective-permute-start(bf16[16,256]{1,0:T(8,128)(2,1)S(1)} %copy-done.4), channel_id=1, source_target_pairs={{0,16},{2,18},{4,20},{6,22},{8,24},{10,26},{12,28},{14,30},{16,0},... | collective-permute-start | bytes 24584 | tf_op jit(solution)/shard_map/ppermute | solution.py:193
  7.0 0.1 pad_add_fusion.place.refs_0_
  7.1 0.9 %shard_map.69 = f32[640,128]{1,0:T(8,128)S(1)} custom-call(s32[2]{0:T(128)S(1)} %pad_add_fusion.place.refs_0_, bf16[512,256]{1,0:T(8,128)(2,1)S(1)} %shard_map.68.own.refs_5_, bf16[512,256]{1,0:T(8,128)(2,1)S(1)} %collective-permute-done.other.refs_6_), custom_call_target="tpu_custom_call" | custom-call | tf_op jit(solution)/shard_map/pallas_call | solution.py:182
  8.1 1.6 %collective-permute-start.1 = (f32[320,128]{1,0:T(8,128)S(1)}, f32[320,128]{1,0:T(8,128)S(1)}, u32[]{:S(2)}, u32[]{:S(2)}) collective-permute-start(f32[320,128]{1,0:T(8,128)S(1)} %get-tuple-element.14), channel_id=1, source_target_pairs={{0,2},{1,9},{2,0},{3,11},{4,6},{5,13},{6,4},{7,15},{8,10},{9,1},{1... | collective-permute-start | bytes 491528 | tf_op jit(solution)/shard_map/ppermute | solution.py:198
  9.6 1.6 %collective-permute-start.3 = (bf16[32,256]{1,0:T(8,128)(2,1)S(1)}, bf16[32,256]{1,0:T(8,128)(2,1)S(1)}, u32[]{:S(2)}, u32[]{:S(2)}) collective-permute-start(bf16[32,256]{1,0:T(8,128)(2,1)S(1)} %constant_dynamic-update-slice_fusion.blocks), channel_id=1, source_target_pairs={{0,8},{2,10},{4,12},{6,14},{8,0},{10,2},{12,4},{14,6},{16,24},{18,... | collective-permute-start | bytes 49160 | tf_op jit(solution)/shard_map/ppermute | solution.py:193
  11.2 2.2 %collective-permute-done.3.got_blocks = bf16[32,256]{1,0:T(8,128)(2,1)S(1)} collective-permute-done((bf16[32,256]{1,0:T(8,128)(2,1)S(1)}, bf16[32,256]{1,0:T(8,128)(2,1)S(1)}, u32[]{:S(2)}, u32[]{:S(2)}) %collective-permute-start.3) | collective-permute-done | bytes 16416 | tf_op jit(solution)/shard_map/ppermute | solution.py:193
  13.4 0.1 collective-permute-done.1.got
  13.5 1.6 %collective-permute-start.4 = (f32[320,128]{1,0:T(8,128)S(1)}, f32[320,128]{1,0:T(8,128)S(1)}, u32[]{:S(2)}, u32[]{:S(2)}) collective-permute-start(f32[320,128]{1,0:T(8,128)S(1)} %get-tuple-element.8.x), channel_id=1, source_target_pairs={{0,8},{1,3},{2,10},{3,1},{4,12},{5,7},{6,14},{7,5},{8,0},{9,11},{1... | collective-permute-start | bytes 491528 | tf_op jit(solution)/shard_map/ppermute | solution.py:198
  15.1 1.5 %collective-permute-start.5 = (bf16[64,256]{1,0:T(8,128)(2,1)S(1)}, bf16[64,256]{1,0:T(8,128)(2,1)S(1)}, u32[]{:S(2)}, u32[]{:S(2)}) collective-permute-start(bf16[64,256]{1,0:T(8,128)(2,1)S(1)} %get-tuple-element.9.blocks), channel_id=1, source_target_pairs={{0,4},{2,6},{4,0},{6,2},{8,12},{10,14},{12,8},{14,10},{16,20},{18,... | collective-permute-start | bytes 98312 | tf_op jit(solution)/shard_map/ppermute | solution.py:193
  16.6 2.4 %collective-permute-done.5.got_blocks = bf16[64,256]{1,0:T(8,128)(2,1)S(1)} collective-permute-done((bf16[64,256]{1,0:T(8,128)(2,1)S(1)}, bf16[64,256]{1,0:T(8,128)(2,1)S(1)}, u32[]{:S(2)}, u32[]{:S(2)}) %collective-permute-start.5) | collective-permute-done | bytes 32800 | tf_op jit(solution)/shard_map/ppermute | solution.py:193
  19.1 1.6 %collective-permute-start.6 = (f32[320,128]{1,0:T(8,128)S(1)}, f32[320,128]{1,0:T(8,128)S(1)}, u32[]{:S(2)}, u32[]{:S(2)}) collective-permute-start(f32[320,128]{1,0:T(8,128)S(1)} %get-tuple-element.10.x), channel_id=1, source_target_pairs={{0,4},{1,17},{2,6},{3,19},{4,0},{5,21},{6,2},{7,23},{8,12},{9,25},... | collective-permute-start | bytes 491528 | tf_op jit(solution)/shard_map/ppermute | solution.py:198
  20.6 1.5 %collective-permute-start.7 = (bf16[128,256]{1,0:T(8,128)(2,1)S(1)}, bf16[128,256]{1,0:T(8,128)(2,1)S(1)}, u32[]{:S(2)}, u32[]{:S(2)}) collective-permute-start(bf16[128,256]{1,0:T(8,128)(2,1)S(1)} %get-tuple-element.11.blocks), channel_id=1, source_target_pairs={{0,2},{2,0},{4,6},{6,4},{8,10},{10,8},{12,14},{14,12},{16,18},{18,... | collective-permute-start | bytes 196616 | tf_op jit(solution)/shard_map/ppermute | solution.py:193
  22.1 2.8 %collective-permute-done.7.got_blocks = bf16[128,256]{1,0:T(8,128)(2,1)S(1)} collective-permute-done((bf16[128,256]{1,0:T(8,128)(2,1)S(1)}, bf16[128,256]{1,0:T(8,128)(2,1)S(1)}, u32[]{:S(2)}, u32[]{:S(2)}) %collective-permute-start.7) | collective-permute-done | bytes 65568 | tf_op jit(solution)/shard_map/ppermute | solution.py:193
  24.9 1.9 %collective-permute-start.8 = (f32[320,128]{1,0:T(8,128)S(1)}, f32[320,128]{1,0:T(8,128)S(1)}, u32[]{:S(2)}, u32[]{:S(2)}) collective-permute-start(f32[320,128]{1,0:T(8,128)S(1)} %get-tuple-element.12), channel_id=1, source_target_pairs={{0,16},{1,5},{2,18},{3,7},{4,20},{5,1},{6,22},{7,3},{8,24},{9,13},... | collective-permute-start | bytes 491528 | tf_op jit(solution)/shard_map/ppermute | solution.py:198
  26.9 6.1 %collective-permute-done.8 = f32[320,128]{1,0:T(8,128)S(1)} collective-permute-done((f32[320,128]{1,0:T(8,128)S(1)}, f32[320,128]{1,0:T(8,128)S(1)}, u32[]{:S(2)}, u32[]{:S(2)}) %collective-permute-start.8) | collective-permute-done | bytes 163872 | tf_op jit(solution)/shard_map/ppermute | solution.py:198
  33.0 1.6 %collective-permute-start.9 = (f32[320,128]{1,0:T(8,128)S(1)}, f32[320,128]{1,0:T(8,128)S(1)}, u32[]{:S(2)}, u32[]{:S(2)}) collective-permute-start(f32[320,128]{1,0:T(8,128)S(1)} %add.3), channel_id=1, source_target_pairs={{0,2},{1,9},{2,0},{3,11},{4,6},{5,13},{6,4},{7,15},{8,10},{9,1},{1... | collective-permute-start | bytes 491528 | tf_op jit(solution)/shard_map/ppermute | solution.py:198
  34.6 3.8 %collective-permute-done.9 = f32[320,128]{1,0:T(8,128)S(1)} collective-permute-done((f32[320,128]{1,0:T(8,128)S(1)}, f32[320,128]{1,0:T(8,128)S(1)}, u32[]{:S(2)}, u32[]{:S(2)}) %collective-permute-start.9) | collective-permute-done | bytes 163872 | tf_op jit(solution)/shard_map/ppermute | solution.py:198
  38.5 0.5 collective-permute-start.11
  39.0 1.3 %collective-permute-done.11.refs_4_ = bf16[256,256]{1,0:T(8,128)(2,1)S(1)} collective-permute-done((bf16[256,256]{1,0:T(8,128)(2,1)S(1)}, bf16[256,256]{1,0:T(8,128)(2,1)S(1)}, u32[]{:S(2)}, u32[]{:S(2)}) %collective-permute-start.11) | collective-permute-done | bytes 131104 | tf_op jit(solution)/shard_map/ppermute | solution.py:193
  40.3 13.3 %shard_map.73 = (f32[256,256]{1,0:T(8,128)}, f32[16,256]{1,0:T(8,128)}) custom-call(s32[2]{0:T(128)S(1)} %pad_add_fusion.place.refs_0_, f32[640,128]{1,0:T(8,128)S(1)} %maximum_select_fusion.refs_1_, f32[640,128]{1,0:T(8,128)S(1)} %collective-permute-done.10.refs_2_, bf16[256,256]{1,0:T(8,128)(2,1)S(1)} %get-tuple-element.13.refs_3_, ...), custom_call_target="tpu_custom_call" | custom-call | tf_op jit(solution)/shard_map/pallas_call | solution.py:182
  (22 shorter events, 0.3 us)
Async XLA Ops:
  0.6 0.7 %copy-start.3 = (s32[256]{0:T(256)S(1)}, s32[256]{0:T(256)}, u32[]{:S(2)}) copy-start(s32[256]{0:T(256)} %param.7) | copy-start | bytes 3076
  0.6 0.7 %copy-start.1 = (f32[512]{0:T(512)S(1)}, f32[512]{0:T(512)}, u32[]{:S(2)}) copy-start(f32[512]{0:T(512)} %param.8) | copy-start | bytes 6148
  0.7 0.7 %copy-start.2 = (s32[256]{0:T(256)S(1)}, s32[256]{0:T(256)}, u32[]{:S(2)}) copy-start(s32[256]{0:T(256)} %param.6) | copy-start | bytes 3076
  1.3 0.9 %copy-start = (bf16[512,256]{1,0:T(8,128)(2,1)S(1)}, bf16[512,256]{1,0:T(8,128)(2,1)}, u32[]{:S(2)}) copy-start(bf16[512,256]{1,0:T(8,128)(2,1)} %dosage.1) | copy-start | bytes 786436
  2.3 0.7 %copy-start.4 = (bf16[16,256]{1,0:T(8,128)(2,1)S(1)}, bf16[16,256]{1,0:T(8,128)(2,1)}, u32[]{:S(2)}) copy-start(bf16[16,256]{1,0:T(8,128)(2,1)} %param.9) | copy-start | bytes 24580
  2.5 4.7 %collective-permute-start = (bf16[512,256]{1,0:T(8,128)(2,1)S(1)}, bf16[512,256]{1,0:T(8,128)(2,1)S(1)}, u32[]{:S(2)}, u32[]{:S(2)}) collective-permute-start(bf16[512,256]{1,0:T(8,128)(2,1)S(1)} %shard_map.68.own.refs_5_), channel_id=1, source_target_pairs={{0,1},{1,0},{2,3},{3,2},{4,5},{5,4},{6,7},{7,6},{8,9},{9,8},{10,11... | collective-permute-start | bytes 786440 | tf_op jit(solution)/shard_map/ppermute | solution.py:193
  3.0 6.6 %collective-permute-start.2 = (bf16[16,256]{1,0:T(8,128)(2,1)S(1)}, bf16[16,256]{1,0:T(8,128)(2,1)S(1)}, u32[]{:S(2)}, u32[]{:S(2)}) collective-permute-start(bf16[16,256]{1,0:T(8,128)(2,1)S(1)} %copy-done.4), channel_id=1, source_target_pairs={{0,16},{2,18},{4,20},{6,22},{8,24},{10,26},{12,28},{14,30},{16,0},... | collective-permute-start | bytes 24584 | tf_op jit(solution)/shard_map/ppermute | solution.py:193
  8.1 5.4 %collective-permute-start.1 = (f32[320,128]{1,0:T(8,128)S(1)}, f32[320,128]{1,0:T(8,128)S(1)}, u32[]{:S(2)}, u32[]{:S(2)}) collective-permute-start(f32[320,128]{1,0:T(8,128)S(1)} %get-tuple-element.14), channel_id=1, source_target_pairs={{0,2},{1,9},{2,0},{3,11},{4,6},{5,13},{6,4},{7,15},{8,10},{9,1},{1... | collective-permute-start | bytes 491528 | tf_op jit(solution)/shard_map/ppermute | solution.py:198
  9.6 3.7 %collective-permute-start.3 = (bf16[32,256]{1,0:T(8,128)(2,1)S(1)}, bf16[32,256]{1,0:T(8,128)(2,1)S(1)}, u32[]{:S(2)}, u32[]{:S(2)}) collective-permute-start(bf16[32,256]{1,0:T(8,128)(2,1)S(1)} %constant_dynamic-update-slice_fusion.blocks), channel_id=1, source_target_pairs={{0,8},{2,10},{4,12},{6,14},{8,0},{10,2},{12,4},{14,6},{16,24},{18,... | collective-permute-start | bytes 49160 | tf_op jit(solution)/shard_map/ppermute | solution.py:193
  13.5 5.6 %collective-permute-start.4 = (f32[320,128]{1,0:T(8,128)S(1)}, f32[320,128]{1,0:T(8,128)S(1)}, u32[]{:S(2)}, u32[]{:S(2)}) collective-permute-start(f32[320,128]{1,0:T(8,128)S(1)} %get-tuple-element.8.x), channel_id=1, source_target_pairs={{0,8},{1,3},{2,10},{3,1},{4,12},{5,7},{6,14},{7,5},{8,0},{9,11},{1... | collective-permute-start | bytes 491528 | tf_op jit(solution)/shard_map/ppermute | solution.py:198
  15.1 3.9 %collective-permute-start.5 = (bf16[64,256]{1,0:T(8,128)(2,1)S(1)}, bf16[64,256]{1,0:T(8,128)(2,1)S(1)}, u32[]{:S(2)}, u32[]{:S(2)}) collective-permute-start(bf16[64,256]{1,0:T(8,128)(2,1)S(1)} %get-tuple-element.9.blocks), channel_id=1, source_target_pairs={{0,4},{2,6},{4,0},{6,2},{8,12},{10,14},{12,8},{14,10},{16,20},{18,... | collective-permute-start | bytes 98312 | tf_op jit(solution)/shard_map/ppermute | solution.py:193
  19.1 5.9 %collective-permute-start.6 = (f32[320,128]{1,0:T(8,128)S(1)}, f32[320,128]{1,0:T(8,128)S(1)}, u32[]{:S(2)}, u32[]{:S(2)}) collective-permute-start(f32[320,128]{1,0:T(8,128)S(1)} %get-tuple-element.10.x), channel_id=1, source_target_pairs={{0,4},{1,17},{2,6},{3,19},{4,0},{5,21},{6,2},{7,23},{8,12},{9,25},... | collective-permute-start | bytes 491528 | tf_op jit(solution)/shard_map/ppermute | solution.py:198
  20.6 4.3 %collective-permute-start.7 = (bf16[128,256]{1,0:T(8,128)(2,1)S(1)}, bf16[128,256]{1,0:T(8,128)(2,1)S(1)}, u32[]{:S(2)}, u32[]{:S(2)}) collective-permute-start(bf16[128,256]{1,0:T(8,128)(2,1)S(1)} %get-tuple-element.11.blocks), channel_id=1, source_target_pairs={{0,2},{2,0},{4,6},{6,4},{8,10},{10,8},{12,14},{14,12},{16,18},{18,... | collective-permute-start | bytes 196616 | tf_op jit(solution)/shard_map/ppermute | solution.py:193
  24.9 8.0 %collective-permute-start.8 = (f32[320,128]{1,0:T(8,128)S(1)}, f32[320,128]{1,0:T(8,128)S(1)}, u32[]{:S(2)}, u32[]{:S(2)}) collective-permute-start(f32[320,128]{1,0:T(8,128)S(1)} %get-tuple-element.12), channel_id=1, source_target_pairs={{0,16},{1,5},{2,18},{3,7},{4,20},{5,1},{6,22},{7,3},{8,24},{9,13},... | collective-permute-start | bytes 491528 | tf_op jit(solution)/shard_map/ppermute | solution.py:198
  33.0 5.4 %collective-permute-start.9 = (f32[320,128]{1,0:T(8,128)S(1)}, f32[320,128]{1,0:T(8,128)S(1)}, u32[]{:S(2)}, u32[]{:S(2)}) collective-permute-start(f32[320,128]{1,0:T(8,128)S(1)} %add.3), channel_id=1, source_target_pairs={{0,2},{1,9},{2,0},{3,11},{4,6},{5,13},{6,4},{7,15},{8,10},{9,1},{1... | collective-permute-start | bytes 491528 | tf_op jit(solution)/shard_map/ppermute | solution.py:198
  38.4 1.9 %collective-permute-start.10 = (f32[640,128]{1,0:T(8,128)S(1)}, f32[640,128]{1,0:T(8,128)S(1)}, u32[]{:S(2)}, u32[]{:S(2)}) collective-permute-start(f32[640,128]{1,0:T(8,128)S(1)} %maximum_select_fusion.refs_1_), channel_id=1, source_target_pairs={{0,1},{1,0},{2,3},{3,2},{4,5},{5,4},{6,7},{7,6},{8,9},{9,8},{10,11... | collective-permute-start | bytes 983048 | tf_op jit(solution)/shard_map/ppermute | solution.py:193
  38.5 1.8 %collective-permute-start.11 = (bf16[256,256]{1,0:T(8,128)(2,1)S(1)}, bf16[256,256]{1,0:T(8,128)(2,1)S(1)}, u32[]{:S(2)}, u32[]{:S(2)}) collective-permute-start(bf16[256,256]{1,0:T(8,128)(2,1)S(1)} %get-tuple-element.13.refs_3_), channel_id=1, source_target_pairs={{0,1},{1,0},{2,3},{3,2},{4,5},{5,4},{6,7},{7,6},{8,9},{9,8},{10,11... | collective-permute-start | bytes 393224 | tf_op jit(solution)/shard_map/ppermute | solution.py:193

commit v3 on v2

--- a/solution.py
+++ b/solution.py
@@ -9,7 +9,7 @@
 
 F32, BF16 = jnp.float32, jnp.bfloat16
 HALF = 128
-BLOCK = 64
+BLOCK = 128
 VMEM = pltpu.VMEM
 
 
@@ -58,17 +58,23 @@
         out[i * HALF : (i + 1) * HALF, :] = dot(a, b, 0, 0, lax.Precision.DEFAULT)
 
 
-def eliminate(groups, width):
-    shape = (8, width)
+def eliminate(groups, slots):
+    shape = groups[0].shape
     lane = lax.broadcasted_iota(jnp.int32, shape, 1)
     sub = lax.broadcasted_iota(jnp.int32, shape, 0)
     spread = lambda x: jnp.broadcast_to(x, shape)
     groups, result = list(groups), []
     for g in range(len(groups)):
         j = 8 * g
-        columns = lambda group: [spread(group[:, j + k : j + k + 1]) for k in range(8)]
-        rows = [spread(groups[g][k : k + 1, :]) for k in range(8)]
-        a = {(i, k): spread(c[i : i + 1, :]) for k, c in enumerate(columns(groups[g])) for i in range(k, 8)}
+        columns = lambda group: [
+            jnp.take_along_axis(group, jnp.full(shape, j + k, jnp.int32), axis=1) for k in range(8)
+        ]
+        slot = 9 * (g % 4)
+        slots[slot + 8] = groups[g]
+        rows = [spread(slots[slot + 8, k : k + 1, :]) for k in range(8)]
+        for k, c in enumerate(columns(groups[g])):
+            slots[slot + k] = c
+        a = {(i, k): spread(slots[slot + k, i : i + 1, :]) for k in range(8) for i in range(k, 8)}
         inside = (lane >= j) & (lane < j + 8)
         root, done, low = [], [], {}
         block = jnp.zeros(shape, F32)
@@ -111,13 +117,13 @@
     return result
 
 
-def inverse_factor(gram, out):
+def inverse_factor(gram, out, slots):
     n = gram.shape[0]
     rest, corner = gram, gram[:BLOCK, :BLOCK]
     for at in range(0, n, BLOCK):
         end = at + BLOCK
         row = rest[:BLOCK]
-        inv = jnp.concatenate(eliminate([corner[i : i + 8, :] for i in range(0, BLOCK, 8)], BLOCK), 0)
+        inv = jnp.concatenate(eliminate([corner[i : i + 8, :] for i in range(0, BLOCK, 8)], slots), 0)
         if end == n:
             out[at:end, :] = jnp.concatenate([dot(inv, row[:, :at], 1, 0), inv], 1) if at else inv
             break
@@ -133,7 +139,7 @@
 
 
 def final_kernel(
-    total, place, blocks, others, test, test_other, standard, standard_other, basis, loadings, moments, inverse, product, gathered
+    total, place, blocks, others, test, test_other, standard, standard_other, basis, loadings, moments, inverse, product, gathered, slots
 ):
     samp, core = place[0], place[1]
     side = 2 * HALF
@@ -162,7 +168,7 @@
     tests = gathered[...]
     product[...] = dot_pieces(pieces(moments[...]), tests, 1, 0)
     gram = dot_pieces_right(tests, pieces(product[...]), 0, 0)
-    inverse_factor(gram, inverse)
+    inverse_factor(gram, inverse, slots)
     share = basis.shape[0]
     rows = pl.ds(pl.multiple_of(core * share, share), share)
     sketch = dot(standard[rows, :], tests[:side], 1, 0, lax.Precision.DEFAULT) + dot(
@@ -284,7 +290,7 @@
         [jax.ShapeDtypeStruct((rows // 2, rank), F32), jax.ShapeDtypeStruct((few, rank), F32)],
         [blocks, others, test, test_other, standard, standard_other],
         place,
-        [VMEM((2 * cols, 2 * cols), F32), VMEM((rank, rank), F32), VMEM((2 * cols, rank), F32), VMEM((2 * cols, rank), BF16)],
+        [VMEM((2 * cols, 2 * cols), F32), VMEM((rank, rank), F32), VMEM((2 * cols, rank), F32), VMEM((2 * cols, rank), BF16), VMEM((36, 8, BLOCK), F32)],
     )
     return basis, loadings
 
@@ -314,7 +320,10 @@
     samp, mark = mesh.shape["samp"], mesh.shape["mark"]
 
     def per_device(dosage, *rest):
-        fits = mark == 2 and samp >= 4 and samp & (samp - 1) == 0 and dosage.shape[1] == 2 * HALF
+        samples, width = dosage.shape
+        few, rank = rest[-1].shape
+        fits = mark == 2 and samp >= 4 and samp & (samp - 1) == 0 and width == 2 * HALF
+        fits = fits and samples % (2 * HALF) == 0 and rank % BLOCK == 0 and few % 16 == 0
         return (two_marks if fits else any_marks)(dosage, *rest)
 
     return jax.shard_map(

time: 53.8 us -> 50.7 us (0.942)
  Pallas kernels: 14.4 us -> 11.3 us
    pallas_call x6, Pallas kernels: 14.4 us -> 11.3 us  [call(): pl.pallas_call(kernel, out_shape=shapes, in_specs=specs, out_specs=[vmem]...]
where the time goes in v3:
time: 50.7 us; the launch traced here: 50.5 us
  waiting for transfers between devices  18.7 us (37%)
  starting transfers between devices  18 us (36%)
  Pallas kernels  11.3 us (22%)
  local copies, waits for them, and re-layouts  1.66 us (3%)
  between operations  0.72 us (1%)
    pallas_call x6, Pallas kernels, call(): pl.pallas_call(kernel, out_shape=shapes, in_specs=specs, out_specs=[vmem]...  11.3 us
    ppermute x5, waiting for transfers between devices, swap_by_core(): return lax.ppermute(x, ('samp', 'mark'), pairs)  10 us
    ppermute x7, starting transfers between devices, swap(): lax.ppermute(x, axis, [(i, i ^ bit) for i in range(lax.axis_size(axis))])  9.71 us
    ppermute x7, waiting for transfers between devices, swap(): lax.ppermute(x, axis, [(i, i ^ bit) for i in range(lax.axis_size(axis))])  8.65 us
    ppermute x5, starting transfers between devices, swap_by_core(): return lax.ppermute(x, ('samp', 'mark'), pairs)  8.29 us
    unnamed x11, local copies, waits for them, and re-layouts  1.66 us
  transfers between devices with their start and end apart: 12, of which 7 were waited for; matrix products, arithmetic and copies ran while one was open for 0% of the time, Pallas kernels for 2%

profile of v3, /device:TPU:0, one launch (start us, length us, event | category | flops | bytes accessed | tf_op | source)
XLA Modules:
  0.0 50.5 jit_solution(10910520247482879350)
XLA Ops:
  0.7 0.7 %copy-done.3 = s32[256]{0:T(256)S(1)} copy-done((s32[256]{0:T(256)S(1)}, s32[256]{0:T(256)}, u32[]{:S(2)}) %copy-start.3) | copy-done | bytes 1048
  1.3 0.9 %copy-done = bf16[512,256]{1,0:T(8,128)(2,1)S(1)} copy-done((bf16[512,256]{1,0:T(8,128)(2,1)S(1)}, bf16[512,256]{1,0:T(8,128)(2,1)}, u32[]{:S(2)}) %copy-start) | copy-done | bytes 262168
  2.3 0.1 shard_map.68.own.refs_5_
  2.5 0.5 %collective-permute-start = (bf16[512,256]{1,0:T(8,128)(2,1)S(1)}, bf16[512,256]{1,0:T(8,128)(2,1)S(1)}, u32[]{:S(2)}, u32[]{:S(2)}) collective-permute-start(bf16[512,256]{1,0:T(8,128)(2,1)S(1)} %shard_map.68.own.refs_5_), channel_id=1, source_target_pairs={{0,1},{1,0},{2,3},{3,2},{4,5},{5,4},{6,7},{7,6},{8,9},{9,8},{10,11... | collective-permute-start | bytes 786440 | tf_op jit(solution)/shard_map/ppermute | solution.py:199
  3.0 4.0 %collective-permute-start.2 = (bf16[16,256]{1,0:T(8,128)(2,1)S(1)}, bf16[16,256]{1,0:T(8,128)(2,1)S(1)}, u32[]{:S(2)}, u32[]{:S(2)}) collective-permute-start(bf16[16,256]{1,0:T(8,128)(2,1)S(1)} %copy-done.4), channel_id=1, source_target_pairs={{0,16},{2,18},{4,20},{6,22},{8,24},{10,26},{12,28},{14,30},{16,0},... | collective-permute-start | bytes 24584 | tf_op jit(solution)/shard_map/ppermute | solution.py:199
  7.0 0.1 pad_add_fusion.place.refs_0_
  7.1 0.9 %shard_map.69 = f32[640,128]{1,0:T(8,128)S(1)} custom-call(s32[2]{0:T(128)S(1)} %pad_add_fusion.place.refs_0_, bf16[512,256]{1,0:T(8,128)(2,1)S(1)} %shard_map.68.own.refs_5_, bf16[512,256]{1,0:T(8,128)(2,1)S(1)} %collective-permute-done.other.refs_6_), custom_call_target="tpu_custom_call" | custom-call | tf_op jit(solution)/shard_map/pallas_call | solution.py:188
  8.1 1.6 %collective-permute-start.1 = (f32[320,128]{1,0:T(8,128)S(1)}, f32[320,128]{1,0:T(8,128)S(1)}, u32[]{:S(2)}, u32[]{:S(2)}) collective-permute-start(f32[320,128]{1,0:T(8,128)S(1)} %get-tuple-element.14), channel_id=1, source_target_pairs={{0,2},{1,9},{2,0},{3,11},{4,6},{5,13},{6,4},{7,15},{8,10},{9,1},{1... | collective-permute-start | bytes 491528 | tf_op jit(solution)/shard_map/ppermute | solution.py:204
  9.6 1.6 %collective-permute-start.3 = (bf16[32,256]{1,0:T(8,128)(2,1)S(1)}, bf16[32,256]{1,0:T(8,128)(2,1)S(1)}, u32[]{:S(2)}, u32[]{:S(2)}) collective-permute-start(bf16[32,256]{1,0:T(8,128)(2,1)S(1)} %constant_dynamic-update-slice_fusion.blocks), channel_id=1, source_target_pairs={{0,8},{2,10},{4,12},{6,14},{8,0},{10,2},{12,4},{14,6},{16,24},{18,... | collective-permute-start | bytes 49160 | tf_op jit(solution)/shard_map/ppermute | solution.py:199
  11.2 2.2 %collective-permute-done.3.got_blocks = bf16[32,256]{1,0:T(8,128)(2,1)S(1)} collective-permute-done((bf16[32,256]{1,0:T(8,128)(2,1)S(1)}, bf16[32,256]{1,0:T(8,128)(2,1)S(1)}, u32[]{:S(2)}, u32[]{:S(2)}) %collective-permute-start.3) | collective-permute-done | bytes 16416 | tf_op jit(solution)/shard_map/ppermute | solution.py:199
  13.4 0.1 collective-permute-done.1.got
  13.5 1.6 %collective-permute-start.4 = (f32[320,128]{1,0:T(8,128)S(1)}, f32[320,128]{1,0:T(8,128)S(1)}, u32[]{:S(2)}, u32[]{:S(2)}) collective-permute-start(f32[320,128]{1,0:T(8,128)S(1)} %get-tuple-element.8.x), channel_id=1, source_target_pairs={{0,8},{1,3},{2,10},{3,1},{4,12},{5,7},{6,14},{7,5},{8,0},{9,11},{1... | collective-permute-start | bytes 491528 | tf_op jit(solution)/shard_map/ppermute | solution.py:204
  15.1 1.5 %collective-permute-start.5 = (bf16[64,256]{1,0:T(8,128)(2,1)S(1)}, bf16[64,256]{1,0:T(8,128)(2,1)S(1)}, u32[]{:S(2)}, u32[]{:S(2)}) collective-permute-start(bf16[64,256]{1,0:T(8,128)(2,1)S(1)} %get-tuple-element.9.blocks), channel_id=1, source_target_pairs={{0,4},{2,6},{4,0},{6,2},{8,12},{10,14},{12,8},{14,10},{16,20},{18,... | collective-permute-start | bytes 98312 | tf_op jit(solution)/shard_map/ppermute | solution.py:199
  16.6 2.4 %collective-permute-done.5.got_blocks = bf16[64,256]{1,0:T(8,128)(2,1)S(1)} collective-permute-done((bf16[64,256]{1,0:T(8,128)(2,1)S(1)}, bf16[64,256]{1,0:T(8,128)(2,1)S(1)}, u32[]{:S(2)}, u32[]{:S(2)}) %collective-permute-start.5) | collective-permute-done | bytes 32800 | tf_op jit(solution)/shard_map/ppermute | solution.py:199
  19.1 1.6 %collective-permute-start.6 = (f32[320,128]{1,0:T(8,128)S(1)}, f32[320,128]{1,0:T(8,128)S(1)}, u32[]{:S(2)}, u32[]{:S(2)}) collective-permute-start(f32[320,128]{1,0:T(8,128)S(1)} %get-tuple-element.10.x), channel_id=1, source_target_pairs={{0,4},{1,17},{2,6},{3,19},{4,0},{5,21},{6,2},{7,23},{8,12},{9,25},... | collective-permute-start | bytes 491528 | tf_op jit(solution)/shard_map/ppermute | solution.py:204
  20.6 1.5 %collective-permute-start.7 = (bf16[128,256]{1,0:T(8,128)(2,1)S(1)}, bf16[128,256]{1,0:T(8,128)(2,1)S(1)}, u32[]{:S(2)}, u32[]{:S(2)}) collective-permute-start(bf16[128,256]{1,0:T(8,128)(2,1)S(1)} %get-tuple-element.11.blocks), channel_id=1, source_target_pairs={{0,2},{2,0},{4,6},{6,4},{8,10},{10,8},{12,14},{14,12},{16,18},{18,... | collective-permute-start | bytes 196616 | tf_op jit(solution)/shard_map/ppermute | solution.py:199
  22.1 2.8 %collective-permute-done.7.got_blocks = bf16[128,256]{1,0:T(8,128)(2,1)S(1)} collective-permute-done((bf16[128,256]{1,0:T(8,128)(2,1)S(1)}, bf16[128,256]{1,0:T(8,128)(2,1)S(1)}, u32[]{:S(2)}, u32[]{:S(2)}) %collective-permute-start.7) | collective-permute-done | bytes 65568 | tf_op jit(solution)/shard_map/ppermute | solution.py:199
  24.9 1.9 %collective-permute-start.8 = (f32[320,128]{1,0:T(8,128)S(1)}, f32[320,128]{1,0:T(8,128)S(1)}, u32[]{:S(2)}, u32[]{:S(2)}) collective-permute-start(f32[320,128]{1,0:T(8,128)S(1)} %get-tuple-element.12), channel_id=1, source_target_pairs={{0,16},{1,5},{2,18},{3,7},{4,20},{5,1},{6,22},{7,3},{8,24},{9,13},... | collective-permute-start | bytes 491528 | tf_op jit(solution)/shard_map/ppermute | solution.py:204
  26.9 6.1 %collective-permute-done.8 = f32[320,128]{1,0:T(8,128)S(1)} collective-permute-done((f32[320,128]{1,0:T(8,128)S(1)}, f32[320,128]{1,0:T(8,128)S(1)}, u32[]{:S(2)}, u32[]{:S(2)}) %collective-permute-start.8) | collective-permute-done | bytes 163872 | tf_op jit(solution)/shard_map/ppermute | solution.py:204
  33.0 1.6 %collective-permute-start.9 = (f32[320,128]{1,0:T(8,128)S(1)}, f32[320,128]{1,0:T(8,128)S(1)}, u32[]{:S(2)}, u32[]{:S(2)}) collective-permute-start(f32[320,128]{1,0:T(8,128)S(1)} %add.3), channel_id=1, source_target_pairs={{0,2},{1,9},{2,0},{3,11},{4,6},{5,13},{6,4},{7,15},{8,10},{9,1},{1... | collective-permute-start | bytes 491528 | tf_op jit(solution)/shard_map/ppermute | solution.py:204
  34.6 3.8 %collective-permute-done.9 = f32[320,128]{1,0:T(8,128)S(1)} collective-permute-done((f32[320,128]{1,0:T(8,128)S(1)}, f32[320,128]{1,0:T(8,128)S(1)}, u32[]{:S(2)}, u32[]{:S(2)}) %collective-permute-start.9) | collective-permute-done | bytes 163872 | tf_op jit(solution)/shard_map/ppermute | solution.py:204
  38.5 0.5 collective-permute-start.11
  39.0 1.3 %collective-permute-done.11.refs_4_ = bf16[256,256]{1,0:T(8,128)(2,1)S(1)} collective-permute-done((bf16[256,256]{1,0:T(8,128)(2,1)S(1)}, bf16[256,256]{1,0:T(8,128)(2,1)S(1)}, u32[]{:S(2)}, u32[]{:S(2)}) %collective-permute-start.11) | collective-permute-done | bytes 131104 | tf_op jit(solution)/shard_map/ppermute | solution.py:199
  40.3 10.2 %shard_map.73 = (f32[256,256]{1,0:T(8,128)}, f32[16,256]{1,0:T(8,128)}) custom-call(s32[2]{0:T(128)S(1)} %pad_add_fusion.place.refs_0_, f32[640,128]{1,0:T(8,128)S(1)} %maximum_select_fusion.refs_1_, f32[640,128]{1,0:T(8,128)S(1)} %collective-permute-done.10.refs_2_, bf16[256,256]{1,0:T(8,128)(2,1)S(1)} %get-tuple-element.13.refs_3_, ...), custom_call_target="tpu_custom_call" | custom-call | tf_op jit(solution)/shard_map/pallas_call | solution.py:188
  (22 shorter events, 0.3 us)
Async XLA Ops:
  0.6 0.7 %copy-start.3 = (s32[256]{0:T(256)S(1)}, s32[256]{0:T(256)}, u32[]{:S(2)}) copy-start(s32[256]{0:T(256)} %param.7) | copy-start | bytes 3076
  0.6 0.7 %copy-start.1 = (f32[512]{0:T(512)S(1)}, f32[512]{0:T(512)}, u32[]{:S(2)}) copy-start(f32[512]{0:T(512)} %param.8) | copy-start | bytes 6148
  0.7 0.7 %copy-start.2 = (s32[256]{0:T(256)S(1)}, s32[256]{0:T(256)}, u32[]{:S(2)}) copy-start(s32[256]{0:T(256)} %param.6) | copy-start | bytes 3076
  1.3 0.9 %copy-start = (bf16[512,256]{1,0:T(8,128)(2,1)S(1)}, bf16[512,256]{1,0:T(8,128)(2,1)}, u32[]{:S(2)}) copy-start(bf16[512,256]{1,0:T(8,128)(2,1)} %dosage.1) | copy-start | bytes 786436
  2.3 0.7 %copy-start.4 = (bf16[16,256]{1,0:T(8,128)(2,1)S(1)}, bf16[16,256]{1,0:T(8,128)(2,1)}, u32[]{:S(2)}) copy-start(bf16[16,256]{1,0:T(8,128)(2,1)} %param.9) | copy-start | bytes 24580
  2.5 4.7 %collective-permute-start = (bf16[512,256]{1,0:T(8,128)(2,1)S(1)}, bf16[512,256]{1,0:T(8,128)(2,1)S(1)}, u32[]{:S(2)}, u32[]{:S(2)}) collective-permute-start(bf16[512,256]{1,0:T(8,128)(2,1)S(1)} %shard_map.68.own.refs_5_), channel_id=1, source_target_pairs={{0,1},{1,0},{2,3},{3,2},{4,5},{5,4},{6,7},{7,6},{8,9},{9,8},{10,11... | collective-permute-start | bytes 786440 | tf_op jit(solution)/shard_map/ppermute | solution.py:199
  3.0 6.6 %collective-permute-start.2 = (bf16[16,256]{1,0:T(8,128)(2,1)S(1)}, bf16[16,256]{1,0:T(8,128)(2,1)S(1)}, u32[]{:S(2)}, u32[]{:S(2)}) collective-permute-start(bf16[16,256]{1,0:T(8,128)(2,1)S(1)} %copy-done.4), channel_id=1, source_target_pairs={{0,16},{2,18},{4,20},{6,22},{8,24},{10,26},{12,28},{14,30},{16,0},... | collective-permute-start | bytes 24584 | tf_op jit(solution)/shard_map/ppermute | solution.py:199
  8.1 5.4 %collective-permute-start.1 = (f32[320,128]{1,0:T(8,128)S(1)}, f32[320,128]{1,0:T(8,128)S(1)}, u32[]{:S(2)}, u32[]{:S(2)}) collective-permute-start(f32[320,128]{1,0:T(8,128)S(1)} %get-tuple-element.14), channel_id=1, source_target_pairs={{0,2},{1,9},{2,0},{3,11},{4,6},{5,13},{6,4},{7,15},{8,10},{9,1},{1... | collective-permute-start | bytes 491528 | tf_op jit(solution)/shard_map/ppermute | solution.py:204
  9.6 3.7 %collective-permute-start.3 = (bf16[32,256]{1,0:T(8,128)(2,1)S(1)}, bf16[32,256]{1,0:T(8,128)(2,1)S(1)}, u32[]{:S(2)}, u32[]{:S(2)}) collective-permute-start(bf16[32,256]{1,0:T(8,128)(2,1)S(1)} %constant_dynamic-update-slice_fusion.blocks), channel_id=1, source_target_pairs={{0,8},{2,10},{4,12},{6,14},{8,0},{10,2},{12,4},{14,6},{16,24},{18,... | collective-permute-start | bytes 49160 | tf_op jit(solution)/shard_map/ppermute | solution.py:199
  13.5 5.6 %collective-permute-start.4 = (f32[320,128]{1,0:T(8,128)S(1)}, f32[320,128]{1,0:T(8,128)S(1)}, u32[]{:S(2)}, u32[]{:S(2)}) collective-permute-start(f32[320,128]{1,0:T(8,128)S(1)} %get-tuple-element.8.x), channel_id=1, source_target_pairs={{0,8},{1,3},{2,10},{3,1},{4,12},{5,7},{6,14},{7,5},{8,0},{9,11},{1... | collective-permute-start | bytes 491528 | tf_op jit(solution)/shard_map/ppermute | solution.py:204
  15.1 3.9 %collective-permute-start.5 = (bf16[64,256]{1,0:T(8,128)(2,1)S(1)}, bf16[64,256]{1,0:T(8,128)(2,1)S(1)}, u32[]{:S(2)}, u32[]{:S(2)}) collective-permute-start(bf16[64,256]{1,0:T(8,128)(2,1)S(1)} %get-tuple-element.9.blocks), channel_id=1, source_target_pairs={{0,4},{2,6},{4,0},{6,2},{8,12},{10,14},{12,8},{14,10},{16,20},{18,... | collective-permute-start | bytes 98312 | tf_op jit(solution)/shard_map/ppermute | solution.py:199
  19.1 5.9 %collective-permute-start.6 = (f32[320,128]{1,0:T(8,128)S(1)}, f32[320,128]{1,0:T(8,128)S(1)}, u32[]{:S(2)}, u32[]{:S(2)}) collective-permute-start(f32[320,128]{1,0:T(8,128)S(1)} %get-tuple-element.10.x), channel_id=1, source_target_pairs={{0,4},{1,17},{2,6},{3,19},{4,0},{5,21},{6,2},{7,23},{8,12},{9,25},... | collective-permute-start | bytes 491528 | tf_op jit(solution)/shard_map/ppermute | solution.py:204
  20.6 4.3 %collective-permute-start.7 = (bf16[128,256]{1,0:T(8,128)(2,1)S(1)}, bf16[128,256]{1,0:T(8,128)(2,1)S(1)}, u32[]{:S(2)}, u32[]{:S(2)}) collective-permute-start(bf16[128,256]{1,0:T(8,128)(2,1)S(1)} %get-tuple-element.11.blocks), channel_id=1, source_target_pairs={{0,2},{2,0},{4,6},{6,4},{8,10},{10,8},{12,14},{14,12},{16,18},{18,... | collective-permute-start | bytes 196616 | tf_op jit(solution)/shard_map/ppermute | solution.py:199
  24.9 8.0 %collective-permute-start.8 = (f32[320,128]{1,0:T(8,128)S(1)}, f32[320,128]{1,0:T(8,128)S(1)}, u32[]{:S(2)}, u32[]{:S(2)}) collective-permute-start(f32[320,128]{1,0:T(8,128)S(1)} %get-tuple-element.12), channel_id=1, source_target_pairs={{0,16},{1,5},{2,18},{3,7},{4,20},{5,1},{6,22},{7,3},{8,24},{9,13},... | collective-permute-start | bytes 491528 | tf_op jit(solution)/shard_map/ppermute | solution.py:204
  33.0 5.4 %collective-permute-start.9 = (f32[320,128]{1,0:T(8,128)S(1)}, f32[320,128]{1,0:T(8,128)S(1)}, u32[]{:S(2)}, u32[]{:S(2)}) collective-permute-start(f32[320,128]{1,0:T(8,128)S(1)} %add.3), channel_id=1, source_target_pairs={{0,2},{1,9},{2,0},{3,11},{4,6},{5,13},{6,4},{7,15},{8,10},{9,1},{1... | collective-permute-start | bytes 491528 | tf_op jit(solution)/shard_map/ppermute | solution.py:204
  38.4 1.9 %collective-permute-start.10 = (f32[640,128]{1,0:T(8,128)S(1)}, f32[640,128]{1,0:T(8,128)S(1)}, u32[]{:S(2)}, u32[]{:S(2)}) collective-permute-start(f32[640,128]{1,0:T(8,128)S(1)} %maximum_select_fusion.refs_1_), channel_id=1, source_target_pairs={{0,1},{1,0},{2,3},{3,2},{4,5},{5,4},{6,7},{7,6},{8,9},{9,8},{10,11... | collective-permute-start | bytes 983048 | tf_op jit(solution)/shard_map/ppermute | solution.py:199
  38.5 1.8 %collective-permute-start.11 = (bf16[256,256]{1,0:T(8,128)(2,1)S(1)}, bf16[256,256]{1,0:T(8,128)(2,1)S(1)}, u32[]{:S(2)}, u32[]{:S(2)}) collective-permute-start(bf16[256,256]{1,0:T(8,128)(2,1)S(1)} %get-tuple-element.13.refs_3_), channel_id=1, source_target_pairs={{0,1},{1,0},{2,3},{3,2},{4,5},{5,4},{6,7},{7,6},{8,9},{9,8},{10,11... | collective-permute-start | bytes 393224 | tf_op jit(solution)/shard_map/ppermute | solution.py:199

commit v4 on v3

--- a/solution.py
+++ b/solution.py
@@ -49,8 +49,8 @@
             out[r : r + HALF, c : c + HALF] = (column * (x - 2.0 * f) * scale[:, c : c + HALF]).astype(BF16)
 
 
-def moment_kernel(place, own, other, out):
-    core = place[1]
+def moment_kernel(own, other, out):
+    core = lax.axis_index("mark")
     low, high = own[:, :HALF], own[:, HALF:]
     first = other[:, pl.ds(pl.multiple_of(core * HALF, HALF), HALF)]
     second = other[:, pl.ds(pl.multiple_of((1 - core) * HALF, HALF), HALF)]
@@ -58,26 +58,29 @@
         out[i * HALF : (i + 1) * HALF, :] = dot(a, b, 0, 0, lax.Precision.DEFAULT)
 
 
-def eliminate(groups, slots):
+def eliminate(groups, slots, factor_slots):
     shape = groups[0].shape
     lane = lax.broadcasted_iota(jnp.int32, shape, 1)
     sub = lax.broadcasted_iota(jnp.int32, shape, 0)
     spread = lambda x: jnp.broadcast_to(x, shape)
+    columns = lambda x, j: [jnp.take_along_axis(x, jnp.full(shape, j + k, jnp.int32), axis=1) for k in range(8)]
     groups, result = list(groups), []
+    pivots = columns(groups[0], 0)
     for g in range(len(groups)):
-        j = 8 * g
-        columns = lambda group: [
-            jnp.take_along_axis(group, jnp.full(shape, j + k, jnp.int32), axis=1) for k in range(8)
-        ]
-        slot = 9 * (g % 4)
+        j, last = 8 * g, g + 1 == len(groups)
+        slot, factor_slot = 9 * (g % 4), 8 * (g % 4)
         slots[slot + 8] = groups[g]
         rows = [spread(slots[slot + 8, k : k + 1, :]) for k in range(8)]
-        for k, c in enumerate(columns(groups[g])):
-            slots[slot + k] = c
+        for k in range(8):
+            slots[slot + k] = pivots[k]
         a = {(i, k): spread(slots[slot + k, i : i + 1, :]) for k in range(8) for i in range(k, 8)}
         inside = (lane >= j) & (lane < j + 8)
-        root, done, low = [], [], {}
+        root, done, low, factors = [], [], {}, []
         block = jnp.zeros(shape, F32)
+        if not last:
+            left = columns(groups[g + 1], j)
+            pivots = columns(groups[g + 1], j + 8)
+            ahead = jnp.where(inside, 0.0, groups[g + 1])
         for k in range(8):
             q = lax.rsqrt(a[k, k])
             root.append(q)
@@ -91,18 +94,19 @@
                 row = row - low[k, m] * done[m]
             done.append(row * q)
             block = jnp.where((sub == k) & (lane <= j + k), done[k], block)
+            if not last:
+                c = left[k]
+                for m in range(k):
+                    c = c - factors[m] * low[k, m]
+                factors.append(c * q)
+                factor_slots[factor_slot + k] = factors[k]
+                for i in range(8):
+                    pivots[i] = pivots[i] - factors[k] * spread(factor_slots[factor_slot + k, i : i + 1, :])
+                ahead = ahead - factors[k] * done[k]
         result.append(block)
-        if g + 1 == len(groups):
+        if last:
             break
-        factors = []
-        for k, c in enumerate(columns(groups[g + 1])):
-            for m in range(k):
-                c = c - factors[m] * low[k, m]
-            factors.append(c * root[k])
-        x = jnp.where(inside, 0.0, groups[g + 1])
-        for k in range(8):
-            x = x - factors[k] * done[k]
-        groups[g + 1] = x
+        groups[g + 1] = ahead
         update = [None] * 8
         for k in reversed(range(8)):
             x = done[k]
@@ -111,21 +115,22 @@
             update[k] = x * root[k]
         for n in range(g + 2, len(groups)):
             x = jnp.where(inside, 0.0, groups[n])
-            for k, c in enumerate(columns(groups[n])):
+            for k, c in enumerate(columns(groups[n], j)):
                 x = x - c * update[k]
             groups[n] = x
     return result
 
 
-def inverse_factor(gram, out, slots):
+def inverse_factor(gram, out, ready, *slots):
     n = gram.shape[0]
     rest, corner = gram, gram[:BLOCK, :BLOCK]
     for at in range(0, n, BLOCK):
         end = at + BLOCK
         row = rest[:BLOCK]
-        inv = jnp.concatenate(eliminate([corner[i : i + 8, :] for i in range(0, BLOCK, 8)], slots), 0)
+        inv = jnp.concatenate(eliminate([corner[i : i + 8, :] for i in range(0, BLOCK, 8)], *slots), 0)
         if end == n:
             out[at:end, :] = jnp.concatenate([dot(inv, row[:, :at], 1, 0), inv], 1) if at else inv
+            ready(at, end)
             break
         ahead = dot(inv, row[:, end : end + BLOCK], 1, 0)
         corner = rest[BLOCK : 2 * BLOCK, end : end + BLOCK] - dot(ahead, ahead, 0, 0)
@@ -133,15 +138,16 @@
         joined = jnp.concatenate(([full[:, :at]] if at else []) + [inv, full[:, end:]], 1)
         lane = lax.broadcasted_iota(jnp.int32, (BLOCK, n), 1)
         out[at:end, :] = jnp.where(lane < end, joined, 0.0)
+        ready(at, end)
         below = rest[BLOCK:]
         lane = lax.broadcasted_iota(jnp.int32, below.shape, 1)
         rest = jnp.where((lane >= at) & (lane < end), 0.0, below) - dot(joined[:, end:], joined, 0, 0)
 
 
 def final_kernel(
-    total, place, blocks, others, test, test_other, standard, standard_other, basis, loadings, moments, inverse, product, gathered, slots
+    total, blocks, others, test, test_other, standard, standard_other, basis, loadings, moments, inverse, product, gathered, *slots
 ):
-    samp, core = place[0], place[1]
+    samp, core = lax.axis_index("samp"), lax.axis_index("mark")
     side = 2 * HALF
     block = lambda ref, i: ref[i * HALF : (i + 1) * HALF, :]
     for ref, at in ((blocks, 0), (others, side)):
@@ -168,27 +174,31 @@
     tests = gathered[...]
     product[...] = dot_pieces(pieces(moments[...]), tests, 1, 0)
     gram = dot_pieces_right(tests, pieces(product[...]), 0, 0)
-    inverse_factor(gram, inverse, slots)
     share = basis.shape[0]
     rows = pl.ds(pl.multiple_of(core * share, share), share)
     sketch = dot(standard[rows, :], tests[:side], 1, 0, lax.Precision.DEFAULT) + dot(
         standard_other[rows, :], tests[side:], 1, 0, lax.Precision.DEFAULT
     )
-    basis[...] = math.sqrt(total) * dot(sketch, inverse[...], 1, 1)
+    sketch_high, sketch_mid, _ = pieces(math.sqrt(total) * sketch)
+    few = loadings.shape[0]
     own = product[pl.ds(pl.multiple_of(samp * few, few), few), :]
-    loadings[...] = dot(own, inverse[...], 1, 1)
-
-
-def call(kernel, shapes, inputs, place=None, scratch=()):
+
+    def ready(at, end):
+        high, mid, _ = pieces(inverse[at:end, :end])
+        once = lambda a, b: dot(a[:, :end], b, 1, 1, lax.Precision.DEFAULT)
+        basis[:, at:end] = once(sketch_high, high) + (once(sketch_high, mid) + once(sketch_mid, high))
+        loadings[:, at:end] = dot(own[:, :end], inverse[at:end, :end], 1, 1)
+
+    inverse_factor(gram, inverse, ready, *slots)
+
+
+def call(kernel, shapes, inputs, scratch=()):
     vmem = pl.BlockSpec(memory_space=VMEM)
-    specs = [vmem] * len(inputs)
-    if place is not None:
-        specs, inputs = [pl.BlockSpec(memory_space=pltpu.SMEM)] + specs, [place] + list(inputs)
     many = isinstance(shapes, (list, tuple))
     return pl.pallas_call(
         kernel,
         out_shape=shapes,
-        in_specs=specs,
+        in_specs=[vmem] * len(inputs),
         out_specs=[vmem] * len(shapes) if many else vmem,
         scratch_shapes=list(scratch),
         compiler_params=pltpu.CompilerParams(vmem_limit_bytes=24 * 2**20),
@@ -225,9 +235,7 @@
 
 def sum_plan(count):
     bits = [1 << i for i in range((count - 1).bit_length())]
-    if len(bits) < 3:
-        return list(zip(bits, bits[::-1]))
-    return list(zip(bits[:1] + bits[2:3] + bits[1:2] + bits[3:], bits[2:3] + bits[:1] + bits[3:] + bits[1:2]))
+    return list(zip(bits[:1] + bits[2:3] + bits[1:2] + bits[3:], bits))
 
 
 def gather_plan(count):
@@ -261,14 +269,15 @@
             kept = kept + got
         sent = kept
     test_other = swap(test, "mark", 1)
-    return in_order(kept, swap_by_core(kept, sums[0]), up), test, test_other
+    got = swap_by_core(kept, sums[0])
+    kept_other = swap(kept, "mark", 1)
+    return in_order(kept, got, up), in_order(kept_other, swap(got, "mark", 1), up), test, test_other
 
 
 def two_marks(dosage, alt_count, obs_count, sample_weight, test_matrix):
     rows, cols = dosage.shape
     few, rank = test_matrix.shape
     samples = rows * lax.axis_size("samp")
-    place = jnp.stack([lax.axis_index("samp"), lax.axis_index("mark")]).astype(jnp.int32)
     standard = call(
         standard_kernel,
         jax.ShapeDtypeStruct((rows, cols), BF16),
@@ -276,21 +285,14 @@
     )
     standard_other = swap(standard, "mark", 1)
     got_test = swap(test_matrix, "samp", gather_plan(lax.axis_size("samp"))[0])
-    blocks = call(
-        moment_kernel,
-        jax.ShapeDtypeStruct((5 * HALF, HALF), F32),
-        [standard, standard_other],
-        place,
-    )
-    blocks, test, test_other = sum_and_gather(blocks, test_matrix, got_test)
-    others = swap(blocks, "mark", 1)
+    blocks = call(moment_kernel, jax.ShapeDtypeStruct((5 * HALF, HALF), F32), [standard, standard_other])
+    blocks, others, test, test_other = sum_and_gather(blocks, test_matrix, got_test)
     kernel = lambda *refs: final_kernel(samples, *refs)
     basis, loadings = call(
         kernel,
         [jax.ShapeDtypeStruct((rows // 2, rank), F32), jax.ShapeDtypeStruct((few, rank), F32)],
         [blocks, others, test, test_other, standard, standard_other],
-        place,
-        [VMEM((2 * cols, 2 * cols), F32), VMEM((rank, rank), F32), VMEM((2 * cols, rank), F32), VMEM((2 * cols, rank), BF16), VMEM((36, 8, BLOCK), F32)],
+        [VMEM((2 * cols, 2 * cols), F32), VMEM((rank, rank), F32), VMEM((2 * cols, rank), F32), VMEM((2 * cols, rank), BF16), VMEM((36, 8, BLOCK), F32), VMEM((32, 8, BLOCK), F32)],
     )
     return basis, loadings
 

time: 50.7 us -> 49.2 us (0.970)
  Pallas kernels: 11.3 us -> 9.66 us
    pallas_call x6, Pallas kernels: 11.3 us -> 9.66 us  [call(): pl.pallas_call(kernel, out_shape=shapes, in_specs=[vmem] * len(inputs), o...]
    ppermute x7 -> x8, waiting for transfers between devices: 8.65 us -> 8.34 us  [swap(): lax.ppermute(x, axis, [(i, i ^ bit) for i in range(lax.axis_size(axis))])]
    ppermute x7 -> x8, starting transfers between devices: 9.71 us -> 9.65 us  [swap(): lax.ppermute(x, axis, [(i, i ^ bit) for i in range(lax.axis_size(axis))])]
  transfers between devices with their start and end apart: 12 -> 13, of which waited for: 7 -> 8; matrix products, arithmetic and copies ran while one was open for 0% -> 0% of each run, Pallas kernels for 2% -> 1%
where the time goes in v4:
time: 49.2 us; the launch traced here: 49 us
  waiting for transfers between devices  18.8 us (38%)
  starting transfers between devices  18 us (37%)
  Pallas kernels  9.66 us (20%)
  local copies, waits for them, and re-layouts  1.66 us (3%)
  between operations  0.73 us (1%)
    ppermute x5, waiting for transfers between devices, swap_by_core(): return lax.ppermute(x, ('samp', 'mark'), pairs)  10.5 us
    pallas_call x6, Pallas kernels, call(): pl.pallas_call(kernel, out_shape=shapes, in_specs=[vmem] * len(inputs), o...  9.66 us
    ppermute x8, starting transfers between devices, swap(): lax.ppermute(x, axis, [(i, i ^ bit) for i in range(lax.axis_size(axis))])  9.65 us
    ppermute x5, starting transfers between devices, swap_by_core(): return lax.ppermute(x, ('samp', 'mark'), pairs)  8.36 us
    ppermute x8, waiting for transfers between devices, swap(): lax.ppermute(x, axis, [(i, i ^ bit) for i in range(lax.axis_size(axis))])  8.34 us
    unnamed x11, local copies, waits for them, and re-layouts  1.66 us
  transfers between devices with their start and end apart: 13, of which 8 were waited for; matrix products, arithmetic and copies ran while one was open for 0% of the time, Pallas kernels for 1%

profile of v4, /device:TPU:0, one launch (start us, length us, event | category | flops | bytes accessed | tf_op | source)
XLA Modules:
  0.0 49.0 jit_solution(10166820127699770118)
XLA Ops:
  0.7 0.7 %copy-done.3 = s32[256]{0:T(256)S(1)} copy-done((s32[256]{0:T(256)S(1)}, s32[256]{0:T(256)}, u32[]{:S(2)}) %copy-start.3) | copy-done | bytes 1048
  1.3 0.9 %copy-done = bf16[512,256]{1,0:T(8,128)(2,1)S(1)} copy-done((bf16[512,256]{1,0:T(8,128)(2,1)S(1)}, bf16[512,256]{1,0:T(8,128)(2,1)}, u32[]{:S(2)}) %copy-start) | copy-done | bytes 262168
  2.3 0.1 shard_map.68.own.refs_4_
  2.5 0.5 %collective-permute-start = (bf16[512,256]{1,0:T(8,128)(2,1)S(1)}, bf16[512,256]{1,0:T(8,128)(2,1)S(1)}, u32[]{:S(2)}, u32[]{:S(2)}) collective-permute-start(bf16[512,256]{1,0:T(8,128)(2,1)S(1)} %shard_map.68.own.refs_4_), channel_id=1, source_target_pairs={{0,1},{1,0},{2,3},{3,2},{4,5},{5,4},{6,7},{7,6},{8,9},{9,8},{10,11... | collective-permute-start | bytes 786440 | tf_op jit(solution)/shard_map/ppermute | solution.py:209
  3.0 4.0 %collective-permute-start.2 = (bf16[16,256]{1,0:T(8,128)(2,1)S(1)}, bf16[16,256]{1,0:T(8,128)(2,1)S(1)}, u32[]{:S(2)}, u32[]{:S(2)}) collective-permute-start(bf16[16,256]{1,0:T(8,128)(2,1)S(1)} %copy-done.4), channel_id=1, source_target_pairs={{0,16},{2,18},{4,20},{6,22},{8,24},{10,26},{12,28},{14,30},{16,0},... | collective-permute-start | bytes 24584 | tf_op jit(solution)/shard_map/ppermute | solution.py:209
  7.0 0.4 shard_map.69
  7.4 1.6 %collective-permute-start.1 = (f32[320,128]{1,0:T(8,128)S(1)}, f32[320,128]{1,0:T(8,128)S(1)}, u32[]{:S(2)}, u32[]{:S(2)}) collective-permute-start(f32[320,128]{1,0:T(8,128)S(1)} %get-tuple-element.14), channel_id=1, source_target_pairs={{0,2},{1,3},{2,0},{3,1},{4,6},{5,7},{6,4},{7,5},{8,10},{9,11},{10,... | collective-permute-start | bytes 491528 | tf_op jit(solution)/shard_map/ppermute | solution.py:214
  9.0 1.6 %collective-permute-start.3 = (bf16[32,256]{1,0:T(8,128)(2,1)S(1)}, bf16[32,256]{1,0:T(8,128)(2,1)S(1)}, u32[]{:S(2)}, u32[]{:S(2)}) collective-permute-start(bf16[32,256]{1,0:T(8,128)(2,1)S(1)} %constant_dynamic-update-slice_fusion.blocks), channel_id=1, source_target_pairs={{0,8},{2,10},{4,12},{6,14},{8,0},{10,2},{12,4},{14,6},{16,24},{18,... | collective-permute-start | bytes 49160 | tf_op jit(solution)/shard_map/ppermute | solution.py:209
  10.6 2.2 %collective-permute-done.3.got_blocks = bf16[32,256]{1,0:T(8,128)(2,1)S(1)} collective-permute-done((bf16[32,256]{1,0:T(8,128)(2,1)S(1)}, bf16[32,256]{1,0:T(8,128)(2,1)S(1)}, u32[]{:S(2)}, u32[]{:S(2)}) %collective-permute-start.3) | collective-permute-done | bytes 16416 | tf_op jit(solution)/shard_map/ppermute | solution.py:209
  12.7 0.6 %collective-permute-done.1.got = f32[320,128]{1,0:T(8,128)S(1)} collective-permute-done((f32[320,128]{1,0:T(8,128)S(1)}, f32[320,128]{1,0:T(8,128)S(1)}, u32[]{:S(2)}, u32[]{:S(2)}) %collective-permute-start.1) | collective-permute-done | bytes 163872 | tf_op jit(solution)/shard_map/ppermute | solution.py:214
  13.4 1.6 %collective-permute-start.4 = (f32[320,128]{1,0:T(8,128)S(1)}, f32[320,128]{1,0:T(8,128)S(1)}, u32[]{:S(2)}, u32[]{:S(2)}) collective-permute-start(f32[320,128]{1,0:T(8,128)S(1)} %get-tuple-element.8.x), channel_id=1, source_target_pairs={{0,8},{1,5},{2,10},{3,7},{4,12},{5,1},{6,14},{7,3},{8,0},{9,13},{1... | collective-permute-start | bytes 491528 | tf_op jit(solution)/shard_map/ppermute | solution.py:214
  15.0 1.5 %collective-permute-start.5 = (bf16[64,256]{1,0:T(8,128)(2,1)S(1)}, bf16[64,256]{1,0:T(8,128)(2,1)S(1)}, u32[]{:S(2)}, u32[]{:S(2)}) collective-permute-start(bf16[64,256]{1,0:T(8,128)(2,1)S(1)} %get-tuple-element.9.blocks), channel_id=1, source_target_pairs={{0,4},{2,6},{4,0},{6,2},{8,12},{10,14},{12,8},{14,10},{16,20},{18,... | collective-permute-start | bytes 98312 | tf_op jit(solution)/shard_map/ppermute | solution.py:209
  16.6 2.4 %collective-permute-done.5.got_blocks = bf16[64,256]{1,0:T(8,128)(2,1)S(1)} collective-permute-done((bf16[64,256]{1,0:T(8,128)(2,1)S(1)}, bf16[64,256]{1,0:T(8,128)(2,1)S(1)}, u32[]{:S(2)}, u32[]{:S(2)}) %collective-permute-start.5) | collective-permute-done | bytes 32800 | tf_op jit(solution)/shard_map/ppermute | solution.py:209
  19.0 1.6 %collective-permute-start.6 = (f32[320,128]{1,0:T(8,128)S(1)}, f32[320,128]{1,0:T(8,128)S(1)}, u32[]{:S(2)}, u32[]{:S(2)}) collective-permute-start(f32[320,128]{1,0:T(8,128)S(1)} %get-tuple-element.10.x), channel_id=1, source_target_pairs={{0,4},{1,9},{2,6},{3,11},{4,0},{5,13},{6,2},{7,15},{8,12},{9,1},{1... | collective-permute-start | bytes 491528 | tf_op jit(solution)/shard_map/ppermute | solution.py:214
  20.6 1.5 %collective-permute-start.7 = (bf16[128,256]{1,0:T(8,128)(2,1)S(1)}, bf16[128,256]{1,0:T(8,128)(2,1)S(1)}, u32[]{:S(2)}, u32[]{:S(2)}) collective-permute-start(bf16[128,256]{1,0:T(8,128)(2,1)S(1)} %get-tuple-element.11.blocks), channel_id=1, source_target_pairs={{0,2},{2,0},{4,6},{6,4},{8,10},{10,8},{12,14},{14,12},{16,18},{18,... | collective-permute-start | bytes 196616 | tf_op jit(solution)/shard_map/ppermute | solution.py:209
  22.1 2.8 %collective-permute-done.7.got_blocks = bf16[128,256]{1,0:T(8,128)(2,1)S(1)} collective-permute-done((bf16[128,256]{1,0:T(8,128)(2,1)S(1)}, bf16[128,256]{1,0:T(8,128)(2,1)S(1)}, u32[]{:S(2)}, u32[]{:S(2)}) %collective-permute-start.7) | collective-permute-done | bytes 65568 | tf_op jit(solution)/shard_map/ppermute | solution.py:209
  24.9 2.0 %collective-permute-start.8 = (f32[320,128]{1,0:T(8,128)S(1)}, f32[320,128]{1,0:T(8,128)S(1)}, u32[]{:S(2)}, u32[]{:S(2)}) collective-permute-start(f32[320,128]{1,0:T(8,128)S(1)} %get-tuple-element.12), channel_id=1, source_target_pairs={{0,16},{1,17},{2,18},{3,19},{4,20},{5,21},{6,22},{7,23},{8,24},{9,... | collective-permute-start | bytes 491528 | tf_op jit(solution)/shard_map/ppermute | solution.py:214
  26.9 6.0 %collective-permute-done.8 = f32[320,128]{1,0:T(8,128)S(1)} collective-permute-done((f32[320,128]{1,0:T(8,128)S(1)}, f32[320,128]{1,0:T(8,128)S(1)}, u32[]{:S(2)}, u32[]{:S(2)}) %collective-permute-start.8) | collective-permute-done | bytes 163872 | tf_op jit(solution)/shard_map/ppermute | solution.py:214
  32.9 1.6 %collective-permute-start.9 = (f32[320,128]{1,0:T(8,128)S(1)}, f32[320,128]{1,0:T(8,128)S(1)}, u32[]{:S(2)}, u32[]{:S(2)}) collective-permute-start(f32[320,128]{1,0:T(8,128)S(1)} %add.3), channel_id=1, source_target_pairs={{0,2},{1,3},{2,0},{3,1},{4,6},{5,7},{6,4},{7,5},{8,10},{9,11},{10,... | collective-permute-start | bytes 491528 | tf_op jit(solution)/shard_map/ppermute | solution.py:214
  34.5 3.8 %collective-permute-done.9 = f32[320,128]{1,0:T(8,128)S(1)} collective-permute-done((f32[320,128]{1,0:T(8,128)S(1)}, f32[320,128]{1,0:T(8,128)S(1)}, u32[]{:S(2)}, u32[]{:S(2)}) %collective-permute-start.9) | collective-permute-done | bytes 163872 | tf_op jit(solution)/shard_map/ppermute | solution.py:214
  38.3 0.5 %collective-permute-start.12 = (bf16[256,256]{1,0:T(8,128)(2,1)S(1)}, bf16[256,256]{1,0:T(8,128)(2,1)S(1)}, u32[]{:S(2)}, u32[]{:S(2)}) collective-permute-start(bf16[256,256]{1,0:T(8,128)(2,1)S(1)} %get-tuple-element.13.refs_2_), channel_id=1, source_target_pairs={{0,1},{1,0},{2,3},{3,2},{4,5},{5,4},{6,7},{7,6},{8,9},{9,8},{10,11... | collective-permute-start | bytes 393224 | tf_op jit(solution)/shard_map/ppermute | solution.py:209
  38.9 0.8 %collective-permute-done.10 = f32[320,128]{1,0:T(8,128)S(1)} collective-permute-done((f32[320,128]{1,0:T(8,128)S(1)}, f32[320,128]{1,0:T(8,128)S(1)}, u32[]{:S(2)}, u32[]{:S(2)}) %collective-permute-start.10) | collective-permute-done | bytes 163872 | tf_op jit(solution)/shard_map/ppermute | solution.py:209
  39.7 0.2 collective-permute-done.12.refs_3_
  39.9 9.1 %shard_map.73 = (f32[256,256]{1,0:T(8,128)}, f32[16,256]{1,0:T(8,128)}) custom-call(f32[640,128]{1,0:T(8,128)S(1)} %maximum_select_fusion.refs_0_, f32[640,128]{1,0:T(8,128)S(1)} %maximum_select_fusion.1.refs_1_, bf16[256,256]{1,0:T(8,128)(2,1)S(1)} %get-tuple-element.13.refs_2_, bf16[256,256]{1,0:T(8,128)(2,1)S(1)} %collective-permute-done.12.refs_3_, ...), custom_call_target="tpu_custom_call" | custom-call | tf_op jit(solution)/shard_map/pallas_call | solution.py:198
  (24 shorter events, 0.2 us)
Async XLA Ops:
  0.6 0.7 %copy-start.3 = (s32[256]{0:T(256)S(1)}, s32[256]{0:T(256)}, u32[]{:S(2)}) copy-start(s32[256]{0:T(256)} %param.7) | copy-start | bytes 3076
  0.6 0.7 %copy-start.1 = (f32[512]{0:T(512)S(1)}, f32[512]{0:T(512)}, u32[]{:S(2)}) copy-start(f32[512]{0:T(512)} %param.8) | copy-start | bytes 6148
  0.7 0.7 %copy-start.2 = (s32[256]{0:T(256)S(1)}, s32[256]{0:T(256)}, u32[]{:S(2)}) copy-start(s32[256]{0:T(256)} %param.6) | copy-start | bytes 3076
  1.3 0.9 %copy-start = (bf16[512,256]{1,0:T(8,128)(2,1)S(1)}, bf16[512,256]{1,0:T(8,128)(2,1)}, u32[]{:S(2)}) copy-start(bf16[512,256]{1,0:T(8,128)(2,1)} %dosage.1) | copy-start | bytes 786436
  2.3 0.7 %copy-start.4 = (bf16[16,256]{1,0:T(8,128)(2,1)S(1)}, bf16[16,256]{1,0:T(8,128)(2,1)}, u32[]{:S(2)}) copy-start(bf16[16,256]{1,0:T(8,128)(2,1)} %param.9) | copy-start | bytes 24580
  2.5 4.6 %collective-permute-start = (bf16[512,256]{1,0:T(8,128)(2,1)S(1)}, bf16[512,256]{1,0:T(8,128)(2,1)S(1)}, u32[]{:S(2)}, u32[]{:S(2)}) collective-permute-start(bf16[512,256]{1,0:T(8,128)(2,1)S(1)} %shard_map.68.own.refs_4_), channel_id=1, source_target_pairs={{0,1},{1,0},{2,3},{3,2},{4,5},{5,4},{6,7},{7,6},{8,9},{9,8},{10,11... | collective-permute-start | bytes 786440 | tf_op jit(solution)/shard_map/ppermute | solution.py:209
  3.0 6.0 %collective-permute-start.2 = (bf16[16,256]{1,0:T(8,128)(2,1)S(1)}, bf16[16,256]{1,0:T(8,128)(2,1)S(1)}, u32[]{:S(2)}, u32[]{:S(2)}) collective-permute-start(bf16[16,256]{1,0:T(8,128)(2,1)S(1)} %copy-done.4), channel_id=1, source_target_pairs={{0,16},{2,18},{4,20},{6,22},{8,24},{10,26},{12,28},{14,30},{16,0},... | collective-permute-start | bytes 24584 | tf_op jit(solution)/shard_map/ppermute | solution.py:209
  7.4 5.9 %collective-permute-start.1 = (f32[320,128]{1,0:T(8,128)S(1)}, f32[320,128]{1,0:T(8,128)S(1)}, u32[]{:S(2)}, u32[]{:S(2)}) collective-permute-start(f32[320,128]{1,0:T(8,128)S(1)} %get-tuple-element.14), channel_id=1, source_target_pairs={{0,2},{1,3},{2,0},{3,1},{4,6},{5,7},{6,4},{7,5},{8,10},{9,11},{10,... | collective-permute-start | bytes 491528 | tf_op jit(solution)/shard_map/ppermute | solution.py:214
  9.0 3.7 %collective-permute-start.3 = (bf16[32,256]{1,0:T(8,128)(2,1)S(1)}, bf16[32,256]{1,0:T(8,128)(2,1)S(1)}, u32[]{:S(2)}, u32[]{:S(2)}) collective-permute-start(bf16[32,256]{1,0:T(8,128)(2,1)S(1)} %constant_dynamic-update-slice_fusion.blocks), channel_id=1, source_target_pairs={{0,8},{2,10},{4,12},{6,14},{8,0},{10,2},{12,4},{14,6},{16,24},{18,... | collective-permute-start | bytes 49160 | tf_op jit(solution)/shard_map/ppermute | solution.py:209
  13.4 5.6 %collective-permute-start.4 = (f32[320,128]{1,0:T(8,128)S(1)}, f32[320,128]{1,0:T(8,128)S(1)}, u32[]{:S(2)}, u32[]{:S(2)}) collective-permute-start(f32[320,128]{1,0:T(8,128)S(1)} %get-tuple-element.8.x), channel_id=1, source_target_pairs={{0,8},{1,5},{2,10},{3,7},{4,12},{5,1},{6,14},{7,3},{8,0},{9,13},{1... | collective-permute-start | bytes 491528 | tf_op jit(solution)/shard_map/ppermute | solution.py:214
  15.0 3.9 %collective-permute-start.5 = (bf16[64,256]{1,0:T(8,128)(2,1)S(1)}, bf16[64,256]{1,0:T(8,128)(2,1)S(1)}, u32[]{:S(2)}, u32[]{:S(2)}) collective-permute-start(bf16[64,256]{1,0:T(8,128)(2,1)S(1)} %get-tuple-element.9.blocks), channel_id=1, source_target_pairs={{0,4},{2,6},{4,0},{6,2},{8,12},{10,14},{12,8},{14,10},{16,20},{18,... | collective-permute-start | bytes 98312 | tf_op jit(solution)/shard_map/ppermute | solution.py:209
  19.0 5.9 %collective-permute-start.6 = (f32[320,128]{1,0:T(8,128)S(1)}, f32[320,128]{1,0:T(8,128)S(1)}, u32[]{:S(2)}, u32[]{:S(2)}) collective-permute-start(f32[320,128]{1,0:T(8,128)S(1)} %get-tuple-element.10.x), channel_id=1, source_target_pairs={{0,4},{1,9},{2,6},{3,11},{4,0},{5,13},{6,2},{7,15},{8,12},{9,1},{1... | collective-permute-start | bytes 491528 | tf_op jit(solution)/shard_map/ppermute | solution.py:214
  20.6 4.3 %collective-permute-start.7 = (bf16[128,256]{1,0:T(8,128)(2,1)S(1)}, bf16[128,256]{1,0:T(8,128)(2,1)S(1)}, u32[]{:S(2)}, u32[]{:S(2)}) collective-permute-start(bf16[128,256]{1,0:T(8,128)(2,1)S(1)} %get-tuple-element.11.blocks), channel_id=1, source_target_pairs={{0,2},{2,0},{4,6},{6,4},{8,10},{10,8},{12,14},{14,12},{16,18},{18,... | collective-permute-start | bytes 196616 | tf_op jit(solution)/shard_map/ppermute | solution.py:209
  24.9 8.0 %collective-permute-start.8 = (f32[320,128]{1,0:T(8,128)S(1)}, f32[320,128]{1,0:T(8,128)S(1)}, u32[]{:S(2)}, u32[]{:S(2)}) collective-permute-start(f32[320,128]{1,0:T(8,128)S(1)} %get-tuple-element.12), channel_id=1, source_target_pairs={{0,16},{1,17},{2,18},{3,19},{4,20},{5,21},{6,22},{7,23},{8,24},{9,... | collective-permute-start | bytes 491528 | tf_op jit(solution)/shard_map/ppermute | solution.py:214
  32.9 5.4 %collective-permute-start.9 = (f32[320,128]{1,0:T(8,128)S(1)}, f32[320,128]{1,0:T(8,128)S(1)}, u32[]{:S(2)}, u32[]{:S(2)}) collective-permute-start(f32[320,128]{1,0:T(8,128)S(1)} %add.3), channel_id=1, source_target_pairs={{0,2},{1,3},{2,0},{3,1},{4,6},{5,7},{6,4},{7,5},{8,10},{9,11},{10,... | collective-permute-start | bytes 491528 | tf_op jit(solution)/shard_map/ppermute | solution.py:214
  34.5 4.4 %collective-permute-start.11 = (f32[320,128]{1,0:T(8,128)S(1)}, f32[320,128]{1,0:T(8,128)S(1)}, u32[]{:S(2)}, u32[]{:S(2)}) collective-permute-start(f32[320,128]{1,0:T(8,128)S(1)} %add.3), channel_id=1, source_target_pairs={{0,1},{1,0},{2,3},{3,2},{4,5},{5,4},{6,7},{7,6},{8,9},{9,8},{10,11... | collective-permute-start | bytes 491528 | tf_op jit(solution)/shard_map/ppermute | solution.py:209
  38.3 1.4 %collective-permute-start.10 = (f32[320,128]{1,0:T(8,128)S(1)}, f32[320,128]{1,0:T(8,128)S(1)}, u32[]{:S(2)}, u32[]{:S(2)}) collective-permute-start(f32[320,128]{1,0:T(8,128)S(1)} %collective-permute-done.9), channel_id=1, source_target_pairs={{0,1},{1,0},{2,3},{3,2},{4,5},{5,4},{6,7},{7,6},{8,9},{9,8},{10,11... | collective-permute-start | bytes 491528 | tf_op jit(solution)/shard_map/ppermute | solution.py:209
  38.3 1.6 %collective-permute-start.12 = (bf16[256,256]{1,0:T(8,128)(2,1)S(1)}, bf16[256,256]{1,0:T(8,128)(2,1)S(1)}, u32[]{:S(2)}, u32[]{:S(2)}) collective-permute-start(bf16[256,256]{1,0:T(8,128)(2,1)S(1)} %get-tuple-element.13.refs_2_), channel_id=1, source_target_pairs={{0,1},{1,0},{2,3},{3,2},{4,5},{5,4},{6,7},{7,6},{8,9},{9,8},{10,11... | collective-permute-start | bytes 393224 | tf_op jit(solution)/shard_map/ppermute | solution.py:209

commit v5 on v4

--- a/solution.py
+++ b/solution.py
@@ -9,6 +9,7 @@
 
 F32, BF16 = jnp.float32, jnp.bfloat16
 HALF = 128
+SQUARE = HALF // 2
 BLOCK = 128
 VMEM = pltpu.VMEM
 
@@ -54,8 +55,13 @@
     low, high = own[:, :HALF], own[:, HALF:]
     first = other[:, pl.ds(pl.multiple_of(core * HALF, HALF), HALF)]
     second = other[:, pl.ds(pl.multiple_of((1 - core) * HALF, HALF), HALF)]
-    for i, (a, b) in enumerate(((low, low), (high, low), (high, high), (low, first), (high, second))):
+    for i, (a, b) in enumerate(((high, low), (low, first), (high, second))):
         out[i * HALF : (i + 1) * HALF, :] = dot(a, b, 0, 0, lax.Precision.DEFAULT)
+    squares = [dot(a, a, 0, 0, lax.Precision.DEFAULT) for a in (low, high)]
+    at = 3 * HALF
+    for x in [x[SQUARE:] for x in squares] + [jnp.concatenate([x[:SQUARE, :SQUARE] for x in squares], 1)]:
+        out[at : at + SQUARE, :] = x
+        at += SQUARE
 
 
 def eliminate(groups, slots, factor_slots):
@@ -151,12 +157,18 @@
     side = 2 * HALF
     block = lambda ref, i: ref[i * HALF : (i + 1) * HALF, :]
     for ref, at in ((blocks, 0), (others, side)):
-        corner = block(ref, 1)
-        moments[at : at + HALF, at : at + HALF] = block(ref, 0)
+        corner = block(ref, 0)
         moments[at + HALF : at + side, at : at + HALF] = corner
         moments[at : at + HALF, at + HALF : at + side] = corner.T
-        moments[at + HALF : at + side, at + HALF : at + side] = block(ref, 2)
-    mine, theirs = (block(blocks, 3), block(blocks, 4)), (block(others, 3), block(others, 4))
+        firsts = ref[3 * HALF + 2 * SQUARE :, :]
+        for h in range(2):
+            lower = ref[3 * HALF + h * SQUARE : 3 * HALF + (h + 1) * SQUARE, :]
+            top, columns = at + h * HALF, slice(at + h * HALF, at + (h + 1) * HALF)
+            moments[top : top + SQUARE, columns] = jnp.concatenate(
+                [firsts[:, h * SQUARE : (h + 1) * SQUARE], lower[:, :SQUARE].T], 1
+            )
+            moments[top + SQUARE : top + HALF, columns] = lower
+    mine, theirs = (block(blocks, 1), block(blocks, 2)), (block(others, 1), block(others, 2))
     for h in range(2):
         column = pl.ds(pl.multiple_of(side + (h + core - 2 * h * core) * HALF, HALF), HALF)
         moments[h * HALF : (h + 1) * HALF, column] = mine[h]
@@ -285,7 +297,7 @@
     )
     standard_other = swap(standard, "mark", 1)
     got_test = swap(test_matrix, "samp", gather_plan(lax.axis_size("samp"))[0])
-    blocks = call(moment_kernel, jax.ShapeDtypeStruct((5 * HALF, HALF), F32), [standard, standard_other])
+    blocks = call(moment_kernel, jax.ShapeDtypeStruct((3 * HALF + 3 * SQUARE, HALF), F32), [standard, standard_other])
     blocks, others, test, test_other = sum_and_gather(blocks, test_matrix, got_test)
     kernel = lambda *refs: final_kernel(samples, *refs)
     basis, loadings = call(

time: 49.2 us -> 48.3 us (0.982)
  waiting for transfers between devices: 18.8 us -> 17.6 us
    ppermute x5, waiting for transfers between devices: 10.5 us -> 9.29 us  [swap_by_core(): return lax.ppermute(x, ('samp', 'mark'), pairs)]
where the time goes in v5:
time: 48.3 us; the launch traced here: 48.1 us
  starting transfers between devices  18.3 us (38%)
  waiting for transfers between devices  17.6 us (36%)
  Pallas kernels  9.69 us (20%)
  local copies, waits for them, and re-layouts  1.66 us (3%)
  between operations  0.72 us (1%)
    pallas_call x6, Pallas kernels, call(): pl.pallas_call(kernel, out_shape=shapes, in_specs=[vmem] * len(inputs), o...  9.69 us
    ppermute x8, starting transfers between devices, swap(): lax.ppermute(x, axis, [(i, i ^ bit) for i in range(lax.axis_size(axis))])  9.65 us
    ppermute x5, waiting for transfers between devices, swap_by_core(): return lax.ppermute(x, ('samp', 'mark'), pairs)  9.29 us
    ppermute x5, starting transfers between devices, swap_by_core(): return lax.ppermute(x, ('samp', 'mark'), pairs)  8.66 us
    ppermute x8, waiting for transfers between devices, swap(): lax.ppermute(x, axis, [(i, i ^ bit) for i in range(lax.axis_size(axis))])  8.32 us
    unnamed x11, local copies, waits for them, and re-layouts  1.66 us
  transfers between devices with their start and end apart: 13, of which 8 were waited for; matrix products, arithmetic and copies ran while one was open for 0% of the time, Pallas kernels for 1%

profile of v5, /device:TPU:0, one launch (start us, length us, event | category | flops | bytes accessed | tf_op | source)
XLA Modules:
  0.0 48.1 jit_solution(17133426963843019330)
XLA Ops:
  0.7 0.7 %copy-done.3 = s32[256]{0:T(256)S(1)} copy-done((s32[256]{0:T(256)S(1)}, s32[256]{0:T(256)}, u32[]{:S(2)}) %copy-start.3) | copy-done | bytes 1048
  1.3 0.9 %copy-done = bf16[512,256]{1,0:T(8,128)(2,1)S(1)} copy-done((bf16[512,256]{1,0:T(8,128)(2,1)S(1)}, bf16[512,256]{1,0:T(8,128)(2,1)}, u32[]{:S(2)}) %copy-start) | copy-done | bytes 262168
  2.3 0.1 shard_map.68.own.refs_4_
  2.5 0.5 %collective-permute-start = (bf16[512,256]{1,0:T(8,128)(2,1)S(1)}, bf16[512,256]{1,0:T(8,128)(2,1)S(1)}, u32[]{:S(2)}, u32[]{:S(2)}) collective-permute-start(bf16[512,256]{1,0:T(8,128)(2,1)S(1)} %shard_map.68.own.refs_4_), channel_id=1, source_target_pairs={{0,1},{1,0},{2,3},{3,2},{4,5},{5,4},{6,7},{7,6},{8,9},{9,8},{10,11... | collective-permute-start | bytes 786440 | tf_op jit(solution)/shard_map/ppermute | solution.py:221
  3.0 4.0 %collective-permute-start.2 = (bf16[16,256]{1,0:T(8,128)(2,1)S(1)}, bf16[16,256]{1,0:T(8,128)(2,1)S(1)}, u32[]{:S(2)}, u32[]{:S(2)}) collective-permute-start(bf16[16,256]{1,0:T(8,128)(2,1)S(1)} %copy-done.4), channel_id=1, source_target_pairs={{0,16},{2,18},{4,20},{6,22},{8,24},{10,26},{12,28},{14,30},{16,0},... | collective-permute-start | bytes 24584 | tf_op jit(solution)/shard_map/ppermute | solution.py:221
  7.0 0.4 shard_map.69
  7.5 1.6 %collective-permute-start.1 = (f32[288,128]{1,0:T(8,128)S(1)}, f32[288,128]{1,0:T(8,128)S(1)}, u32[]{:S(2)}, u32[]{:S(2)}) collective-permute-start(f32[288,128]{1,0:T(8,128)S(1)} %get-tuple-element.14), channel_id=1, source_target_pairs={{0,2},{1,3},{2,0},{3,1},{4,6},{5,7},{6,4},{7,5},{8,10},{9,11},{10,... | collective-permute-start | bytes 442376 | tf_op jit(solution)/shard_map/ppermute | solution.py:226
  9.1 1.6 %collective-permute-start.3 = (bf16[32,256]{1,0:T(8,128)(2,1)S(1)}, bf16[32,256]{1,0:T(8,128)(2,1)S(1)}, u32[]{:S(2)}, u32[]{:S(2)}) collective-permute-start(bf16[32,256]{1,0:T(8,128)(2,1)S(1)} %constant_dynamic-update-slice_fusion.blocks), channel_id=1, source_target_pairs={{0,8},{2,10},{4,12},{6,14},{8,0},{10,2},{12,4},{14,6},{16,24},{18,... | collective-permute-start | bytes 49160 | tf_op jit(solution)/shard_map/ppermute | solution.py:221
  10.6 2.2 %collective-permute-done.3.got_blocks = bf16[32,256]{1,0:T(8,128)(2,1)S(1)} collective-permute-done((bf16[32,256]{1,0:T(8,128)(2,1)S(1)}, bf16[32,256]{1,0:T(8,128)(2,1)S(1)}, u32[]{:S(2)}, u32[]{:S(2)}) %collective-permute-start.3) | collective-permute-done | bytes 16416 | tf_op jit(solution)/shard_map/ppermute | solution.py:221
  12.8 0.3 collective-permute-done.1.got
  13.1 1.6 %collective-permute-start.4 = (f32[288,128]{1,0:T(8,128)S(1)}, f32[288,128]{1,0:T(8,128)S(1)}, u32[]{:S(2)}, u32[]{:S(2)}) collective-permute-start(f32[288,128]{1,0:T(8,128)S(1)} %get-tuple-element.8.x), channel_id=1, source_target_pairs={{0,8},{1,5},{2,10},{3,7},{4,12},{5,1},{6,14},{7,3},{8,0},{9,13},{1... | collective-permute-start | bytes 442376 | tf_op jit(solution)/shard_map/ppermute | solution.py:226
  14.7 1.5 %collective-permute-start.5 = (bf16[64,256]{1,0:T(8,128)(2,1)S(1)}, bf16[64,256]{1,0:T(8,128)(2,1)S(1)}, u32[]{:S(2)}, u32[]{:S(2)}) collective-permute-start(bf16[64,256]{1,0:T(8,128)(2,1)S(1)} %get-tuple-element.9.blocks), channel_id=1, source_target_pairs={{0,4},{2,6},{4,0},{6,2},{8,12},{10,14},{12,8},{14,10},{16,20},{18,... | collective-permute-start | bytes 98312 | tf_op jit(solution)/shard_map/ppermute | solution.py:221
  16.3 2.4 %collective-permute-done.5.got_blocks = bf16[64,256]{1,0:T(8,128)(2,1)S(1)} collective-permute-done((bf16[64,256]{1,0:T(8,128)(2,1)S(1)}, bf16[64,256]{1,0:T(8,128)(2,1)S(1)}, u32[]{:S(2)}, u32[]{:S(2)}) %collective-permute-start.5) | collective-permute-done | bytes 32800 | tf_op jit(solution)/shard_map/ppermute | solution.py:221
  18.7 1.6 %collective-permute-start.6 = (f32[288,128]{1,0:T(8,128)S(1)}, f32[288,128]{1,0:T(8,128)S(1)}, u32[]{:S(2)}, u32[]{:S(2)}) collective-permute-start(f32[288,128]{1,0:T(8,128)S(1)} %get-tuple-element.10.x), channel_id=1, source_target_pairs={{0,4},{1,9},{2,6},{3,11},{4,0},{5,13},{6,2},{7,15},{8,12},{9,1},{1... | collective-permute-start | bytes 442376 | tf_op jit(solution)/shard_map/ppermute | solution.py:226
  20.3 1.5 %collective-permute-start.7 = (bf16[128,256]{1,0:T(8,128)(2,1)S(1)}, bf16[128,256]{1,0:T(8,128)(2,1)S(1)}, u32[]{:S(2)}, u32[]{:S(2)}) collective-permute-start(bf16[128,256]{1,0:T(8,128)(2,1)S(1)} %get-tuple-element.11.blocks), channel_id=1, source_target_pairs={{0,2},{2,0},{4,6},{6,4},{8,10},{10,8},{12,14},{14,12},{16,18},{18,... | collective-permute-start | bytes 196616 | tf_op jit(solution)/shard_map/ppermute | solution.py:221
  21.8 2.8 %collective-permute-done.7.got_blocks = bf16[128,256]{1,0:T(8,128)(2,1)S(1)} collective-permute-done((bf16[128,256]{1,0:T(8,128)(2,1)S(1)}, bf16[128,256]{1,0:T(8,128)(2,1)S(1)}, u32[]{:S(2)}, u32[]{:S(2)}) %collective-permute-start.7) | collective-permute-done | bytes 65568 | tf_op jit(solution)/shard_map/ppermute | solution.py:221
  24.6 2.3 %collective-permute-start.8 = (f32[288,128]{1,0:T(8,128)S(1)}, f32[288,128]{1,0:T(8,128)S(1)}, u32[]{:S(2)}, u32[]{:S(2)}) collective-permute-start(f32[288,128]{1,0:T(8,128)S(1)} %get-tuple-element.12), channel_id=1, source_target_pairs={{0,16},{1,17},{2,18},{3,19},{4,20},{5,21},{6,22},{7,23},{8,24},{9,... | collective-permute-start | bytes 442376 | tf_op jit(solution)/shard_map/ppermute | solution.py:226
  26.9 5.4 %collective-permute-done.8 = f32[288,128]{1,0:T(8,128)S(1)} collective-permute-done((f32[288,128]{1,0:T(8,128)S(1)}, f32[288,128]{1,0:T(8,128)S(1)}, u32[]{:S(2)}, u32[]{:S(2)}) %collective-permute-start.8) | collective-permute-done | bytes 147488 | tf_op jit(solution)/shard_map/ppermute | solution.py:226
  32.3 1.6 %collective-permute-start.9 = (f32[288,128]{1,0:T(8,128)S(1)}, f32[288,128]{1,0:T(8,128)S(1)}, u32[]{:S(2)}, u32[]{:S(2)}) collective-permute-start(f32[288,128]{1,0:T(8,128)S(1)} %add.3), channel_id=1, source_target_pairs={{0,2},{1,3},{2,0},{3,1},{4,6},{5,7},{6,4},{7,5},{8,10},{9,11},{10,... | collective-permute-start | bytes 442376 | tf_op jit(solution)/shard_map/ppermute | solution.py:226
  33.8 3.6 %collective-permute-done.9 = f32[288,128]{1,0:T(8,128)S(1)} collective-permute-done((f32[288,128]{1,0:T(8,128)S(1)}, f32[288,128]{1,0:T(8,128)S(1)}, u32[]{:S(2)}, u32[]{:S(2)}) %collective-permute-start.9) | collective-permute-done | bytes 147488 | tf_op jit(solution)/shard_map/ppermute | solution.py:226
  37.5 0.5 %collective-permute-start.12 = (bf16[256,256]{1,0:T(8,128)(2,1)S(1)}, bf16[256,256]{1,0:T(8,128)(2,1)S(1)}, u32[]{:S(2)}, u32[]{:S(2)}) collective-permute-start(bf16[256,256]{1,0:T(8,128)(2,1)S(1)} %get-tuple-element.13.refs_2_), channel_id=1, source_target_pairs={{0,1},{1,0},{2,3},{3,2},{4,5},{5,4},{6,7},{7,6},{8,9},{9,8},{10,11... | collective-permute-start | bytes 393224 | tf_op jit(solution)/shard_map/ppermute | solution.py:221
  38.0 0.8 %collective-permute-done.10 = f32[288,128]{1,0:T(8,128)S(1)} collective-permute-done((f32[288,128]{1,0:T(8,128)S(1)}, f32[288,128]{1,0:T(8,128)S(1)}, u32[]{:S(2)}, u32[]{:S(2)}) %collective-permute-start.10) | collective-permute-done | bytes 147488 | tf_op jit(solution)/shard_map/ppermute | solution.py:221
  38.9 0.2 collective-permute-done.12.refs_3_
  39.0 9.1 %shard_map.73 = (f32[256,256]{1,0:T(8,128)}, f32[16,256]{1,0:T(8,128)}) custom-call(f32[576,128]{1,0:T(8,128)S(1)} %maximum_select_fusion.refs_0_, f32[576,128]{1,0:T(8,128)S(1)} %maximum_select_fusion.1.refs_1_, bf16[256,256]{1,0:T(8,128)(2,1)S(1)} %get-tuple-element.13.refs_2_, bf16[256,256]{1,0:T(8,128)(2,1)S(1)} %collective-permute-done.12.refs_3_, ...), custom_call_target="tpu_custom_call" | custom-call | tf_op jit(solution)/shard_map/pallas_call | solution.py:210
  (24 shorter events, 0.3 us)
Async XLA Ops:
  0.6 0.7 %copy-start.3 = (s32[256]{0:T(256)S(1)}, s32[256]{0:T(256)}, u32[]{:S(2)}) copy-start(s32[256]{0:T(256)} %param.7) | copy-start | bytes 3076
  0.6 0.7 %copy-start.1 = (f32[512]{0:T(512)S(1)}, f32[512]{0:T(512)}, u32[]{:S(2)}) copy-start(f32[512]{0:T(512)} %param.8) | copy-start | bytes 6148
  0.7 0.7 %copy-start.2 = (s32[256]{0:T(256)S(1)}, s32[256]{0:T(256)}, u32[]{:S(2)}) copy-start(s32[256]{0:T(256)} %param.6) | copy-start | bytes 3076
  1.3 0.9 %copy-start = (bf16[512,256]{1,0:T(8,128)(2,1)S(1)}, bf16[512,256]{1,0:T(8,128)(2,1)}, u32[]{:S(2)}) copy-start(bf16[512,256]{1,0:T(8,128)(2,1)} %dosage.1) | copy-start | bytes 786436
  2.3 0.7 %copy-start.4 = (bf16[16,256]{1,0:T(8,128)(2,1)S(1)}, bf16[16,256]{1,0:T(8,128)(2,1)}, u32[]{:S(2)}) copy-start(bf16[16,256]{1,0:T(8,128)(2,1)} %param.9) | copy-start | bytes 24580
  2.5 4.6 %collective-permute-start = (bf16[512,256]{1,0:T(8,128)(2,1)S(1)}, bf16[512,256]{1,0:T(8,128)(2,1)S(1)}, u32[]{:S(2)}, u32[]{:S(2)}) collective-permute-start(bf16[512,256]{1,0:T(8,128)(2,1)S(1)} %shard_map.68.own.refs_4_), channel_id=1, source_target_pairs={{0,1},{1,0},{2,3},{3,2},{4,5},{5,4},{6,7},{7,6},{8,9},{9,8},{10,11... | collective-permute-start | bytes 786440 | tf_op jit(solution)/shard_map/ppermute | solution.py:221
  3.0 6.1 %collective-permute-start.2 = (bf16[16,256]{1,0:T(8,128)(2,1)S(1)}, bf16[16,256]{1,0:T(8,128)(2,1)S(1)}, u32[]{:S(2)}, u32[]{:S(2)}) collective-permute-start(bf16[16,256]{1,0:T(8,128)(2,1)S(1)} %copy-done.4), channel_id=1, source_target_pairs={{0,16},{2,18},{4,20},{6,22},{8,24},{10,26},{12,28},{14,30},{16,0},... | collective-permute-start | bytes 24584 | tf_op jit(solution)/shard_map/ppermute | solution.py:221
  7.5 5.6 %collective-permute-start.1 = (f32[288,128]{1,0:T(8,128)S(1)}, f32[288,128]{1,0:T(8,128)S(1)}, u32[]{:S(2)}, u32[]{:S(2)}) collective-permute-start(f32[288,128]{1,0:T(8,128)S(1)} %get-tuple-element.14), channel_id=1, source_target_pairs={{0,2},{1,3},{2,0},{3,1},{4,6},{5,7},{6,4},{7,5},{8,10},{9,11},{10,... | collective-permute-start | bytes 442376 | tf_op jit(solution)/shard_map/ppermute | solution.py:226
  9.1 3.7 %collective-permute-start.3 = (bf16[32,256]{1,0:T(8,128)(2,1)S(1)}, bf16[32,256]{1,0:T(8,128)(2,1)S(1)}, u32[]{:S(2)}, u32[]{:S(2)}) collective-permute-start(bf16[32,256]{1,0:T(8,128)(2,1)S(1)} %constant_dynamic-update-slice_fusion.blocks), channel_id=1, source_target_pairs={{0,8},{2,10},{4,12},{6,14},{8,0},{10,2},{12,4},{14,6},{16,24},{18,... | collective-permute-start | bytes 49160 | tf_op jit(solution)/shard_map/ppermute | solution.py:221
  13.1 5.6 %collective-permute-start.4 = (f32[288,128]{1,0:T(8,128)S(1)}, f32[288,128]{1,0:T(8,128)S(1)}, u32[]{:S(2)}, u32[]{:S(2)}) collective-permute-start(f32[288,128]{1,0:T(8,128)S(1)} %get-tuple-element.8.x), channel_id=1, source_target_pairs={{0,8},{1,5},{2,10},{3,7},{4,12},{5,1},{6,14},{7,3},{8,0},{9,13},{1... | collective-permute-start | bytes 442376 | tf_op jit(solution)/shard_map/ppermute | solution.py:226
  14.7 3.9 %collective-permute-start.5 = (bf16[64,256]{1,0:T(8,128)(2,1)S(1)}, bf16[64,256]{1,0:T(8,128)(2,1)S(1)}, u32[]{:S(2)}, u32[]{:S(2)}) collective-permute-start(bf16[64,256]{1,0:T(8,128)(2,1)S(1)} %get-tuple-element.9.blocks), channel_id=1, source_target_pairs={{0,4},{2,6},{4,0},{6,2},{8,12},{10,14},{12,8},{14,10},{16,20},{18,... | collective-permute-start | bytes 98312 | tf_op jit(solution)/shard_map/ppermute | solution.py:221
  18.7 5.9 %collective-permute-start.6 = (f32[288,128]{1,0:T(8,128)S(1)}, f32[288,128]{1,0:T(8,128)S(1)}, u32[]{:S(2)}, u32[]{:S(2)}) collective-permute-start(f32[288,128]{1,0:T(8,128)S(1)} %get-tuple-element.10.x), channel_id=1, source_target_pairs={{0,4},{1,9},{2,6},{3,11},{4,0},{5,13},{6,2},{7,15},{8,12},{9,1},{1... | collective-permute-start | bytes 442376 | tf_op jit(solution)/shard_map/ppermute | solution.py:226
  20.3 4.3 %collective-permute-start.7 = (bf16[128,256]{1,0:T(8,128)(2,1)S(1)}, bf16[128,256]{1,0:T(8,128)(2,1)S(1)}, u32[]{:S(2)}, u32[]{:S(2)}) collective-permute-start(bf16[128,256]{1,0:T(8,128)(2,1)S(1)} %get-tuple-element.11.blocks), channel_id=1, source_target_pairs={{0,2},{2,0},{4,6},{6,4},{8,10},{10,8},{12,14},{14,12},{16,18},{18,... | collective-permute-start | bytes 196616 | tf_op jit(solution)/shard_map/ppermute | solution.py:221
  24.6 7.7 %collective-permute-start.8 = (f32[288,128]{1,0:T(8,128)S(1)}, f32[288,128]{1,0:T(8,128)S(1)}, u32[]{:S(2)}, u32[]{:S(2)}) collective-permute-start(f32[288,128]{1,0:T(8,128)S(1)} %get-tuple-element.12), channel_id=1, source_target_pairs={{0,16},{1,17},{2,18},{3,19},{4,20},{5,21},{6,22},{7,23},{8,24},{9,... | collective-permute-start | bytes 442376 | tf_op jit(solution)/shard_map/ppermute | solution.py:226
  32.3 5.2 %collective-permute-start.9 = (f32[288,128]{1,0:T(8,128)S(1)}, f32[288,128]{1,0:T(8,128)S(1)}, u32[]{:S(2)}, u32[]{:S(2)}) collective-permute-start(f32[288,128]{1,0:T(8,128)S(1)} %add.3), channel_id=1, source_target_pairs={{0,2},{1,3},{2,0},{3,1},{4,6},{5,7},{6,4},{7,5},{8,10},{9,11},{10,... | collective-permute-start | bytes 442376 | tf_op jit(solution)/shard_map/ppermute | solution.py:226
  33.8 4.2 %collective-permute-start.11 = (f32[288,128]{1,0:T(8,128)S(1)}, f32[288,128]{1,0:T(8,128)S(1)}, u32[]{:S(2)}, u32[]{:S(2)}) collective-permute-start(f32[288,128]{1,0:T(8,128)S(1)} %add.3), channel_id=1, source_target_pairs={{0,1},{1,0},{2,3},{3,2},{4,5},{5,4},{6,7},{7,6},{8,9},{9,8},{10,11... | collective-permute-start | bytes 442376 | tf_op jit(solution)/shard_map/ppermute | solution.py:221
  37.5 1.4 %collective-permute-start.10 = (f32[288,128]{1,0:T(8,128)S(1)}, f32[288,128]{1,0:T(8,128)S(1)}, u32[]{:S(2)}, u32[]{:S(2)}) collective-permute-start(f32[288,128]{1,0:T(8,128)S(1)} %collective-permute-done.9), channel_id=1, source_target_pairs={{0,1},{1,0},{2,3},{3,2},{4,5},{5,4},{6,7},{7,6},{8,9},{9,8},{10,11... | collective-permute-start | bytes 442376 | tf_op jit(solution)/shard_map/ppermute | solution.py:221
  37.5 1.6 %collective-permute-start.12 = (bf16[256,256]{1,0:T(8,128)(2,1)S(1)}, bf16[256,256]{1,0:T(8,128)(2,1)S(1)}, u32[]{:S(2)}, u32[]{:S(2)}) collective-permute-start(bf16[256,256]{1,0:T(8,128)(2,1)S(1)} %get-tuple-element.13.refs_2_), channel_id=1, source_target_pairs={{0,1},{1,0},{2,3},{3,2},{4,5},{5,4},{6,7},{7,6},{8,9},{9,8},{10,11... | collective-permute-start | bytes 393224 | tf_op jit(solution)/shard_map/ppermute | solution.py:221

commit v6 on v5

--- a/solution.py
+++ b/solution.py
@@ -150,9 +150,22 @@
         rest = jnp.where((lane >= at) & (lane < end), 0.0, below) - dot(joined[:, end:], joined, 0, 0)
 
 
-def final_kernel(
-    total, blocks, others, test, test_other, standard, standard_other, basis, loadings, moments, inverse, product, gathered, *slots
-):
+def sketch_kernel(total, few, test, test_other, standard, standard_other, tests, high, mid):
+    samp, core = lax.axis_index("samp"), lax.axis_index("mark")
+    side, count = test.shape[0], test.shape[0] // few
+    for ref, at in ((test, 0), (test_other, side)):
+        for i in range(count):
+            row = pl.multiple_of(at + (samp ^ source(i, count)) * few, few)
+            tests[pl.ds(row, few), :] = ref[i * few : (i + 1) * few, :]
+    share = high.shape[0]
+    rows = pl.ds(pl.multiple_of(core * share, share), share)
+    sketch = dot(standard[rows, :], tests[:side, :], 1, 0, lax.Precision.DEFAULT) + dot(
+        standard_other[rows, :], tests[side:, :], 1, 0, lax.Precision.DEFAULT
+    )
+    high[...], mid[...], _ = pieces(math.sqrt(total) * sketch)
+
+
+def final_kernel(blocks, others, gathered, sketch_high, sketch_mid, basis, loadings, moments, inverse, product, *slots):
     samp, core = lax.axis_index("samp"), lax.axis_index("mark")
     side = 2 * HALF
     block = lambda ref, i: ref[i * HALF : (i + 1) * HALF, :]
@@ -177,21 +190,9 @@
         column = pl.ds(pl.multiple_of((h + away - 2 * h * away) * HALF, HALF), HALF)
         moments[side + h * HALF : side + (h + 1) * HALF, column] = theirs[h]
         moments[column, side + h * HALF : side + (h + 1) * HALF] = theirs[h].T
-    few = loadings.shape[0]
-    count = test.shape[0] // few
-    for ref, at in ((test, 0), (test_other, side)):
-        for i in range(count):
-            row = pl.multiple_of(at + (samp ^ source(i, count)) * few, few)
-            gathered[pl.ds(row, few), :] = ref[i * few : (i + 1) * few, :]
     tests = gathered[...]
     product[...] = dot_pieces(pieces(moments[...]), tests, 1, 0)
     gram = dot_pieces_right(tests, pieces(product[...]), 0, 0)
-    share = basis.shape[0]
-    rows = pl.ds(pl.multiple_of(core * share, share), share)
-    sketch = dot(standard[rows, :], tests[:side], 1, 0, lax.Precision.DEFAULT) + dot(
-        standard_other[rows, :], tests[side:], 1, 0, lax.Precision.DEFAULT
-    )
-    sketch_high, sketch_mid, _ = pieces(math.sqrt(total) * sketch)
     few = loadings.shape[0]
     own = product[pl.ds(pl.multiple_of(samp * few, few), few), :]
 
@@ -299,12 +300,24 @@
     got_test = swap(test_matrix, "samp", gather_plan(lax.axis_size("samp"))[0])
     blocks = call(moment_kernel, jax.ShapeDtypeStruct((3 * HALF + 3 * SQUARE, HALF), F32), [standard, standard_other])
     blocks, others, test, test_other = sum_and_gather(blocks, test_matrix, got_test)
-    kernel = lambda *refs: final_kernel(samples, *refs)
+    prepare = lambda *refs: sketch_kernel(samples, few, *refs)
+    share = jax.ShapeDtypeStruct((rows // 2, rank), BF16)
+    prepared = call(
+        prepare,
+        [jax.ShapeDtypeStruct((2 * cols, rank), BF16), share, share],
+        [test, test_other, standard, standard_other],
+    )
     basis, loadings = call(
-        kernel,
+        final_kernel,
         [jax.ShapeDtypeStruct((rows // 2, rank), F32), jax.ShapeDtypeStruct((few, rank), F32)],
-        [blocks, others, test, test_other, standard, standard_other],
-        [VMEM((2 * cols, 2 * cols), F32), VMEM((rank, rank), F32), VMEM((2 * cols, rank), F32), VMEM((2 * cols, rank), BF16), VMEM((36, 8, BLOCK), F32), VMEM((32, 8, BLOCK), F32)],
+        [blocks, others, *prepared],
+        [
+            VMEM((2 * cols, 2 * cols), F32),
+            VMEM((rank, rank), F32),
+            VMEM((2 * cols, rank), F32),
+            VMEM((36, 8, BLOCK), F32),
+            VMEM((32, 8, BLOCK), F32),
+        ],
     )
     return basis, loadings
 

time: 48.3 us -> 48.1 us (level)
    ppermute x5, waiting for transfers between devices: 9.29 us -> 8.78 us  [swap_by_core(): return lax.ppermute(x, ('samp', 'mark'), pairs)]
    pallas_call x6 -> x7, Pallas kernels: 9.69 us -> 9.94 us  [call(): pl.pallas_call(kernel, out_shape=shapes, in_specs=[vmem] * len(inputs), o...]
  transfers between devices with their start and end apart: 13 -> 13, of which waited for: 8 -> 7; matrix products, arithmetic and copies ran while one was open for 0% -> 0% of each run, Pallas kernels for 1% -> 1%
where the time goes in v6:
time: 48.1 us; the launch traced here: 47.9 us
  starting transfers between devices  18.3 us (38%)
  waiting for transfers between devices  17.2 us (36%)
  Pallas kernels  9.94 us (21%)
  local copies, waits for them, and re-layouts  1.66 us (3%)
  between operations  0.74 us (2%)
    pallas_call x7, Pallas kernels, call(): pl.pallas_call(kernel, out_shape=shapes, in_specs=[vmem] * len(inputs), o...  9.94 us
    ppermute x8, starting transfers between devices, swap(): lax.ppermute(x, axis, [(i, i ^ bit) for i in range(lax.axis_size(axis))])  9.65 us
    ppermute x5, waiting for transfers between devices, swap_by_core(): return lax.ppermute(x, ('samp', 'mark'), pairs)  8.78 us
    ppermute x5, starting transfers between devices, swap_by_core(): return lax.ppermute(x, ('samp', 'mark'), pairs)  8.66 us
    ppermute x8, waiting for transfers between devices, swap(): lax.ppermute(x, axis, [(i, i ^ bit) for i in range(lax.axis_size(axis))])  8.39 us
    unnamed x11, local copies, waits for them, and re-layouts  1.66 us
  transfers between devices with their start and end apart: 13, of which 7 were waited for; matrix products, arithmetic and copies ran while one was open for 0% of the time, Pallas kernels for 1%

profile of v6, /device:TPU:0, one launch (start us, length us, event | category | flops | bytes accessed | tf_op | source)
XLA Modules:
  0.0 47.9 jit_solution(10141234817201328531)
XLA Ops:
  0.7 0.7 %copy-done.3 = s32[256]{0:T(256)S(1)} copy-done((s32[256]{0:T(256)S(1)}, s32[256]{0:T(256)}, u32[]{:S(2)}) %copy-start.3) | copy-done | bytes 1048
  1.3 0.9 %copy-done = bf16[512,256]{1,0:T(8,128)(2,1)S(1)} copy-done((bf16[512,256]{1,0:T(8,128)(2,1)S(1)}, bf16[512,256]{1,0:T(8,128)(2,1)}, u32[]{:S(2)}) %copy-start) | copy-done | bytes 262168
  2.3 0.1 shard_map.68.own.refs_2_
  2.5 0.5 %collective-permute-start = (bf16[512,256]{1,0:T(8,128)(2,1)S(1)}, bf16[512,256]{1,0:T(8,128)(2,1)S(1)}, u32[]{:S(2)}, u32[]{:S(2)}) collective-permute-start(bf16[512,256]{1,0:T(8,128)(2,1)S(1)} %shard_map.68.own.refs_2_), channel_id=1, source_target_pairs={{0,1},{1,0},{2,3},{3,2},{4,5},{5,4},{6,7},{7,6},{8,9},{9,8},{10,11... | collective-permute-start | bytes 786440 | tf_op jit(solution)/shard_map/ppermute | solution.py:222
  3.0 4.0 %collective-permute-start.2 = (bf16[16,256]{1,0:T(8,128)(2,1)S(1)}, bf16[16,256]{1,0:T(8,128)(2,1)S(1)}, u32[]{:S(2)}, u32[]{:S(2)}) collective-permute-start(bf16[16,256]{1,0:T(8,128)(2,1)S(1)} %copy-done.4), channel_id=1, source_target_pairs={{0,16},{2,18},{4,20},{6,22},{8,24},{10,26},{12,28},{14,30},{16,0},... | collective-permute-start | bytes 24584 | tf_op jit(solution)/shard_map/ppermute | solution.py:222
  7.0 0.4 shard_map.69
  7.5 1.6 %collective-permute-start.1 = (f32[288,128]{1,0:T(8,128)S(1)}, f32[288,128]{1,0:T(8,128)S(1)}, u32[]{:S(2)}, u32[]{:S(2)}) collective-permute-start(f32[288,128]{1,0:T(8,128)S(1)} %get-tuple-element.20), channel_id=1, source_target_pairs={{0,2},{1,3},{2,0},{3,1},{4,6},{5,7},{6,4},{7,5},{8,10},{9,11},{10,... | collective-permute-start | bytes 442376 | tf_op jit(solution)/shard_map/ppermute | solution.py:227
  9.1 1.6 %collective-permute-start.3 = (bf16[32,256]{1,0:T(8,128)(2,1)S(1)}, bf16[32,256]{1,0:T(8,128)(2,1)S(1)}, u32[]{:S(2)}, u32[]{:S(2)}) collective-permute-start(bf16[32,256]{1,0:T(8,128)(2,1)S(1)} %constant_dynamic-update-slice_fusion.blocks), channel_id=1, source_target_pairs={{0,8},{2,10},{4,12},{6,14},{8,0},{10,2},{12,4},{14,6},{16,24},{18,... | collective-permute-start | bytes 49160 | tf_op jit(solution)/shard_map/ppermute | solution.py:222
  10.6 2.2 %collective-permute-done.3.got_blocks = bf16[32,256]{1,0:T(8,128)(2,1)S(1)} collective-permute-done((bf16[32,256]{1,0:T(8,128)(2,1)S(1)}, bf16[32,256]{1,0:T(8,128)(2,1)S(1)}, u32[]{:S(2)}, u32[]{:S(2)}) %collective-permute-start.3) | collective-permute-done | bytes 16416 | tf_op jit(solution)/shard_map/ppermute | solution.py:222
  12.8 0.3 collective-permute-done.1.got
  13.1 1.6 %collective-permute-start.4 = (f32[288,128]{1,0:T(8,128)S(1)}, f32[288,128]{1,0:T(8,128)S(1)}, u32[]{:S(2)}, u32[]{:S(2)}) collective-permute-start(f32[288,128]{1,0:T(8,128)S(1)} %get-tuple-element.11.x), channel_id=1, source_target_pairs={{0,8},{1,5},{2,10},{3,7},{4,12},{5,1},{6,14},{7,3},{8,0},{9,13},{1... | collective-permute-start | bytes 442376 | tf_op jit(solution)/shard_map/ppermute | solution.py:227
  14.7 1.5 %collective-permute-start.5 = (bf16[64,256]{1,0:T(8,128)(2,1)S(1)}, bf16[64,256]{1,0:T(8,128)(2,1)S(1)}, u32[]{:S(2)}, u32[]{:S(2)}) collective-permute-start(bf16[64,256]{1,0:T(8,128)(2,1)S(1)} %get-tuple-element.12.blocks), channel_id=1, source_target_pairs={{0,4},{2,6},{4,0},{6,2},{8,12},{10,14},{12,8},{14,10},{16,20},{18,... | collective-permute-start | bytes 98312 | tf_op jit(solution)/shard_map/ppermute | solution.py:222
  16.3 2.4 %collective-permute-done.5.got_blocks = bf16[64,256]{1,0:T(8,128)(2,1)S(1)} collective-permute-done((bf16[64,256]{1,0:T(8,128)(2,1)S(1)}, bf16[64,256]{1,0:T(8,128)(2,1)S(1)}, u32[]{:S(2)}, u32[]{:S(2)}) %collective-permute-start.5) | collective-permute-done | bytes 32800 | tf_op jit(solution)/shard_map/ppermute | solution.py:222
  18.7 1.6 %collective-permute-start.6 = (f32[288,128]{1,0:T(8,128)S(1)}, f32[288,128]{1,0:T(8,128)S(1)}, u32[]{:S(2)}, u32[]{:S(2)}) collective-permute-start(f32[288,128]{1,0:T(8,128)S(1)} %get-tuple-element.13.x), channel_id=1, source_target_pairs={{0,4},{1,9},{2,6},{3,11},{4,0},{5,13},{6,2},{7,15},{8,12},{9,1},{1... | collective-permute-start | bytes 442376 | tf_op jit(solution)/shard_map/ppermute | solution.py:227
  20.3 1.5 %collective-permute-start.7 = (bf16[128,256]{1,0:T(8,128)(2,1)S(1)}, bf16[128,256]{1,0:T(8,128)(2,1)S(1)}, u32[]{:S(2)}, u32[]{:S(2)}) collective-permute-start(bf16[128,256]{1,0:T(8,128)(2,1)S(1)} %get-tuple-element.14.blocks), channel_id=1, source_target_pairs={{0,2},{2,0},{4,6},{6,4},{8,10},{10,8},{12,14},{14,12},{16,18},{18,... | collective-permute-start | bytes 196616 | tf_op jit(solution)/shard_map/ppermute | solution.py:222
  21.8 2.8 %collective-permute-done.7.got_blocks = bf16[128,256]{1,0:T(8,128)(2,1)S(1)} collective-permute-done((bf16[128,256]{1,0:T(8,128)(2,1)S(1)}, bf16[128,256]{1,0:T(8,128)(2,1)S(1)}, u32[]{:S(2)}, u32[]{:S(2)}) %collective-permute-start.7) | collective-permute-done | bytes 65568 | tf_op jit(solution)/shard_map/ppermute | solution.py:222
  24.6 2.3 %collective-permute-start.8 = (f32[288,128]{1,0:T(8,128)S(1)}, f32[288,128]{1,0:T(8,128)S(1)}, u32[]{:S(2)}, u32[]{:S(2)}) collective-permute-start(f32[288,128]{1,0:T(8,128)S(1)} %get-tuple-element.15), channel_id=1, source_target_pairs={{0,16},{1,17},{2,18},{3,19},{4,20},{5,21},{6,22},{7,23},{8,24},{9,... | collective-permute-start | bytes 442376 | tf_op jit(solution)/shard_map/ppermute | solution.py:227
  26.9 5.4 %collective-permute-done.8 = f32[288,128]{1,0:T(8,128)S(1)} collective-permute-done((f32[288,128]{1,0:T(8,128)S(1)}, f32[288,128]{1,0:T(8,128)S(1)}, u32[]{:S(2)}, u32[]{:S(2)}) %collective-permute-start.8) | collective-permute-done | bytes 147488 | tf_op jit(solution)/shard_map/ppermute | solution.py:227
  32.3 1.6 %collective-permute-start.9 = (f32[288,128]{1,0:T(8,128)S(1)}, f32[288,128]{1,0:T(8,128)S(1)}, u32[]{:S(2)}, u32[]{:S(2)}) collective-permute-start(f32[288,128]{1,0:T(8,128)S(1)} %add.3), channel_id=1, source_target_pairs={{0,2},{1,3},{2,0},{3,1},{4,6},{5,7},{6,4},{7,5},{8,10},{9,11},{10,... | collective-permute-start | bytes 442376 | tf_op jit(solution)/shard_map/ppermute | solution.py:227
  33.8 0.5 %collective-permute-start.11 = (f32[288,128]{1,0:T(8,128)S(1)}, f32[288,128]{1,0:T(8,128)S(1)}, u32[]{:S(2)}, u32[]{:S(2)}) collective-permute-start(f32[288,128]{1,0:T(8,128)S(1)} %add.3), channel_id=1, source_target_pairs={{0,1},{1,0},{2,3},{3,2},{4,5},{5,4},{6,7},{7,6},{8,9},{9,8},{10,11... | collective-permute-start | bytes 442376 | tf_op jit(solution)/shard_map/ppermute | solution.py:222
  34.3 3.1 %collective-permute-done.9 = f32[288,128]{1,0:T(8,128)S(1)} collective-permute-done((f32[288,128]{1,0:T(8,128)S(1)}, f32[288,128]{1,0:T(8,128)S(1)}, u32[]{:S(2)}, u32[]{:S(2)}) %collective-permute-start.9) | collective-permute-done | bytes 147488 | tf_op jit(solution)/shard_map/ppermute | solution.py:227
  37.5 0.3 shard_map.73
  37.8 1.1 %collective-permute-done.10 = f32[288,128]{1,0:T(8,128)S(1)} collective-permute-done((f32[288,128]{1,0:T(8,128)S(1)}, f32[288,128]{1,0:T(8,128)S(1)}, u32[]{:S(2)}, u32[]{:S(2)}) %collective-permute-start.10) | collective-permute-done | bytes 147488 | tf_op jit(solution)/shard_map/ppermute | solution.py:222
  38.9 9.0 %shard_map.74 = (f32[256,256]{1,0:T(8,128)}, f32[16,256]{1,0:T(8,128)}) custom-call(f32[576,128]{1,0:T(8,128)S(1)} %maximum_select_fusion.blocks, f32[576,128]{1,0:T(8,128)S(1)} %maximum_select_fusion.1.others, bf16[512,256]{1,0:T(8,128)(2,1)S(1)} %get-tuple-element.17.gathered, bf16[256,256]{1,0:T(8,128)(2,1)S(1)} %get-tuple-element.18.sketch_high, ...), custom_call_target="tpu_custom_call" | custom-call | tf_op jit(solution)/shard_map/pallas_call | solution.py:211
  (25 shorter events, 0.2 us)
Async XLA Ops:
  0.6 0.7 %copy-start.3 = (s32[256]{0:T(256)S(1)}, s32[256]{0:T(256)}, u32[]{:S(2)}) copy-start(s32[256]{0:T(256)} %param.7) | copy-start | bytes 3076
  0.6 0.7 %copy-start.1 = (f32[512]{0:T(512)S(1)}, f32[512]{0:T(512)}, u32[]{:S(2)}) copy-start(f32[512]{0:T(512)} %param.8) | copy-start | bytes 6148
  0.7 0.7 %copy-start.2 = (s32[256]{0:T(256)S(1)}, s32[256]{0:T(256)}, u32[]{:S(2)}) copy-start(s32[256]{0:T(256)} %param.6) | copy-start | bytes 3076
  1.3 0.9 %copy-start = (bf16[512,256]{1,0:T(8,128)(2,1)S(1)}, bf16[512,256]{1,0:T(8,128)(2,1)}, u32[]{:S(2)}) copy-start(bf16[512,256]{1,0:T(8,128)(2,1)} %dosage.1) | copy-start | bytes 786436
  2.3 0.7 %copy-start.4 = (bf16[16,256]{1,0:T(8,128)(2,1)S(1)}, bf16[16,256]{1,0:T(8,128)(2,1)}, u32[]{:S(2)}) copy-start(bf16[16,256]{1,0:T(8,128)(2,1)} %param.9) | copy-start | bytes 24580
  2.5 4.6 %collective-permute-start = (bf16[512,256]{1,0:T(8,128)(2,1)S(1)}, bf16[512,256]{1,0:T(8,128)(2,1)S(1)}, u32[]{:S(2)}, u32[]{:S(2)}) collective-permute-start(bf16[512,256]{1,0:T(8,128)(2,1)S(1)} %shard_map.68.own.refs_2_), channel_id=1, source_target_pairs={{0,1},{1,0},{2,3},{3,2},{4,5},{5,4},{6,7},{7,6},{8,9},{9,8},{10,11... | collective-permute-start | bytes 786440 | tf_op jit(solution)/shard_map/ppermute | solution.py:222
  3.0 6.1 %collective-permute-start.2 = (bf16[16,256]{1,0:T(8,128)(2,1)S(1)}, bf16[16,256]{1,0:T(8,128)(2,1)S(1)}, u32[]{:S(2)}, u32[]{:S(2)}) collective-permute-start(bf16[16,256]{1,0:T(8,128)(2,1)S(1)} %copy-done.4), channel_id=1, source_target_pairs={{0,16},{2,18},{4,20},{6,22},{8,24},{10,26},{12,28},{14,30},{16,0},... | collective-permute-start | bytes 24584 | tf_op jit(solution)/shard_map/ppermute | solution.py:222
  7.5 5.6 %collective-permute-start.1 = (f32[288,128]{1,0:T(8,128)S(1)}, f32[288,128]{1,0:T(8,128)S(1)}, u32[]{:S(2)}, u32[]{:S(2)}) collective-permute-start(f32[288,128]{1,0:T(8,128)S(1)} %get-tuple-element.20), channel_id=1, source_target_pairs={{0,2},{1,3},{2,0},{3,1},{4,6},{5,7},{6,4},{7,5},{8,10},{9,11},{10,... | collective-permute-start | bytes 442376 | tf_op jit(solution)/shard_map/ppermute | solution.py:227
  9.1 3.7 %collective-permute-start.3 = (bf16[32,256]{1,0:T(8,128)(2,1)S(1)}, bf16[32,256]{1,0:T(8,128)(2,1)S(1)}, u32[]{:S(2)}, u32[]{:S(2)}) collective-permute-start(bf16[32,256]{1,0:T(8,128)(2,1)S(1)} %constant_dynamic-update-slice_fusion.blocks), channel_id=1, source_target_pairs={{0,8},{2,10},{4,12},{6,14},{8,0},{10,2},{12,4},{14,6},{16,24},{18,... | collective-permute-start | bytes 49160 | tf_op jit(solution)/shard_map/ppermute | solution.py:222
  13.1 5.6 %collective-permute-start.4 = (f32[288,128]{1,0:T(8,128)S(1)}, f32[288,128]{1,0:T(8,128)S(1)}, u32[]{:S(2)}, u32[]{:S(2)}) collective-permute-start(f32[288,128]{1,0:T(8,128)S(1)} %get-tuple-element.11.x), channel_id=1, source_target_pairs={{0,8},{1,5},{2,10},{3,7},{4,12},{5,1},{6,14},{7,3},{8,0},{9,13},{1... | collective-permute-start | bytes 442376 | tf_op jit(solution)/shard_map/ppermute | solution.py:227
  14.7 3.9 %collective-permute-start.5 = (bf16[64,256]{1,0:T(8,128)(2,1)S(1)}, bf16[64,256]{1,0:T(8,128)(2,1)S(1)}, u32[]{:S(2)}, u32[]{:S(2)}) collective-permute-start(bf16[64,256]{1,0:T(8,128)(2,1)S(1)} %get-tuple-element.12.blocks), channel_id=1, source_target_pairs={{0,4},{2,6},{4,0},{6,2},{8,12},{10,14},{12,8},{14,10},{16,20},{18,... | collective-permute-start | bytes 98312 | tf_op jit(solution)/shard_map/ppermute | solution.py:222
  18.7 5.9 %collective-permute-start.6 = (f32[288,128]{1,0:T(8,128)S(1)}, f32[288,128]{1,0:T(8,128)S(1)}, u32[]{:S(2)}, u32[]{:S(2)}) collective-permute-start(f32[288,128]{1,0:T(8,128)S(1)} %get-tuple-element.13.x), channel_id=1, source_target_pairs={{0,4},{1,9},{2,6},{3,11},{4,0},{5,13},{6,2},{7,15},{8,12},{9,1},{1... | collective-permute-start | bytes 442376 | tf_op jit(solution)/shard_map/ppermute | solution.py:227
  20.3 4.3 %collective-permute-start.7 = (bf16[128,256]{1,0:T(8,128)(2,1)S(1)}, bf16[128,256]{1,0:T(8,128)(2,1)S(1)}, u32[]{:S(2)}, u32[]{:S(2)}) collective-permute-start(bf16[128,256]{1,0:T(8,128)(2,1)S(1)} %get-tuple-element.14.blocks), channel_id=1, source_target_pairs={{0,2},{2,0},{4,6},{6,4},{8,10},{10,8},{12,14},{14,12},{16,18},{18,... | collective-permute-start | bytes 196616 | tf_op jit(solution)/shard_map/ppermute | solution.py:222
  24.6 7.7 %collective-permute-start.8 = (f32[288,128]{1,0:T(8,128)S(1)}, f32[288,128]{1,0:T(8,128)S(1)}, u32[]{:S(2)}, u32[]{:S(2)}) collective-permute-start(f32[288,128]{1,0:T(8,128)S(1)} %get-tuple-element.15), channel_id=1, source_target_pairs={{0,16},{1,17},{2,18},{3,19},{4,20},{5,21},{6,22},{7,23},{8,24},{9,... | collective-permute-start | bytes 442376 | tf_op jit(solution)/shard_map/ppermute | solution.py:227
  32.3 5.2 %collective-permute-start.9 = (f32[288,128]{1,0:T(8,128)S(1)}, f32[288,128]{1,0:T(8,128)S(1)}, u32[]{:S(2)}, u32[]{:S(2)}) collective-permute-start(f32[288,128]{1,0:T(8,128)S(1)} %add.3), channel_id=1, source_target_pairs={{0,2},{1,3},{2,0},{3,1},{4,6},{5,7},{6,4},{7,5},{8,10},{9,11},{10,... | collective-permute-start | bytes 442376 | tf_op jit(solution)/shard_map/ppermute | solution.py:227
  33.8 3.7 %collective-permute-start.12 = (bf16[256,256]{1,0:T(8,128)(2,1)S(1)}, bf16[256,256]{1,0:T(8,128)(2,1)S(1)}, u32[]{:S(2)}, u32[]{:S(2)}) collective-permute-start(bf16[256,256]{1,0:T(8,128)(2,1)S(1)} %get-tuple-element.16.refs_0_), channel_id=1, source_target_pairs={{0,1},{1,0},{2,3},{3,2},{4,5},{5,4},{6,7},{7,6},{8,9},{9,8},{10,11... | collective-permute-start | bytes 393224 | tf_op jit(solution)/shard_map/ppermute | solution.py:222
  33.8 4.0 %collective-permute-start.11 = (f32[288,128]{1,0:T(8,128)S(1)}, f32[288,128]{1,0:T(8,128)S(1)}, u32[]{:S(2)}, u32[]{:S(2)}) collective-permute-start(f32[288,128]{1,0:T(8,128)S(1)} %add.3), channel_id=1, source_target_pairs={{0,1},{1,0},{2,3},{3,2},{4,5},{5,4},{6,7},{7,6},{8,9},{9,8},{10,11... | collective-permute-start | bytes 442376 | tf_op jit(solution)/shard_map/ppermute | solution.py:222
  37.5 1.4 %collective-permute-start.10 = (f32[288,128]{1,0:T(8,128)S(1)}, f32[288,128]{1,0:T(8,128)S(1)}, u32[]{:S(2)}, u32[]{:S(2)}) collective-permute-start(f32[288,128]{1,0:T(8,128)S(1)} %collective-permute-done.9), channel_id=1, source_target_pairs={{0,1},{1,0},{2,3},{3,2},{4,5},{5,4},{6,7},{7,6},{8,9},{9,8},{10,11... | collective-permute-start | bytes 442376 | tf_op jit(solution)/shard_map/ppermute | solution.py:222

commit v7 on v6

--- a/solution.py
+++ b/solution.py
@@ -140,14 +140,16 @@
             break
         ahead = dot(inv, row[:, end : end + BLOCK], 1, 0)
         corner = rest[BLOCK : 2 * BLOCK, end : end + BLOCK] - dot(ahead, ahead, 0, 0)
-        full = dot(inv, row, 1, 0)
-        joined = jnp.concatenate(([full[:, :at]] if at else []) + [inv, full[:, end:]], 1)
+        left = [dot(inv, row[:, :at], 1, 0)] if at else []
+        right = [dot(inv, row[:, end + BLOCK :], 1, 0)] if end + BLOCK < n else []
+        joined = jnp.concatenate(left + [inv, ahead] + right, 1)
         lane = lax.broadcasted_iota(jnp.int32, (BLOCK, n), 1)
         out[at:end, :] = jnp.where(lane < end, joined, 0.0)
         ready(at, end)
-        below = rest[BLOCK:]
+        stop = n if right else end
+        below = rest[BLOCK:, :stop]
         lane = lax.broadcasted_iota(jnp.int32, below.shape, 1)
-        rest = jnp.where((lane >= at) & (lane < end), 0.0, below) - dot(joined[:, end:], joined, 0, 0)
+        rest = jnp.where((lane >= at) & (lane < end), 0.0, below) - dot(joined[:, end:], joined[:, :stop], 0, 0)
 
 
 def sketch_kernel(total, few, test, test_other, standard, standard_other, tests, high, mid):

time: 48.1 us -> 48.1 us (level)
  no operation moved by 1% of the time
where the time goes in v7:
time: 48.1 us; the launch traced here: 47.8 us
  starting transfers between devices  18.3 us (38%)
  waiting for transfers between devices  17.2 us (36%)
  Pallas kernels  9.87 us (21%)
  local copies, waits for them, and re-layouts  1.66 us (3%)
  between operations  0.74 us (2%)
    pallas_call x7, Pallas kernels, call(): pl.pallas_call(kernel, out_shape=shapes, in_specs=[vmem] * len(inputs), o...  9.87 us
    ppermute x8, starting transfers between devices, swap(): lax.ppermute(x, axis, [(i, i ^ bit) for i in range(lax.axis_size(axis))])  9.65 us
    ppermute x5, waiting for transfers between devices, swap_by_core(): return lax.ppermute(x, ('samp', 'mark'), pairs)  8.78 us
    ppermute x5, starting transfers between devices, swap_by_core(): return lax.ppermute(x, ('samp', 'mark'), pairs)  8.66 us
    ppermute x8, waiting for transfers between devices, swap(): lax.ppermute(x, axis, [(i, i ^ bit) for i in range(lax.axis_size(axis))])  8.39 us
    unnamed x11, local copies, waits for them, and re-layouts  1.66 us
  transfers between devices with their start and end apart: 13, of which 7 were waited for; matrix products, arithmetic and copies ran while one was open for 0% of the time, Pallas kernels for 1%

profile of v7, /device:TPU:0, one launch (start us, length us, event | category | flops | bytes accessed | tf_op | source)
XLA Modules:
  0.0 47.8 jit_solution(16918340645982953481)
XLA Ops:
  0.7 0.7 %copy-done.3 = s32[256]{0:T(256)S(1)} copy-done((s32[256]{0:T(256)S(1)}, s32[256]{0:T(256)}, u32[]{:S(2)}) %copy-start.3) | copy-done | bytes 1048
  1.3 0.9 %copy-done = bf16[512,256]{1,0:T(8,128)(2,1)S(1)} copy-done((bf16[512,256]{1,0:T(8,128)(2,1)S(1)}, bf16[512,256]{1,0:T(8,128)(2,1)}, u32[]{:S(2)}) %copy-start) | copy-done | bytes 262168
  2.3 0.1 shard_map.68.own.refs_2_
  2.5 0.5 %collective-permute-start = (bf16[512,256]{1,0:T(8,128)(2,1)S(1)}, bf16[512,256]{1,0:T(8,128)(2,1)S(1)}, u32[]{:S(2)}, u32[]{:S(2)}) collective-permute-start(bf16[512,256]{1,0:T(8,128)(2,1)S(1)} %shard_map.68.own.refs_2_), channel_id=1, source_target_pairs={{0,1},{1,0},{2,3},{3,2},{4,5},{5,4},{6,7},{7,6},{8,9},{9,8},{10,11... | collective-permute-start | bytes 786440 | tf_op jit(solution)/shard_map/ppermute | solution.py:224
  3.0 4.0 %collective-permute-start.2 = (bf16[16,256]{1,0:T(8,128)(2,1)S(1)}, bf16[16,256]{1,0:T(8,128)(2,1)S(1)}, u32[]{:S(2)}, u32[]{:S(2)}) collective-permute-start(bf16[16,256]{1,0:T(8,128)(2,1)S(1)} %copy-done.4), channel_id=1, source_target_pairs={{0,16},{2,18},{4,20},{6,22},{8,24},{10,26},{12,28},{14,30},{16,0},... | collective-permute-start | bytes 24584 | tf_op jit(solution)/shard_map/ppermute | solution.py:224
  7.0 0.4 shard_map.69
  7.5 1.6 %collective-permute-start.1 = (f32[288,128]{1,0:T(8,128)S(1)}, f32[288,128]{1,0:T(8,128)S(1)}, u32[]{:S(2)}, u32[]{:S(2)}) collective-permute-start(f32[288,128]{1,0:T(8,128)S(1)} %get-tuple-element.20), channel_id=1, source_target_pairs={{0,2},{1,3},{2,0},{3,1},{4,6},{5,7},{6,4},{7,5},{8,10},{9,11},{10,... | collective-permute-start | bytes 442376 | tf_op jit(solution)/shard_map/ppermute | solution.py:229
  9.1 1.6 %collective-permute-start.3 = (bf16[32,256]{1,0:T(8,128)(2,1)S(1)}, bf16[32,256]{1,0:T(8,128)(2,1)S(1)}, u32[]{:S(2)}, u32[]{:S(2)}) collective-permute-start(bf16[32,256]{1,0:T(8,128)(2,1)S(1)} %constant_dynamic-update-slice_fusion.blocks), channel_id=1, source_target_pairs={{0,8},{2,10},{4,12},{6,14},{8,0},{10,2},{12,4},{14,6},{16,24},{18,... | collective-permute-start | bytes 49160 | tf_op jit(solution)/shard_map/ppermute | solution.py:224
  10.6 2.2 %collective-permute-done.3.got_blocks = bf16[32,256]{1,0:T(8,128)(2,1)S(1)} collective-permute-done((bf16[32,256]{1,0:T(8,128)(2,1)S(1)}, bf16[32,256]{1,0:T(8,128)(2,1)S(1)}, u32[]{:S(2)}, u32[]{:S(2)}) %collective-permute-start.3) | collective-permute-done | bytes 16416 | tf_op jit(solution)/shard_map/ppermute | solution.py:224
  12.8 0.3 collective-permute-done.1.got
  13.1 1.6 %collective-permute-start.4 = (f32[288,128]{1,0:T(8,128)S(1)}, f32[288,128]{1,0:T(8,128)S(1)}, u32[]{:S(2)}, u32[]{:S(2)}) collective-permute-start(f32[288,128]{1,0:T(8,128)S(1)} %get-tuple-element.11.x), channel_id=1, source_target_pairs={{0,8},{1,5},{2,10},{3,7},{4,12},{5,1},{6,14},{7,3},{8,0},{9,13},{1... | collective-permute-start | bytes 442376 | tf_op jit(solution)/shard_map/ppermute | solution.py:229
  14.7 1.5 %collective-permute-start.5 = (bf16[64,256]{1,0:T(8,128)(2,1)S(1)}, bf16[64,256]{1,0:T(8,128)(2,1)S(1)}, u32[]{:S(2)}, u32[]{:S(2)}) collective-permute-start(bf16[64,256]{1,0:T(8,128)(2,1)S(1)} %get-tuple-element.12.blocks), channel_id=1, source_target_pairs={{0,4},{2,6},{4,0},{6,2},{8,12},{10,14},{12,8},{14,10},{16,20},{18,... | collective-permute-start | bytes 98312 | tf_op jit(solution)/shard_map/ppermute | solution.py:224
  16.3 2.4 %collective-permute-done.5.got_blocks = bf16[64,256]{1,0:T(8,128)(2,1)S(1)} collective-permute-done((bf16[64,256]{1,0:T(8,128)(2,1)S(1)}, bf16[64,256]{1,0:T(8,128)(2,1)S(1)}, u32[]{:S(2)}, u32[]{:S(2)}) %collective-permute-start.5) | collective-permute-done | bytes 32800 | tf_op jit(solution)/shard_map/ppermute | solution.py:224
  18.7 1.6 %collective-permute-start.6 = (f32[288,128]{1,0:T(8,128)S(1)}, f32[288,128]{1,0:T(8,128)S(1)}, u32[]{:S(2)}, u32[]{:S(2)}) collective-permute-start(f32[288,128]{1,0:T(8,128)S(1)} %get-tuple-element.13.x), channel_id=1, source_target_pairs={{0,4},{1,9},{2,6},{3,11},{4,0},{5,13},{6,2},{7,15},{8,12},{9,1},{1... | collective-permute-start | bytes 442376 | tf_op jit(solution)/shard_map/ppermute | solution.py:229
  20.3 1.5 %collective-permute-start.7 = (bf16[128,256]{1,0:T(8,128)(2,1)S(1)}, bf16[128,256]{1,0:T(8,128)(2,1)S(1)}, u32[]{:S(2)}, u32[]{:S(2)}) collective-permute-start(bf16[128,256]{1,0:T(8,128)(2,1)S(1)} %get-tuple-element.14.blocks), channel_id=1, source_target_pairs={{0,2},{2,0},{4,6},{6,4},{8,10},{10,8},{12,14},{14,12},{16,18},{18,... | collective-permute-start | bytes 196616 | tf_op jit(solution)/shard_map/ppermute | solution.py:224
  21.8 2.8 %collective-permute-done.7.got_blocks = bf16[128,256]{1,0:T(8,128)(2,1)S(1)} collective-permute-done((bf16[128,256]{1,0:T(8,128)(2,1)S(1)}, bf16[128,256]{1,0:T(8,128)(2,1)S(1)}, u32[]{:S(2)}, u32[]{:S(2)}) %collective-permute-start.7) | collective-permute-done | bytes 65568 | tf_op jit(solution)/shard_map/ppermute | solution.py:224
  24.6 2.3 %collective-permute-start.8 = (f32[288,128]{1,0:T(8,128)S(1)}, f32[288,128]{1,0:T(8,128)S(1)}, u32[]{:S(2)}, u32[]{:S(2)}) collective-permute-start(f32[288,128]{1,0:T(8,128)S(1)} %get-tuple-element.15), channel_id=1, source_target_pairs={{0,16},{1,17},{2,18},{3,19},{4,20},{5,21},{6,22},{7,23},{8,24},{9,... | collective-permute-start | bytes 442376 | tf_op jit(solution)/shard_map/ppermute | solution.py:229
  26.9 5.4 %collective-permute-done.8 = f32[288,128]{1,0:T(8,128)S(1)} collective-permute-done((f32[288,128]{1,0:T(8,128)S(1)}, f32[288,128]{1,0:T(8,128)S(1)}, u32[]{:S(2)}, u32[]{:S(2)}) %collective-permute-start.8) | collective-permute-done | bytes 147488 | tf_op jit(solution)/shard_map/ppermute | solution.py:229
  32.3 1.6 %collective-permute-start.9 = (f32[288,128]{1,0:T(8,128)S(1)}, f32[288,128]{1,0:T(8,128)S(1)}, u32[]{:S(2)}, u32[]{:S(2)}) collective-permute-start(f32[288,128]{1,0:T(8,128)S(1)} %add.3), channel_id=1, source_target_pairs={{0,2},{1,3},{2,0},{3,1},{4,6},{5,7},{6,4},{7,5},{8,10},{9,11},{10,... | collective-permute-start | bytes 442376 | tf_op jit(solution)/shard_map/ppermute | solution.py:229
  33.8 0.5 %collective-permute-start.11 = (f32[288,128]{1,0:T(8,128)S(1)}, f32[288,128]{1,0:T(8,128)S(1)}, u32[]{:S(2)}, u32[]{:S(2)}) collective-permute-start(f32[288,128]{1,0:T(8,128)S(1)} %add.3), channel_id=1, source_target_pairs={{0,1},{1,0},{2,3},{3,2},{4,5},{5,4},{6,7},{7,6},{8,9},{9,8},{10,11... | collective-permute-start | bytes 442376 | tf_op jit(solution)/shard_map/ppermute | solution.py:224
  34.3 3.1 %collective-permute-done.9 = f32[288,128]{1,0:T(8,128)S(1)} collective-permute-done((f32[288,128]{1,0:T(8,128)S(1)}, f32[288,128]{1,0:T(8,128)S(1)}, u32[]{:S(2)}, u32[]{:S(2)}) %collective-permute-start.9) | collective-permute-done | bytes 147488 | tf_op jit(solution)/shard_map/ppermute | solution.py:229
  37.5 0.3 shard_map.73
  37.8 1.1 %collective-permute-done.10 = f32[288,128]{1,0:T(8,128)S(1)} collective-permute-done((f32[288,128]{1,0:T(8,128)S(1)}, f32[288,128]{1,0:T(8,128)S(1)}, u32[]{:S(2)}, u32[]{:S(2)}) %collective-permute-start.10) | collective-permute-done | bytes 147488 | tf_op jit(solution)/shard_map/ppermute | solution.py:224
  38.9 9.0 %shard_map.74 = (f32[256,256]{1,0:T(8,128)}, f32[16,256]{1,0:T(8,128)}) custom-call(f32[576,128]{1,0:T(8,128)S(1)} %maximum_select_fusion.blocks, f32[576,128]{1,0:T(8,128)S(1)} %maximum_select_fusion.1.others, bf16[512,256]{1,0:T(8,128)(2,1)S(1)} %get-tuple-element.17.gathered, bf16[256,256]{1,0:T(8,128)(2,1)S(1)} %get-tuple-element.18.sketch_high, ...), custom_call_target="tpu_custom_call" | custom-call | tf_op jit(solution)/shard_map/pallas_call | solution.py:213
  (25 shorter events, 0.2 us)
Async XLA Ops:
  0.6 0.7 %copy-start.3 = (s32[256]{0:T(256)S(1)}, s32[256]{0:T(256)}, u32[]{:S(2)}) copy-start(s32[256]{0:T(256)} %param.7) | copy-start | bytes 3076
  0.6 0.7 %copy-start.1 = (f32[512]{0:T(512)S(1)}, f32[512]{0:T(512)}, u32[]{:S(2)}) copy-start(f32[512]{0:T(512)} %param.8) | copy-start | bytes 6148
  0.7 0.7 %copy-start.2 = (s32[256]{0:T(256)S(1)}, s32[256]{0:T(256)}, u32[]{:S(2)}) copy-start(s32[256]{0:T(256)} %param.6) | copy-start | bytes 3076
  1.3 0.9 %copy-start = (bf16[512,256]{1,0:T(8,128)(2,1)S(1)}, bf16[512,256]{1,0:T(8,128)(2,1)}, u32[]{:S(2)}) copy-start(bf16[512,256]{1,0:T(8,128)(2,1)} %dosage.1) | copy-start | bytes 786436
  2.3 0.7 %copy-start.4 = (bf16[16,256]{1,0:T(8,128)(2,1)S(1)}, bf16[16,256]{1,0:T(8,128)(2,1)}, u32[]{:S(2)}) copy-start(bf16[16,256]{1,0:T(8,128)(2,1)} %param.9) | copy-start | bytes 24580
  2.5 4.6 %collective-permute-start = (bf16[512,256]{1,0:T(8,128)(2,1)S(1)}, bf16[512,256]{1,0:T(8,128)(2,1)S(1)}, u32[]{:S(2)}, u32[]{:S(2)}) collective-permute-start(bf16[512,256]{1,0:T(8,128)(2,1)S(1)} %shard_map.68.own.refs_2_), channel_id=1, source_target_pairs={{0,1},{1,0},{2,3},{3,2},{4,5},{5,4},{6,7},{7,6},{8,9},{9,8},{10,11... | collective-permute-start | bytes 786440 | tf_op jit(solution)/shard_map/ppermute | solution.py:224
  3.0 6.1 %collective-permute-start.2 = (bf16[16,256]{1,0:T(8,128)(2,1)S(1)}, bf16[16,256]{1,0:T(8,128)(2,1)S(1)}, u32[]{:S(2)}, u32[]{:S(2)}) collective-permute-start(bf16[16,256]{1,0:T(8,128)(2,1)S(1)} %copy-done.4), channel_id=1, source_target_pairs={{0,16},{2,18},{4,20},{6,22},{8,24},{10,26},{12,28},{14,30},{16,0},... | collective-permute-start | bytes 24584 | tf_op jit(solution)/shard_map/ppermute | solution.py:224
  7.5 5.6 %collective-permute-start.1 = (f32[288,128]{1,0:T(8,128)S(1)}, f32[288,128]{1,0:T(8,128)S(1)}, u32[]{:S(2)}, u32[]{:S(2)}) collective-permute-start(f32[288,128]{1,0:T(8,128)S(1)} %get-tuple-element.20), channel_id=1, source_target_pairs={{0,2},{1,3},{2,0},{3,1},{4,6},{5,7},{6,4},{7,5},{8,10},{9,11},{10,... | collective-permute-start | bytes 442376 | tf_op jit(solution)/shard_map/ppermute | solution.py:229
  9.1 3.7 %collective-permute-start.3 = (bf16[32,256]{1,0:T(8,128)(2,1)S(1)}, bf16[32,256]{1,0:T(8,128)(2,1)S(1)}, u32[]{:S(2)}, u32[]{:S(2)}) collective-permute-start(bf16[32,256]{1,0:T(8,128)(2,1)S(1)} %constant_dynamic-update-slice_fusion.blocks), channel_id=1, source_target_pairs={{0,8},{2,10},{4,12},{6,14},{8,0},{10,2},{12,4},{14,6},{16,24},{18,... | collective-permute-start | bytes 49160 | tf_op jit(solution)/shard_map/ppermute | solution.py:224
  13.1 5.6 %collective-permute-start.4 = (f32[288,128]{1,0:T(8,128)S(1)}, f32[288,128]{1,0:T(8,128)S(1)}, u32[]{:S(2)}, u32[]{:S(2)}) collective-permute-start(f32[288,128]{1,0:T(8,128)S(1)} %get-tuple-element.11.x), channel_id=1, source_target_pairs={{0,8},{1,5},{2,10},{3,7},{4,12},{5,1},{6,14},{7,3},{8,0},{9,13},{1... | collective-permute-start | bytes 442376 | tf_op jit(solution)/shard_map/ppermute | solution.py:229
  14.7 3.9 %collective-permute-start.5 = (bf16[64,256]{1,0:T(8,128)(2,1)S(1)}, bf16[64,256]{1,0:T(8,128)(2,1)S(1)}, u32[]{:S(2)}, u32[]{:S(2)}) collective-permute-start(bf16[64,256]{1,0:T(8,128)(2,1)S(1)} %get-tuple-element.12.blocks), channel_id=1, source_target_pairs={{0,4},{2,6},{4,0},{6,2},{8,12},{10,14},{12,8},{14,10},{16,20},{18,... | collective-permute-start | bytes 98312 | tf_op jit(solution)/shard_map/ppermute | solution.py:224
  18.7 5.9 %collective-permute-start.6 = (f32[288,128]{1,0:T(8,128)S(1)}, f32[288,128]{1,0:T(8,128)S(1)}, u32[]{:S(2)}, u32[]{:S(2)}) collective-permute-start(f32[288,128]{1,0:T(8,128)S(1)} %get-tuple-element.13.x), channel_id=1, source_target_pairs={{0,4},{1,9},{2,6},{3,11},{4,0},{5,13},{6,2},{7,15},{8,12},{9,1},{1... | collective-permute-start | bytes 442376 | tf_op jit(solution)/shard_map/ppermute | solution.py:229
  20.3 4.3 %collective-permute-start.7 = (bf16[128,256]{1,0:T(8,128)(2,1)S(1)}, bf16[128,256]{1,0:T(8,128)(2,1)S(1)}, u32[]{:S(2)}, u32[]{:S(2)}) collective-permute-start(bf16[128,256]{1,0:T(8,128)(2,1)S(1)} %get-tuple-element.14.blocks), channel_id=1, source_target_pairs={{0,2},{2,0},{4,6},{6,4},{8,10},{10,8},{12,14},{14,12},{16,18},{18,... | collective-permute-start | bytes 196616 | tf_op jit(solution)/shard_map/ppermute | solution.py:224
  24.6 7.7 %collective-permute-start.8 = (f32[288,128]{1,0:T(8,128)S(1)}, f32[288,128]{1,0:T(8,128)S(1)}, u32[]{:S(2)}, u32[]{:S(2)}) collective-permute-start(f32[288,128]{1,0:T(8,128)S(1)} %get-tuple-element.15), channel_id=1, source_target_pairs={{0,16},{1,17},{2,18},{3,19},{4,20},{5,21},{6,22},{7,23},{8,24},{9,... | collective-permute-start | bytes 442376 | tf_op jit(solution)/shard_map/ppermute | solution.py:229
  32.3 5.2 %collective-permute-start.9 = (f32[288,128]{1,0:T(8,128)S(1)}, f32[288,128]{1,0:T(8,128)S(1)}, u32[]{:S(2)}, u32[]{:S(2)}) collective-permute-start(f32[288,128]{1,0:T(8,128)S(1)} %add.3), channel_id=1, source_target_pairs={{0,2},{1,3},{2,0},{3,1},{4,6},{5,7},{6,4},{7,5},{8,10},{9,11},{10,... | collective-permute-start | bytes 442376 | tf_op jit(solution)/shard_map/ppermute | solution.py:229
  33.8 3.7 %collective-permute-start.12 = (bf16[256,256]{1,0:T(8,128)(2,1)S(1)}, bf16[256,256]{1,0:T(8,128)(2,1)S(1)}, u32[]{:S(2)}, u32[]{:S(2)}) collective-permute-start(bf16[256,256]{1,0:T(8,128)(2,1)S(1)} %get-tuple-element.16.refs_0_), channel_id=1, source_target_pairs={{0,1},{1,0},{2,3},{3,2},{4,5},{5,4},{6,7},{7,6},{8,9},{9,8},{10,11... | collective-permute-start | bytes 393224 | tf_op jit(solution)/shard_map/ppermute | solution.py:224
  33.8 4.0 %collective-permute-start.11 = (f32[288,128]{1,0:T(8,128)S(1)}, f32[288,128]{1,0:T(8,128)S(1)}, u32[]{:S(2)}, u32[]{:S(2)}) collective-permute-start(f32[288,128]{1,0:T(8,128)S(1)} %add.3), channel_id=1, source_target_pairs={{0,1},{1,0},{2,3},{3,2},{4,5},{5,4},{6,7},{7,6},{8,9},{9,8},{10,11... | collective-permute-start | bytes 442376 | tf_op jit(solution)/shard_map/ppermute | solution.py:224
  37.5 1.4 %collective-permute-start.10 = (f32[288,128]{1,0:T(8,128)S(1)}, f32[288,128]{1,0:T(8,128)S(1)}, u32[]{:S(2)}, u32[]{:S(2)}) collective-permute-start(f32[288,128]{1,0:T(8,128)S(1)} %collective-permute-done.9), channel_id=1, source_target_pairs={{0,1},{1,0},{2,3},{3,2},{4,5},{5,4},{6,7},{7,6},{8,9},{9,8},{10,11... | collective-permute-start | bytes 442376 | tf_op jit(solution)/shard_map/ppermute | solution.py:224
